TPU v7x, 32 devices: a whole 2x2x4 slice. The times are simulated.
32 devices in a mesh: head: 8 (over z, y), blk: 4 (over x, core).
Axes of the slice: x: 2, y: 2, z: 4, core: 2. Of those that a mesh axis runs over, the one named last changes fastest.
Arguments:
- inputs: bfloat16 [2, 4, 1024, 1024], P(None, 'blk', 'head'), may hold values from -6 to 6
- segments: int32 [2, 4, 1024], replicated, may hold values from 0 to 8, as said below
- bucket_table: int32 [257], replicated, may hold values from 0 to 31, as said below
- norm_gain: bfloat16 [1024], P(('head', 'blk')), may hold values from 0.25 to 1.75
- w_query: bfloat16 [1024, 1024], P(('head', 'blk')), may hold values from -0.09375 to 0.09375
- w_key: bfloat16 [1024, 1024], P(('head', 'blk')), may hold values from -0.09375 to 0.09375
- w_value: bfloat16 [1024, 1024], P(('head', 'blk')), may hold values from -0.1875 to 0.1875
- w_out: bfloat16 [1024, 1024], P(('head', 'blk')), may hold values from -0.375 to 0.375
- rel_bias: bfloat16 [512], P(('head', 'blk')), may hold values from -4 to 4
- ff_gain: bfloat16 [1024], P(('head', 'blk')), may hold values from 0.25 to 1.75
- w_in: bfloat16 [1024, 4096], P(('head', 'blk')), may hold values from -0.1875 to 0.1875
- w_down: bfloat16 [4096, 1024], P(('head', 'blk')), may hold values from -0.09375 to 0.09375
- cotangent: bfloat16 [2, 4, 1024, 1024], P(None, 'blk', 'head'), may hold values from -6 to 6
Outputs:
- layer_out: bfloat16 [2, 4, 1024, 1024], P(None, 'blk', 'head')
- input_grad: bfloat16 [2, 4, 1024, 1024], P(None, 'blk', 'head')
- grad_norm_gain: float32 [1024], P(('head', 'blk'))
- grad_query: float32 [1024, 1024], P(('head', 'blk'))
- grad_key: float32 [1024, 1024], P(('head', 'blk'))
- grad_value: float32 [1024, 1024], P(('head', 'blk'))
- grad_out: float32 [1024, 1024], P(('head', 'blk'))
- grad_rel: float32 [512], P(('head', 'blk'))
- grad_ff_gain: float32 [1024], P(('head', 'blk'))
- grad_in: float32 [1024, 4096], P(('head', 'blk'))
- grad_down: float32 [4096, 1024], P(('head', 'blk'))
Inputs may be any that keep to these rules, and one draw needn't show every extreme that they name: `segments`: document numbers start at 0 in each sequence and never fall along it. In one sequence drawn from the seed the whole sequence is one document; in every other one each aligned run of min(512, 4096) positions holds exactly one document start, lying at least an eighth of the run away from the run's ends. `bucket_table`: A relabelling drawn from the seed of the bidirectional T5 buckets (32 buckets; exact distances below a quarter of them on each side, logarithmic up to 128) for offsets minus 128 to 128; entry 128 is offset 0.
All inputs are finite; a program needn't handle non-finite values.
Results may differ from a plain program's by a relative error of at most 0.02.
Values may be sent and summed in bfloat16 or wider, within the bound.
No kernel may reach another device: no remote copies, remote signals or barrier semaphores. Data moves between devices by JAX's collectives and lax.ppermute only.
A program may use at most 256 MiB of HBM per device.

v0:
```python
import jax
import jax.numpy as jnp
from jax import lax
from jax.sharding import PartitionSpec as P

HEADS = 16
HD = 64
BUCKETS = 32
MAXREL = 128


EPS = 1e-06
FLOOR = -1e30


def from_behind(block, axis, distance):
    devices = range(lax.axis_size(axis))
    route = [((i - distance) % len(devices), i) for i in devices]
    return lax.ppermute(block, axis, route)


def rms_scale(token_rows, gain_vector):
    return (
        token_rows
        * lax.rsqrt(jnp.mean(token_rows * token_rows, axis=-1, keepdims=True) + EPS)
        * gain_vector
    )


def smooth(values):
    return jax.nn.gelu(values, approximate=True)


def band_layout(span_len):
    tile_side = min(128, span_len)
    reach = MAXREL // tile_side + 2
    return (tile_side, span_len // tile_side, reach)


def band_tables(bucket_table, rel_here, span_len):
    tile_side, _, reach = band_layout(span_len)
    kinds = 2 * reach + 1
    gaps = lax.iota(jnp.int32, kinds) - reach
    rows_in = lax.iota(jnp.int32, tile_side)
    offsets = gaps[:, None, None] * tile_side + rows_in[None, None, :] - rows_in[None, :, None]
    lookup = jnp.clip(offsets, -MAXREL, MAXREL) + MAXREL
    bucket = jnp.take(bucket_table, lookup.reshape(-1), axis=0)
    onehot = (bucket[:, None] == lax.iota(jnp.int32, BUCKETS)[None, :]).astype(jnp.float32)
    band_bias = jnp.dot(rel_here, onehot.T, precision=lax.Precision.HIGHEST)
    return (band_bias.reshape(rel_here.shape[0], kinds, tile_side, tile_side), onehot)


def band_index(block_gap, span_len):
    _, tiles, reach = band_layout(span_len)
    row_tile = lax.iota(jnp.int32, tiles)[:, None, None, None]
    col_tile = lax.iota(jnp.int32, tiles)[None, None, :, None]
    return jnp.clip(block_gap * tiles + col_tile - row_tile, -reach, reach) + reach


def bias_tile(band_bias, block_gap, span_len):
    heads_count, kinds, tile_side, _ = band_bias.shape
    tiles = span_len // tile_side
    which = band_index(block_gap, span_len)
    result = jnp.zeros((heads_count, tiles, tile_side, tiles, tile_side), jnp.float32)
    for kind in range(kinds):
        result = jnp.where(which[None] == kind, band_bias[:, kind][:, None, :, None, :], result)
    return result.reshape(heads_count, span_len, span_len)


def band_sums(tile_sum, block_gap, span_len):
    tile_side, tiles, reach = band_layout(span_len)
    heads_count = tile_sum.shape[0]
    split_sum = tile_sum.reshape(heads_count, tiles, tile_side, tiles, tile_side)
    which = band_index(block_gap, span_len)
    parts = []
    for kind in range(2 * reach + 1):
        parts.append(jnp.sum(jnp.where(which[None] == kind, split_sum, 0.0), axis=(1, 3)))
    return jnp.stack(parts, axis=1).reshape(heads_count, -1)


def pass_grads(key_grad, value_grad):
    return (
        from_behind(key_grad.astype(jnp.bfloat16), "blk", 1).astype(key_grad.dtype),
        from_behind(value_grad.astype(jnp.bfloat16), "blk", 1).astype(value_grad.dtype),
    )


def body(
    inputs,
    segments,
    bucket_table,
    norm_gain,
    w_query,
    w_key,
    w_value,
    w_out,
    rel_bias,
    ff_gain,
    w_in,
    w_down,
    cotangent,
):
    seq_count, _, part_len, width = inputs.shape
    cycle_size = lax.axis_size("blk")
    head_groups = lax.axis_size("head")
    heads_here = HEADS // head_groups
    span_len = part_len * head_groups
    cycle_place = lax.axis_index("blk")
    head_place = lax.axis_index("head")
    gathered = (
        lax.all_gather(norm_gain, ("head", "blk"), axis=0, tiled=True),
        lax.all_gather(w_query, ("head", "blk"), axis=0, tiled=True),
        lax.all_gather(w_key, ("head", "blk"), axis=0, tiled=True),
        lax.all_gather(w_value, ("head", "blk"), axis=0, tiled=True),
        lax.all_gather(w_out, ("head", "blk"), axis=0, tiled=True),
        lax.all_gather(rel_bias, ("head", "blk"), axis=0, tiled=True),
        lax.all_gather(ff_gain, ("head", "blk"), axis=0, tiled=True),
        lax.all_gather(w_in, ("head", "blk"), axis=0, tiled=True),
        lax.all_gather(w_down, ("head", "blk"), axis=0, tiled=True),
    )
    gain_one, query_w, key_w, value_w, out_w, rel_flat, gain_two, in_w, down_w = gathered
    token_rows = inputs.reshape(-1, width).astype(jnp.float32)
    normed, norm_one_back = jax.vjp(rms_scale, token_rows, gain_one.astype(jnp.float32))
    first_in = normed.astype(jnp.bfloat16)

    def project(weight):
        made_rows = jnp.dot(first_in, weight, preferred_element_type=jnp.float32)
        return made_rows.astype(jnp.bfloat16).reshape(seq_count, part_len, -1)

    queries, keys_home, values_home = (
        lax.all_to_all(project(query_w), "head", split_axis=2, concat_axis=1, tiled=True),
        lax.all_to_all(project(key_w), "head", split_axis=2, concat_axis=1, tiled=True),
        lax.all_to_all(project(value_w), "head", split_axis=2, concat_axis=1, tiled=True),
    )
    head_shape = (seq_count, span_len, heads_here, HD)
    queries = queries.reshape(head_shape)
    keys_home = keys_home.reshape(head_shape)
    values_home = values_home.reshape(head_shape)
    rel_table = rel_flat.astype(jnp.float32).reshape(HEADS, BUCKETS)
    rel_here = lax.dynamic_slice_in_dim(rel_table, head_place * heads_here, heads_here, 0)
    band_bias, band_onehot = band_tables(bucket_table, rel_here, span_len)

    def tile_scores(query_rows, key_rows, query_block, key_block):
        query_ids = lax.dynamic_index_in_dim(segments, query_block, 1, keepdims=False)
        key_ids = lax.dynamic_index_in_dim(segments, key_block, 1, keepdims=False)
        plain_scores = (
            jnp.einsum("sihd,sjhd->shij", query_rows, key_rows, preferred_element_type=jnp.float32)
            + bias_tile(band_bias, key_block - query_block, span_len)[None]
        )
        same_doc = query_ids[:, None, :, None] == key_ids[:, None, None, :]
        return jnp.where(same_doc, plain_scores, FLOOR)

    first_scores = tile_scores(queries, keys_home, cycle_place, cycle_place)
    row_max = jnp.max(first_scores, axis=-1)
    first_weights = jnp.exp(first_scores - row_max[..., None])
    row_total = jnp.sum(first_weights, axis=-1)
    summed = jnp.einsum(
        "shij,sjhd->sihd",
        first_weights.astype(jnp.bfloat16),
        values_home,
        preferred_element_type=jnp.float32,
    )

    def forward_turn(cycle_turn, state_now):
        old_max, old_total, old_summed, key_rows, value_rows = state_now
        key_rows, value_rows = from_behind((key_rows, value_rows), "blk", 1)
        source = (cycle_place - cycle_turn) % cycle_size
        scores = tile_scores(queries, key_rows, cycle_place, source)
        new_max = jnp.maximum(old_max, jnp.max(scores, axis=-1))
        shrink = jnp.exp(old_max - new_max)
        weights_now = jnp.exp(scores - new_max[..., None])
        new_total = old_total * shrink + jnp.sum(weights_now, axis=-1)
        new_summed = old_summed * jnp.transpose(shrink, (0, 2, 1))[..., None] + jnp.einsum(
            "shij,sjhd->sihd",
            weights_now.astype(jnp.bfloat16),
            value_rows,
            preferred_element_type=jnp.float32,
        )
        return (new_max, new_total, new_summed, key_rows, value_rows)

    row_max, row_total, summed, _, _ = lax.fori_loop(
        1, cycle_size, forward_turn, (row_max, row_total, summed, keys_home, values_home)
    )
    log_total = row_max + jnp.log(row_total)
    attended = summed / jnp.transpose(row_total, (0, 2, 1))[..., None]
    attended_low = attended.astype(jnp.bfloat16).reshape(seq_count, span_len, heads_here * HD)
    attn_rows = lax.all_to_all(
        attended_low, "head", split_axis=1, concat_axis=2, tiled=True
    ).reshape(-1, HEADS * HD)
    hidden_one = token_rows + jnp.dot(attn_rows, out_w, preferred_element_type=jnp.float32)
    normed_two, norm_two_back = jax.vjp(rms_scale, hidden_one, gain_two.astype(jnp.float32))
    second_in = normed_two.astype(jnp.bfloat16)
    upward = jnp.dot(second_in, in_w, preferred_element_type=jnp.float32)
    activated, smooth_back = jax.vjp(smooth, upward)
    activated_low = activated.astype(jnp.bfloat16)
    layer_rows = hidden_one + jnp.dot(activated_low, down_w, preferred_element_type=jnp.float32)
    layer_out = layer_rows.astype(jnp.bfloat16).reshape(inputs.shape)
    back_query, back_key, back_value, back_out, back_in, back_down = (
        query_w,
        key_w,
        value_w,
        out_w,
        in_w,
        down_w,
    )
    incoming_low = cotangent.reshape(-1, width)
    incoming = incoming_low.astype(jnp.float32)
    grad_down = jnp.dot(activated_low.T, incoming_low, preferred_element_type=jnp.float32)
    (up_grad,) = smooth_back(jnp.dot(incoming_low, back_down.T, preferred_element_type=jnp.float32))
    up_low = up_grad.astype(jnp.bfloat16)
    grad_in = jnp.dot(second_in.T, up_low, preferred_element_type=jnp.float32)
    hidden_part, grad_gain_two = norm_two_back(
        jnp.dot(up_low, back_in.T, preferred_element_type=jnp.float32)
    )
    hidden_grad = incoming + hidden_part
    branch_low = hidden_grad.astype(jnp.bfloat16)
    grad_out = jnp.dot(attn_rows.T, branch_low, preferred_element_type=jnp.float32)
    attn_grad_low = jnp.dot(branch_low, back_out.T, preferred_element_type=jnp.float32).astype(
        jnp.bfloat16
    )
    grad_heads = lax.all_to_all(
        attn_grad_low.reshape(seq_count, part_len, HEADS * HD),
        "head",
        split_axis=2,
        concat_axis=1,
        tiled=True,
    ).reshape(head_shape)
    row_delta = jnp.transpose(
        jnp.sum(grad_heads.astype(jnp.float32) * attended, axis=-1), (0, 2, 1)
    )

    def tile_grads(
        query_rows, grad_rows, log_rows, delta_rows, key_rows, value_rows, query_block, key_block
    ):
        scores = tile_scores(query_rows, key_rows, query_block, key_block)
        probs = jnp.exp(scores - log_rows[..., None])
        value_part = jnp.einsum(
            "shij,sihd->sjhd",
            probs.astype(jnp.bfloat16),
            grad_rows,
            preferred_element_type=jnp.float32,
        )
        prob_grad = jnp.einsum(
            "sihd,sjhd->shij", grad_rows, value_rows, preferred_element_type=jnp.float32
        )
        score_low = (probs * (prob_grad - delta_rows[..., None])).astype(jnp.bfloat16)
        query_part = jnp.einsum(
            "shij,sjhd->sihd", score_low, key_rows, preferred_element_type=jnp.float32
        )
        key_part = jnp.einsum(
            "shij,sihd->sjhd", score_low, query_rows, preferred_element_type=jnp.float32
        )
        tile_sum = jnp.sum(score_low.astype(jnp.float32), axis=0)
        rel_part = jnp.dot(
            band_sums(tile_sum, key_block - query_block, span_len),
            band_onehot,
            precision=lax.Precision.HIGHEST,
        )
        return (query_part, key_part, value_part, rel_part)

    query_grad, key_grad, value_grad, rel_grad = tile_grads(
        queries, grad_heads, log_total, row_delta, keys_home, values_home, cycle_place, cycle_place
    )

    def key_turn(cycle_turn, state_now):
        key_rows, value_rows, key_sum, value_sum, query_sum, rel_sum = state_now
        key_sum, value_sum = pass_grads(key_sum, value_sum)
        key_rows, value_rows = from_behind((key_rows, value_rows), "blk", 1)
        source = (cycle_place - cycle_turn) % cycle_size
        query_part, key_part, value_part, rel_part = tile_grads(
            queries, grad_heads, log_total, row_delta, key_rows, value_rows, cycle_place, source
        )
        return (
            key_rows,
            value_rows,
            key_sum + key_part,
            value_sum + value_part,
            query_sum + query_part,
            rel_sum + rel_part,
        )

    state_first = (keys_home, values_home, key_grad, value_grad, query_grad, rel_grad)
    _, _, key_grad, value_grad, query_grad, rel_grad = lax.fori_loop(
        1, cycle_size, key_turn, state_first
    )
    key_grad, value_grad = pass_grads(key_grad, value_grad)
    block_shape = (seq_count, span_len, heads_here * HD)
    query_rows, key_rows_back, value_rows_back = (
        lax.all_to_all(
            query_grad.astype(jnp.bfloat16).reshape(block_shape),
            "head",
            split_axis=1,
            concat_axis=2,
            tiled=True,
        ),
        lax.all_to_all(
            key_grad.astype(jnp.bfloat16).reshape(block_shape),
            "head",
            split_axis=1,
            concat_axis=2,
            tiled=True,
        ),
        lax.all_to_all(
            value_grad.astype(jnp.bfloat16).reshape(block_shape),
            "head",
            split_axis=1,
            concat_axis=2,
            tiled=True,
        ),
    )
    query_rows = query_rows.reshape(-1, HEADS * HD)
    key_rows_back = key_rows_back.reshape(-1, HEADS * HD)
    value_rows_back = value_rows_back.reshape(-1, HEADS * HD)
    grad_query = jnp.dot(first_in.T, query_rows, preferred_element_type=jnp.float32)
    grad_key = jnp.dot(first_in.T, key_rows_back, preferred_element_type=jnp.float32)
    grad_value = jnp.dot(first_in.T, value_rows_back, preferred_element_type=jnp.float32)
    first_grad = (
        jnp.dot(query_rows, back_query.T, preferred_element_type=jnp.float32)
        + jnp.dot(key_rows_back, back_key.T, preferred_element_type=jnp.float32)
        + jnp.dot(value_rows_back, back_value.T, preferred_element_type=jnp.float32)
    )
    input_part, grad_gain_one = norm_one_back(first_grad)
    input_grad = (hidden_grad + input_part).astype(jnp.bfloat16).reshape(inputs.shape)
    rel_full = lax.dynamic_update_slice_in_dim(
        jnp.zeros((HEADS, BUCKETS), jnp.float32), rel_grad, head_place * heads_here, 0
    ).reshape(-1)
    shards = tuple(
        (
            lax.psum_scatter(grad_gain_one, ("head", "blk"), scatter_dimension=0, tiled=True),
            lax.psum_scatter(grad_query, ("head", "blk"), scatter_dimension=0, tiled=True),
            lax.psum_scatter(grad_key, ("head", "blk"), scatter_dimension=0, tiled=True),
            lax.psum_scatter(grad_value, ("head", "blk"), scatter_dimension=0, tiled=True),
            lax.psum_scatter(grad_out, ("head", "blk"), scatter_dimension=0, tiled=True),
            lax.psum_scatter(rel_full, ("head", "blk"), scatter_dimension=0, tiled=True),
            lax.psum_scatter(grad_gain_two, ("head", "blk"), scatter_dimension=0, tiled=True),
            lax.psum_scatter(grad_in, ("head", "blk"), scatter_dimension=0, tiled=True),
            lax.psum_scatter(grad_down, ("head", "blk"), scatter_dimension=0, tiled=True),
        )
    )
    return (
        layer_out,
        input_grad,
        shards[0],
        shards[1],
        shards[2],
        shards[3],
        shards[4],
        shards[5],
        shards[6],
        shards[7],
        shards[8],
    )


def solution(mesh):
    placed = (
        P(None, "blk", "head", None),
        P(),
        P(),
        P(("head", "blk")),
        P(("head", "blk"), None),
        P(("head", "blk"), None),
        P(("head", "blk"), None),
        P(("head", "blk"), None),
        P(("head", "blk")),
        P(("head", "blk")),
        P(("head", "blk"), None),
        P(("head", "blk"), None),
        P(None, "blk", "head", None),
    )
    return jax.shard_map(
        body,
        mesh=mesh,
        in_specs=placed,
        out_specs=(
            P(None, "blk", "head", None),
            P(None, "blk", "head", None),
            P(("head", "blk")),
            P(("head", "blk"), None),
            P(("head", "blk"), None),
            P(("head", "blk"), None),
            P(("head", "blk"), None),
            P(("head", "blk")),
            P(("head", "blk")),
            P(("head", "blk"), None),
            P(("head", "blk"), None),
        ),
        check_vma=False,
    )
```

profile of v0, /device:TPU:0, one launch (start us, length us, event | category | flops | bytes accessed | tf_op | source)
XLA Modules:
  0.0 3108.1 jit_solution(307776744829169974)
XLA Ops:
  16.8 713.1 %gather_fusion = s32[114688]{0:T(1024)S(1)} fusion(s32[257]{0:T(512)S(1)} %copy-done, s32[114688]{0:T(1024)S(1)} %broadcast_clamp_fusion), kind=kCustom, calls=%fused_computation | custom fusion | bytes 1376256 | tf_op jit(solution)/shard_map/jit(_take)/gather | solution.py:47
  730.5 42.1 %all-reduce.8 = (bf16[1024]{0:T(1024)(128)(2,1)S(1)}, bf16[16,32]{1,0:T(8,128)(2,1)S(1)}, bf16[1024]{0:T(1024)(128)(2,1)}) all-reduce(bf16[1024]{0:T(1024)(128)(2,1)S(1)} %dynamic-update-slice, bf16[16,32]{1,0:T(8,128)(2,1)S(1)} %reshape.1130, bf16[1024]{0:T(1024)(128)(2,1)S(1)} %dynamic-update-slice.2), channel_id=1, replica_groups=mesh['head'=8,'blk'=4] {'head','blk'}, use_global_device_ids=true, to_apply=%add | all-reduce | flops 2560 | bytes 10240
  792.8 9.3 broadcast_in_dim.1038
  819.8 9.3 broadcast_in_dim.1050
  860.4 9.6 broadcast_in_dim.1068
  919.4 25.8 select_select_fusion.2
  958.5 10.2 fusion.54
  977.4 10.1 fusion.70
  988.3 496.1 %while.49 = (s32[]{:T(128)}, f32[2,2,1024]{2,1,0:T(2,128)}, f32[2,2,1024]{2,1,0:T(2,128)}, f32[2,1024,2,64]{1,3,2,0:T(8,128)}, bf16[2,1024,2,64]{1,3,2,0:T(8,128...) while((s32[]{:T(128)}, f32[2,2,1024]{2,1,0:T(2,128)}, ...), condition=%wide.region_6.7_spmd, body=%wide.region_3.6_spmd.sunk | while | flops 1137193600 | bytes 410617408 | solution.py:181
  1007.7 9.3 broadcast_in_dim.1310
  1061.6 9.3 broadcast_in_dim.1318
  1093.2 25.7 select_select_fusion.5
  1120.9 10.2 fusion.208
  1172.2 9.3 broadcast_in_dim.1310
  1226.0 9.3 broadcast_in_dim.1318
  1257.6 25.7 select_select_fusion.5
  1285.4 10.2 fusion.208
  1337.7 9.3 broadcast_in_dim.1310
  1364.6 9.3 broadcast_in_dim.1314
  1391.6 9.3 broadcast_in_dim.1318
  1423.2 25.7 select_select_fusion.5
  1450.9 10.2 fusion.208
  1492.9 14.7 all-to-all-done.3
  1518.9 11.0 fusion.69
  1557.6 12.6 fusion.73
  1570.2 16.9 convert_reduce_fusion.1
  1600.6 10.1 select_reduce_fusion.7
  1619.2 666.7 %while.50 = (s32[]{:T(128)}, bf16[2,1024,2,64]{1,3,2,0:T(8,128)(2,1)}, bf16[2,1024,2,64]{1,3,2,0:T(8,128)(2,1)}, bf16[2,1024,2,64]{1,3,2,0:T(8,128)(2,1)}, bf16[...) while((s32[]{:T(128)}, ...), condition=%wide.region_27.28_spmd.clone, body=%wide.region_18.27_spmd.clone.sunk | while | flops 2875752960 | bytes 498748224 | solution.py:283
  1626.2 9.4 broadcast_in_dim.1339
  1653.1 9.4 broadcast_in_dim.1343
  1726.1 26.5 select_select_fusion.6
  1754.6 9.4 fusion.224
  1764.0 16.7 convert_reduce_fusion.3
  1786.2 9.9 select_reduce_fusion.15
  1799.4 10.4 convert_add_fusion.5
  1814.0 13.3 fusion.227
  1846.5 9.3 broadcast_in_dim.1339
  1873.3 9.3 broadcast_in_dim.1343
  1946.3 26.7 select_select_fusion.6
  1975.1 9.4 fusion.224
  1984.5 16.7 convert_reduce_fusion.3
  2006.6 9.9 select_reduce_fusion.15
  2019.9 10.3 convert_add_fusion.5
  2034.4 13.3 fusion.227
  2066.9 9.3 broadcast_in_dim.1339
  2093.8 9.3 broadcast_in_dim.1343
  2166.7 26.5 select_select_fusion.6
  2195.3 9.4 fusion.224
  2204.7 16.7 convert_reduce_fusion.3
  2226.8 9.9 select_reduce_fusion.15
  2240.1 10.4 convert_add_fusion.5
  2254.6 13.3 fusion.227
  2293.4 13.9 all-to-all-done.5
  2310.7 11.4 collective-permute-done.6
  2322.5 16.8 all_to_all.120
  2342.6 11.1 collective-permute-done.7
  2355.8 20.4 all_to_all.121
  2379.5 9.9 fusion.128
  2390.4 10.8 fusion.130
  2415.6 37.8 %all-reduce.7 = (f32[1024]{0:T(1024)S(1)}, f32[512]{0:T(512)S(1)}, f32[1024]{0:T(1024)S(1)}) all-reduce(f32[1024]{0:T(1024)S(1)} %get-tuple-element.994, f32[512]{0:T(512)S(1)} %reshape.1149, f32[1024]{0:T(1024)S(1)} %copy-done.70), channel_id=2, replica_groups=mesh['head'=8,'blk'=4] {'head','blk'}, use_global_device_ids=true, to_apply=%region_30.31.clone | all-reduce | flops 2560 | bytes 20480
  2456.3 135.8 %reduce-scatter.9.cloned.1.call-done = f32[32,1024]{1,0:T(8,128)} async-done(((f32[1024,1024]{1,0:T(8,128)}), f32[32,1024]{1,0:T(8,128)}) %reduce-scatter.9.cloned.1.call-update) | async-done | bytes 131088 | tf_op jit(solution)/shard_map/reduce_scatter | solution.py:331
  2592.1 139.7 %reduce-scatter.11.cloned.1.call-done = f32[32,1024]{1,0:T(8,128)} async-done(((f32[1024,1024]{1,0:T(8,128)}), f32[32,1024]{1,0:T(8,128)}) %reduce-scatter.11.cloned.1.call-update) | async-done | bytes 131088 | tf_op jit(solution)/shard_map/reduce_scatter | solution.py:332
  2731.8 181.7 %reduce-scatter.15.cloned.1.call-done = f32[32,4096]{1,0:T(8,128)} async-done(((f32[1024,4096]{1,0:T(8,128)}), f32[32,4096]{1,0:T(8,128)}) %reduce-scatter.15.cloned.1.call-update) | async-done | bytes 524304 | tf_op jit(solution)/shard_map/reduce_scatter | solution.py:336
  2913.5 187.4 %reduce-scatter.17.cloned.1.call-done = f32[128,1024]{1,0:T(8,128)} async-done(((f32[4096,1024]{1,0:T(8,128)}), f32[128,1024]{1,0:T(8,128)}) %reduce-scatter.17.cloned.1.call-update) | async-done | bytes 524304 | tf_op jit(solution)/shard_map/reduce_scatter | solution.py:337
  (712 shorter events, 917.6 us)
Async XLA Ops:
  7.2 868.2 %all-gather.7.cloned.1.call-start = ((), (), s32[]{:S(2)}) async-start(), calls=%async_computation.14 | async-start | bytes 2162688 | tf_op jit(solution)/shard_map/all_gather | solution.py:112
  7.9 879.7 %all-gather.9.cloned.1.call-start = ((), (), s32[]{:S(2)}) async-start(), calls=%async_computation.15 | async-start | bytes 2162688 | tf_op jit(solution)/shard_map/all_gather | solution.py:113
  8.7 896.5 %all-gather.11.cloned.1.call-start = ((), (), s32[]{:S(2)}) async-start(), calls=%async_computation.16 | async-start | bytes 2162688 | tf_op jit(solution)/shard_map/all_gather | solution.py:114
  9.4 1498.7 %all-gather.13.cloned.1.call-start = ((), (), s32[]{:S(2)}) async-start(), calls=%async_computation.17 | async-start | bytes 2162688 | tf_op jit(solution)/shard_map/all_gather | solution.py:115
  10.0 1500.8 %all-gather.17.cloned.1.call-start = ((), (), s32[]{:S(2)}) async-start(), calls=%async_computation.19 | async-start | bytes 8650752 | tf_op jit(solution)/shard_map/all_gather | solution.py:119
  10.6 1508.3 %all-gather.15.cloned.1.call-start = ((), (), s32[]{:S(2)}) async-start(), calls=%async_computation.18 | async-start | bytes 8650752 | tf_op jit(solution)/shard_map/all_gather | solution.py:118
  16.8 713.1 %copy-start.74 = (bf16[32]{0:T(256)(128)(2,1)S(1)}, bf16[32]{0:T(256)(128)(2,1)}, u32[]{:S(2)}) copy-start(bf16[32]{0:T(256)(128)(2,1)} %param.20) | copy-start | bytes 196
  16.8 713.4 %copy-start.75 = (bf16[32]{0:T(256)(128)(2,1)S(1)}, bf16[32]{0:T(256)(128)(2,1)}, u32[]{:S(2)}) copy-start(bf16[32]{0:T(256)(128)(2,1)} %param.26) | copy-start | bytes 196
  730.5 44.5 %copy-start.46 = (s32[114688]{0:T(1024)}, s32[114688]{0:T(1024)S(1)}, u32[]{:S(2)}) copy-start(s32[114688]{0:T(1024)S(1)} %and_select_fusion) | copy-start | bytes 1376260
  775.0 170.2 %copy-start.18 = (f32[1,2,896,128]{3,2,1,0:T(8,128)}, f32[1,2,896,128]{3,2,1,0:T(8,128)S(1)}, u32[]{:S(2)}) copy-start(f32[1,2,896,128]{3,2,1,0:T(8,128)S(1)} %copy.352) | copy-start | bytes 2752516
  875.3 26.1 copy-start.65
  878.9 18.4 all-to-all-start
  897.3 47.9 %copy-start.37 = (bf16[2,128,1024]{1,0,2:T(2,128)(2,1)}, bf16[2,128,1024]{1,0,2:T(2,128)(2,1)S(1)}, u32[]{:S(2)}) copy-start(bf16[2,128,1024]{1,0,2:T(2,128)(2,1)S(1)} %all-to-all-done) | copy-start | bytes 1572868
  897.3 17.4 all-to-all-start.1
  914.8 38.2 %all-to-all-start.2 = ((bf16[2,128,1024]{1,0,2:T(2,128)(2,1)}), bf16[2,128,1024]{1,0,2:T(2,128)(2,1)}, u32[]{:S(2)}, u32[]{:S(2)}) async-start(bf16[2,128,1024]{1,0,2:T(2,128)(2,1)} %copy.301), calls=%async_computation.2 | async-start | bytes 1048576 | tf_op jit(solution)/shard_map/all_to_all | solution.py:133
  947.8 29.6 copy-start.4
  956.4 31.1 %copy-start.20 = (bf16[2,1024,2,64]{1,3,2,0:T(8,128)(2,1)}, bf16[2,1024,2,64]{1,3,2,0:T(8,128)(2,1)S(1)}, u32[]{:S(2)}) copy-start(bf16[2,1024,2,64]{1,3,2,0:T(8,128)(2,1)S(1)} %reshape.1133) | copy-start | bytes 1572868
  988.3 504.6 %copy-start.71 = (bf16[1024]{0:T(1024)(128)(2,1)S(1)}, bf16[1024]{0:T(1024)(128)(2,1)}, u32[]{:S(2)}) copy-start(bf16[1024]{0:T(1024)(128)(2,1)} %get-tuple-element.1055) | copy-start | bytes 6148
  988.5 132.4 %collective-permute-start = (bf16[2,1024,2,64]{1,3,2,0:T(8,128)(2,1)}, bf16[2,1024,2,64]{1,3,2,0:T(8,128)(2,1)}, u32[]{:S(2)}, u32[]{:S(2)}) collective-permute-start(bf16[2,1024,2,64]{1,3,2,0:T(8,128)(2,1)} %get-tuple-element.1417), channel_id=1, source_target_pairs={{3,0},{0,1},{1,2},{2,3},{7,4},{4,5},{5,6},{6,7},{11,8},{8,9},{9,10... | collective-permute-start | bytes 1572872 | tf_op jit(solution)/shard_map/while/body/eval_jaxpr/ppermute | solution.py:19
  988.5 153.4 %collective-permute-start.1 = (bf16[2,1024,2,64]{1,3,2,0:T(8,128)(2,1)}, bf16[2,1024,2,64]{1,3,2,0:T(8,128)(2,1)}, u32[]{:S(2)}, u32[]{:S(2)}) collective-permute-start(bf16[2,1024,2,64]{1,3,2,0:T(8,128)(2,1)} %get-tuple-element.1418), channel_id=1, source_target_pairs={{3,0},{0,1},{1,2},{2,3},{7,4},{4,5},{5,6},{6,7},{11,8},{8,9},{9,10... | collective-permute-start | bytes 1572872 | tf_op jit(solution)/shard_map/while/body/eval_jaxpr/ppermute | solution.py:19
  1154.0 131.3 %collective-permute-start = (bf16[2,1024,2,64]{1,3,2,0:T(8,128)(2,1)}, bf16[2,1024,2,64]{1,3,2,0:T(8,128)(2,1)}, u32[]{:S(2)}, u32[]{:S(2)}) collective-permute-start(bf16[2,1024,2,64]{1,3,2,0:T(8,128)(2,1)} %get-tuple-element.1417), channel_id=1, source_target_pairs={{3,0},{0,1},{1,2},{2,3},{7,4},{4,5},{5,6},{6,7},{11,8},{8,9},{9,10... | collective-permute-start | bytes 1572872 | tf_op jit(solution)/shard_map/while/body/eval_jaxpr/ppermute | solution.py:19
  1154.1 152.3 %collective-permute-start.1 = (bf16[2,1024,2,64]{1,3,2,0:T(8,128)(2,1)}, bf16[2,1024,2,64]{1,3,2,0:T(8,128)(2,1)}, u32[]{:S(2)}, u32[]{:S(2)}) collective-permute-start(bf16[2,1024,2,64]{1,3,2,0:T(8,128)(2,1)} %get-tuple-element.1418), channel_id=1, source_target_pairs={{3,0},{0,1},{1,2},{2,3},{7,4},{4,5},{5,6},{6,7},{11,8},{8,9},{9,10... | collective-permute-start | bytes 1572872 | tf_op jit(solution)/shard_map/while/body/eval_jaxpr/ppermute | solution.py:19
  1318.5 132.4 %collective-permute-start = (bf16[2,1024,2,64]{1,3,2,0:T(8,128)(2,1)}, bf16[2,1024,2,64]{1,3,2,0:T(8,128)(2,1)}, u32[]{:S(2)}, u32[]{:S(2)}) collective-permute-start(bf16[2,1024,2,64]{1,3,2,0:T(8,128)(2,1)} %get-tuple-element.1417), channel_id=1, source_target_pairs={{3,0},{0,1},{1,2},{2,3},{7,4},{4,5},{5,6},{6,7},{11,8},{8,9},{9,10... | collective-permute-start | bytes 1572872 | tf_op jit(solution)/shard_map/while/body/eval_jaxpr/ppermute | solution.py:19
  1318.6 153.3 %collective-permute-start.1 = (bf16[2,1024,2,64]{1,3,2,0:T(8,128)(2,1)}, bf16[2,1024,2,64]{1,3,2,0:T(8,128)(2,1)}, u32[]{:S(2)}, u32[]{:S(2)}) collective-permute-start(bf16[2,1024,2,64]{1,3,2,0:T(8,128)(2,1)} %get-tuple-element.1418), channel_id=1, source_target_pairs={{3,0},{0,1},{1,2},{2,3},{7,4},{4,5},{5,6},{6,7},{11,8},{8,9},{9,10... | collective-permute-start | bytes 1572872 | tf_op jit(solution)/shard_map/while/body/eval_jaxpr/ppermute | solution.py:19
  1484.4 26.4 copy-start.34
  1486.9 20.7 all-to-all-start.3
  1492.9 40.3 %copy-start.47 = (f32[1024]{0:T(1024)}, f32[1024]{0:T(1024)S(1)}, u32[]{:S(2)}) copy-start(f32[1024]{0:T(1024)S(1)} %convert_element_type.186) | copy-start | bytes 12292
  1510.7 22.5 copy-start.25
  1510.8 22.4 copy-start.51
  1535.1 22.2 copy-start.8
  1537.2 18.5 all-to-all-start.4
  1541.4 914.9 %reduce-scatter.13.cloned.1.call-start = ((), (), s32[]{:S(2)}) async-start(), calls=%async_computation.23 | async-start | bytes 4325376 | tf_op jit(solution)/shard_map/reduce_scatter | solution.py:333
  1619.2 672.9 %copy-start.54 = (f32[2,128]{1,0:T(2,128)S(1)}, f32[2,128]{1,0:T(2,128)}, u32[]{:S(2)}) copy-start(f32[2,128]{1,0:T(2,128)} %copy-done.53) | copy-start | bytes 3076
  1619.2 672.9 %copy-start.50 = (f32[1024]{0:T(1024)S(1)}, f32[1024]{0:T(1024)}, u32[]{:S(2)}) copy-start(f32[1024]{0:T(1024)} %copy-done.49) | copy-start | bytes 12292
  1619.7 134.9 %collective-permute-start.2 = (bf16[2,1024,2,64]{1,3,2,0:T(8,128)(2,1)}, bf16[2,1024,2,64]{1,3,2,0:T(8,128)(2,1)S(1)}, u32[]{:S(2)}, u32[]{:S(2)}) collective-permute-start(bf16[2,1024,2,64]{1,3,2,0:T(8,128)(2,1)} %get-tuple-element.1467), channel_id=1, source_target_pairs={{3,0},{0,1},{1,2},{2,3},{7,4},{4,5},{5,6},{6,7},{11,8},{8,9},{9,10... | collective-permute-start | bytes 1572872 | tf_op jit(solution)/shard_map/while/body/eval_jaxpr/ppermute | solution.py:19
  1620.3 143.7 %collective-permute-start.3 = (bf16[2,1024,2,64]{1,3,2,0:T(8,128)(2,1)}, bf16[2,1024,2,64]{1,3,2,0:T(8,128)(2,1)S(1)}, u32[]{:S(2)}, u32[]{:S(2)}) collective-permute-start(bf16[2,1024,2,64]{1,3,2,0:T(8,128)(2,1)} %get-tuple-element.1468), channel_id=1, source_target_pairs={{3,0},{0,1},{1,2},{2,3},{7,4},{4,5},{5,6},{6,7},{11,8},{8,9},{9,10... | collective-permute-start | bytes 1572872 | tf_op jit(solution)/shard_map/while/body/eval_jaxpr/ppermute | solution.py:19
  1620.4 206.8 %collective-permute-start.4 = (bf16[2,1024,2,64]{1,3,2,0:T(8,128)(2,1)}, bf16[2,1024,2,64]{1,3,2,0:T(8,128)(2,1)}, u32[]{:S(2)}, u32[]{:S(2)}) collective-permute-start(bf16[2,1024,2,64]{1,3,2,0:T(8,128)(2,1)} %get-tuple-element.1469), channel_id=1, source_target_pairs={{3,0},{0,1},{1,2},{2,3},{7,4},{4,5},{5,6},{6,7},{11,8},{8,9},{9,10... | collective-permute-start | bytes 1572872 | tf_op jit(solution)/shard_map/while/body/eval_jaxpr/ppermute | solution.py:19
  1620.9 178.5 %collective-permute-start.5 = (bf16[2,1024,2,64]{1,3,2,0:T(8,128)(2,1)}, bf16[2,1024,2,64]{1,3,2,0:T(8,128)(2,1)}, u32[]{:S(2)}, u32[]{:S(2)}) collective-permute-start(bf16[2,1024,2,64]{1,3,2,0:T(8,128)(2,1)} %get-tuple-element.1470), channel_id=1, source_target_pairs={{3,0},{0,1},{1,2},{2,3},{7,4},{4,5},{5,6},{6,7},{11,8},{8,9},{9,10... | collective-permute-start | bytes 1572872 | tf_op jit(solution)/shard_map/while/body/eval_jaxpr/ppermute | solution.py:19
  1812.3 21.4 slice-start.4
  1840.0 135.0 %collective-permute-start.2 = (bf16[2,1024,2,64]{1,3,2,0:T(8,128)(2,1)}, bf16[2,1024,2,64]{1,3,2,0:T(8,128)(2,1)S(1)}, u32[]{:S(2)}, u32[]{:S(2)}) collective-permute-start(bf16[2,1024,2,64]{1,3,2,0:T(8,128)(2,1)} %get-tuple-element.1467), channel_id=1, source_target_pairs={{3,0},{0,1},{1,2},{2,3},{7,4},{4,5},{5,6},{6,7},{11,8},{8,9},{9,10... | collective-permute-start | bytes 1572872 | tf_op jit(solution)/shard_map/while/body/eval_jaxpr/ppermute | solution.py:19
  1840.6 143.9 %collective-permute-start.3 = (bf16[2,1024,2,64]{1,3,2,0:T(8,128)(2,1)}, bf16[2,1024,2,64]{1,3,2,0:T(8,128)(2,1)S(1)}, u32[]{:S(2)}, u32[]{:S(2)}) collective-permute-start(bf16[2,1024,2,64]{1,3,2,0:T(8,128)(2,1)} %get-tuple-element.1468), channel_id=1, source_target_pairs={{3,0},{0,1},{1,2},{2,3},{7,4},{4,5},{5,6},{6,7},{11,8},{8,9},{9,10... | collective-permute-start | bytes 1572872 | tf_op jit(solution)/shard_map/while/body/eval_jaxpr/ppermute | solution.py:19
  1841.1 206.5 %collective-permute-start.4 = (bf16[2,1024,2,64]{1,3,2,0:T(8,128)(2,1)}, bf16[2,1024,2,64]{1,3,2,0:T(8,128)(2,1)}, u32[]{:S(2)}, u32[]{:S(2)}) collective-permute-start(bf16[2,1024,2,64]{1,3,2,0:T(8,128)(2,1)} %get-tuple-element.1469), channel_id=1, source_target_pairs={{3,0},{0,1},{1,2},{2,3},{7,4},{4,5},{5,6},{6,7},{11,8},{8,9},{9,10... | collective-permute-start | bytes 1572872 | tf_op jit(solution)/shard_map/while/body/eval_jaxpr/ppermute | solution.py:19
  1841.2 178.6 %collective-permute-start.5 = (bf16[2,1024,2,64]{1,3,2,0:T(8,128)(2,1)}, bf16[2,1024,2,64]{1,3,2,0:T(8,128)(2,1)}, u32[]{:S(2)}, u32[]{:S(2)}) collective-permute-start(bf16[2,1024,2,64]{1,3,2,0:T(8,128)(2,1)} %get-tuple-element.1470), channel_id=1, source_target_pairs={{3,0},{0,1},{1,2},{2,3},{7,4},{4,5},{5,6},{6,7},{11,8},{8,9},{9,10... | collective-permute-start | bytes 1572872 | tf_op jit(solution)/shard_map/while/body/eval_jaxpr/ppermute | solution.py:19
  2060.4 134.8 %collective-permute-start.2 = (bf16[2,1024,2,64]{1,3,2,0:T(8,128)(2,1)}, bf16[2,1024,2,64]{1,3,2,0:T(8,128)(2,1)S(1)}, u32[]{:S(2)}, u32[]{:S(2)}) collective-permute-start(bf16[2,1024,2,64]{1,3,2,0:T(8,128)(2,1)} %get-tuple-element.1467), channel_id=1, source_target_pairs={{3,0},{0,1},{1,2},{2,3},{7,4},{4,5},{5,6},{6,7},{11,8},{8,9},{9,10... | collective-permute-start | bytes 1572872 | tf_op jit(solution)/shard_map/while/body/eval_jaxpr/ppermute | solution.py:19
  2061.0 143.6 %collective-permute-start.3 = (bf16[2,1024,2,64]{1,3,2,0:T(8,128)(2,1)}, bf16[2,1024,2,64]{1,3,2,0:T(8,128)(2,1)S(1)}, u32[]{:S(2)}, u32[]{:S(2)}) collective-permute-start(bf16[2,1024,2,64]{1,3,2,0:T(8,128)(2,1)} %get-tuple-element.1468), channel_id=1, source_target_pairs={{3,0},{0,1},{1,2},{2,3},{7,4},{4,5},{5,6},{6,7},{11,8},{8,9},{9,10... | collective-permute-start | bytes 1572872 | tf_op jit(solution)/shard_map/while/body/eval_jaxpr/ppermute | solution.py:19
  2061.6 206.3 %collective-permute-start.4 = (bf16[2,1024,2,64]{1,3,2,0:T(8,128)(2,1)}, bf16[2,1024,2,64]{1,3,2,0:T(8,128)(2,1)}, u32[]{:S(2)}, u32[]{:S(2)}) collective-permute-start(bf16[2,1024,2,64]{1,3,2,0:T(8,128)(2,1)} %get-tuple-element.1469), channel_id=1, source_target_pairs={{3,0},{0,1},{1,2},{2,3},{7,4},{4,5},{5,6},{6,7},{11,8},{8,9},{9,10... | collective-permute-start | bytes 1572872 | tf_op jit(solution)/shard_map/while/body/eval_jaxpr/ppermute | solution.py:19
  2062.1 178.0 %collective-permute-start.5 = (bf16[2,1024,2,64]{1,3,2,0:T(8,128)(2,1)}, bf16[2,1024,2,64]{1,3,2,0:T(8,128)(2,1)}, u32[]{:S(2)}, u32[]{:S(2)}) collective-permute-start(bf16[2,1024,2,64]{1,3,2,0:T(8,128)(2,1)} %get-tuple-element.1470), channel_id=1, source_target_pairs={{3,0},{0,1},{1,2},{2,3},{7,4},{4,5},{5,6},{6,7},{11,8},{8,9},{9,10... | collective-permute-start | bytes 1572872 | tf_op jit(solution)/shard_map/while/body/eval_jaxpr/ppermute | solution.py:19
  2253.0 21.4 slice-start.4
  2253.0 21.4 copy-start.9
  2286.0 24.7 copy-start.43
  2288.4 18.9 all-to-all-start.5
  2292.1 164.2 %reduce-scatter.7.cloned.1.call-start = ((), (), s32[]{:S(2)}) async-start(), calls=%async_computation.20 | async-start | bytes 4325376 | tf_op jit(solution)/shard_map/reduce_scatter | solution.py:330
  2310.6 31.9 %copy-start.42 = (bf16[2,1024,2,64]{1,3,2,0:T(8,128)(2,1)S(1)}, bf16[2,1024,2,64]{1,3,2,0:T(8,128)(2,1)}, u32[]{:S(2)}) copy-start(bf16[2,1024,2,64]{1,3,2,0:T(8,128)(2,1)} %get-tuple-element.1530) | copy-start | bytes 1572868
  2310.6 281.5 %reduce-scatter.9.cloned.1.call-start = ((), (), s32[]{:S(2)}) async-start(), calls=%async_computation.21 | async-start | bytes 4325376 | tf_op jit(solution)/shard_map/reduce_scatter | solution.py:331
  2310.7 11.5 collective-permute-start.6
  2342.4 37.1 %copy-start.26 = (f32[256,1024]{1,0:T(8,128)S(1)}, f32[256,1024]{1,0:T(8,128)}, u32[]{:S(2)}) copy-start(f32[256,1024]{1,0:T(8,128)} %copy-done.25) | copy-start | bytes 3145732
  2342.4 37.1 %copy-start.48 = (f32[1024]{0:T(1024)S(1)}, f32[1024]{0:T(1024)}, u32[]{:S(2)}) copy-start(f32[1024]{0:T(1024)} %copy-done.47) | copy-start | bytes 12292
  2342.4 37.1 %copy-start.52 = (f32[256]{0:T(256)S(1)}, f32[256]{0:T(256)}, u32[]{:S(2)}) copy-start(f32[256]{0:T(256)} %copy-done.51) | copy-start | bytes 3076
  2342.5 389.4 %reduce-scatter.11.cloned.1.call-start = ((), (), s32[]{:S(2)}) async-start(), calls=%async_computation.22 | async-start | bytes 4325376 | tf_op jit(solution)/shard_map/reduce_scatter | solution.py:332
  2342.5 11.1 collective-permute-start.7
  2379.5 534.0 %reduce-scatter.15.cloned.1.call-start = ((), (), s32[]{:S(2)}) async-start(), calls=%async_computation.24 | async-start | bytes 17301504 | tf_op jit(solution)/shard_map/reduce_scatter | solution.py:336
  2389.4 711.4 %reduce-scatter.17.cloned.1.call-start = ((), (), s32[]{:S(2)}) async-start(), calls=%async_computation.25 | async-start | bytes 17301504 | tf_op jit(solution)/shard_map/reduce_scatter | solution.py:337
  2409.5 45.7 %copy-start.17 = (f32[256,1024]{1,0:T(8,128)S(1)}, f32[256,1024]{1,0:T(8,128)}, u32[]{:S(2)}) copy-start(f32[256,1024]{1,0:T(8,128)} %copy-done.16) | copy-start | bytes 3145732
  2409.6 691.3 %copy-start.1 = (s32[257]{0:T(512)S(1)}, s32[257]{0:T(512)}, u32[]{:S(2)}) copy-start(s32[257]{0:T(512)} %param.19) | copy-start | bytes 3088
  (104 other events, 898.8 us)
Sparse Core Ops, SparseCore 0:
  10.9 59.0 all-gather.6
  72.9 55.2 all-gather.8
  131.0 55.2 all-gather.10
  189.0 55.2 all-gather.12
  246.9 76.3 all-gather.16
  326.0 76.0 all-gather.14
  1546.6 142.1 reduce-scatter.12
  2310.7 141.4 reduce-scatter.6
  2455.1 136.9 reduce-scatter.8
  2594.8 136.9 reduce-scatter.10
  2734.7 178.7 reduce-scatter.14
  2916.2 184.5 reduce-scatter.16
where the time goes:
time: 3130 us; the launch traced here: 3110 us
  local copies, waits for them, and re-layouts  1540 us (49%)
  waiting for transfers between devices  717 us (23%)
  matrix products  389 us (12%)
  other arithmetic  277 us (9%)
  blocking collectives  117 us (4%)
  starting transfers between devices  39.3 us (1%)
    broadcast_in_dim x182, local copies, waits for them, and re-layouts, bias_tile(): jnp.where(which[None] == kind, band_bias[:, kind][:, None, :, None, :], r...  722 us
    gather x1, local copies, waits for them, and re-layouts, band_tables(): bucket = jnp.take(bucket_table, lookup.reshape(-1), axis=0)  713 us
    reduce_scatter x1, waiting for transfers between devices, body(): lax.psum_scatter(grad_down, ('head', 'blk'), scatter_dimension=0, tiled=T...  187 us
    select_n x7, other arithmetic, bias_tile(): jnp.where(which[None] == kind, band_bias[:, kind][:, None, :, None, :], r...  182 us
    reduce_scatter x1, waiting for transfers between devices, body(): lax.psum_scatter(grad_in, ('head', 'blk'), scatter_dimension=0, tiled=True)  182 us
    reduce_scatter x1, waiting for transfers between devices, body(): lax.psum_scatter(grad_value, ('head', 'blk'), scatter_dimension=0, tiled=...  140 us
    reduce_scatter x1, waiting for transfers between devices, body(): lax.psum_scatter(grad_key, ('head', 'blk'), scatter_dimension=0, tiled=True)  136 us
    unnamed x2, blocking collectives  79.9 us
  transfers between devices with their start and end apart: 38, of which 11 were waited for; matrix products, arithmetic and copies ran while one was open for 70% of the time, Pallas kernels for 0%

commit v1 on v0

--- a/solution.py
+++ b/solution.py
@@ -1,14 +1,17 @@
+import functools
+
 import jax
 import jax.numpy as jnp
+import numpy as np
 from jax import lax
+from jax.experimental import pallas as pl
+from jax.experimental.pallas import tpu as pltpu
 from jax.sharding import PartitionSpec as P
 
 HEADS = 16
 HD = 64
 BUCKETS = 32
 MAXREL = 128
-
-
 EPS = 1e-06
 FLOOR = -1e30
 
@@ -85,7 +88,7 @@
     )
 
 
-def body(
+def ring_body(
     inputs,
     segments,
     bucket_table,
@@ -352,6 +355,692 @@
     )
 
 
+TQ = 512
+KT = 512
+MARGIN = 256
+AUG = 80
+NT = (((1,), (1,)), ((), ()))
+
+
+def nn(left, right):
+    return jnp.dot(left, right, preferred_element_type=jnp.float32)
+
+
+def flipped(block):
+    return block.astype(jnp.float32).T.astype(jnp.bfloat16)
+
+
+def ones_row(width):
+    first = lax.broadcasted_iota(jnp.int32, (AUG - HD, width), 0) == 0
+    return jnp.where(first, 1.0, 0.0).astype(jnp.bfloat16)
+
+
+def pieces_of(seq_count, part_len, groups):
+    for seq in range(seq_count):
+        for near in range(2):
+            for source in range(groups):
+                yield seq, near, source, slice((near * seq_count + seq) * part_len, (near * seq_count + seq + 1) * part_len)
+
+
+def lanes_of(ref, lead, tile_at, per_tile, part_len, lane_base):
+    parts = [ref[lead + (tile_at * per_tile + k, slice(None), pl.ds(lane_base, part_len))] for k in range(per_tile)]
+    return parts[0] if per_tile == 1 else jnp.concatenate(parts, axis=1)
+
+
+def tile_class(edge_ref, row, key_at, query_at):
+    first_start, last_start, first_end, last_end = (edge_ref[row * 4 + k] for k in range(4))
+    touched = (key_at + KT > first_start) & (key_at < last_end)
+    gap = key_at - query_at
+    whole = (key_at >= last_start) & (key_at + KT <= first_end)
+    plain = whole & ((gap + KT <= -MAXREL + 1) | (gap >= TQ + MAXREL - 1))
+    strip_at = jnp.clip(gap, -(KT + MARGIN), TQ + MARGIN) + KT + MARGIN
+    return touched, plain, gap, pl.ds(pl.multiple_of(strip_at, 256), KT)
+
+
+def masked(scores, bias, key_at, start_row, end_row):
+    places = lax.broadcasted_iota(jnp.int32, scores.shape, 0) + key_at
+    return jnp.where((places >= start_row) & (places < end_row), scores + bias, FLOOR)
+
+
+def attend_kernel(chips, base_ref, edge_ref, far_ref, q_ref, *refs):
+    kv_refs = refs[:chips]
+    start_ref, end_ref, bias_ref, o_ref, ob_ref, lse_ref, k_rows, v_aug, top_ref, acc_ref = refs[chips:]
+    groups, _, span = q_ref.shape
+    blocks, seq_count, span_len, _ = k_rows.shape
+    part_len = span_len // groups
+    per_tile = TQ // part_len
+    tiles, key_tiles = span_len // TQ, span_len // KT
+    per_key = KT // part_len
+    for far in range(chips):
+        for seq, near, source, lanes in pieces_of(seq_count, part_len, groups):
+            block = 2 * far + near
+            k_rows[block, seq, source * part_len : (source + 1) * part_len, :] = flipped(kv_refs[far][source, :HD, lanes])
+            at = source % per_key * part_len
+            v_aug[block, seq, source // per_key, :HD, at : at + part_len] = kv_refs[far][source, HD:, lanes]
+    for block in range(blocks):
+        for seq in range(seq_count):
+            for tile in range(key_tiles):
+                v_aug[block, seq, tile, HD:, :] = ones_row(KT)
+
+    for seq in range(seq_count):
+        for near in range(2):
+            lane_base = (near * seq_count + seq) * part_len
+
+            def query_tile(tile, _, seq=seq, near=near, lane_base=lane_base):
+                query_at = base_ref[near] + tile * TQ
+                row = (near * seq_count + seq) * tiles + tile
+                queries = lanes_of(q_ref, (), tile, per_tile, part_len, lane_base)
+                top_ref[...] = jnp.full_like(top_ref, FLOOR)
+                acc_ref[...] = jnp.zeros_like(acc_ref)
+                start_row = start_ref[near, seq, pl.ds(tile, 1), :]
+                end_row = end_ref[near, seq, pl.ds(tile, 1), :]
+
+                def take(scores, shift, block, key_tile):
+                    old_top = top_ref[0:1, :]
+                    new_top = jnp.maximum(old_top, jnp.max(scores, axis=0, keepdims=True) + shift)
+                    weights = jnp.exp(scores - (new_top - shift))
+                    acc_ref[...] = acc_ref[...] * jnp.exp(old_top - new_top) + nn(
+                        v_aug[block, seq, key_tile], weights.astype(jnp.bfloat16)
+                    )
+                    top_ref[0:1, :] = new_top
+
+                def key_step(step, _):
+                    block, key_tile = step // key_tiles, step % key_tiles
+                    key_at = base_ref[block] + key_tile * KT
+                    touched, plain, gap, strip = tile_class(edge_ref, row, key_at, query_at)
+
+                    def raw():
+                        keys = k_rows[block, seq, pl.ds(pl.multiple_of(key_tile * KT, KT), KT), :]
+                        return nn(keys, queries)
+
+                    @pl.when(touched & plain)
+                    def _():
+                        take(raw(), jnp.where(gap < 0, far_ref[0], far_ref[1]), block, key_tile)
+
+                    @pl.when(touched & jnp.logical_not(plain))
+                    def _():
+                        take(masked(raw(), bias_ref[strip, :], key_at, start_row, end_row), 0.0, block, key_tile)
+
+                    return 0
+
+                lax.fori_loop(0, blocks * key_tiles, key_step, 0)
+                total = acc_ref[HD : HD + 1, :]
+                outs = acc_ref[:HD, :] / total
+                lse_ref[near, seq, pl.ds(tile, 1), :] = top_ref[0:1, :] + jnp.log(total)
+                for k in range(per_tile):
+                    part = outs[:, k * part_len : (k + 1) * part_len]
+                    o_ref[tile * per_tile + k, :, lane_base : lane_base + part_len] = part
+                    ob_ref[tile * per_tile + k, :, lane_base : lane_base + part_len] = part.astype(jnp.bfloat16)
+                return 0
+
+            lax.fori_loop(0, tiles, query_tile, 0)
+
+
+def attend_back_kernel(chips, base_ref, edge_ref, far_ref, q_ref, g_ref, o_ref, lse_ref, *refs):
+    kv_refs = refs[:chips]
+    start_ref, end_ref, bias_ref, dq_ref = refs[chips : chips + 4]
+    dkv_refs = refs[chips + 4 : 2 * chips + 4]
+    band_ref, sides_ref, k_rows, v_rows, k_aug, dk_acc, dv_acc, dq_acc = refs[2 * chips + 4 :]
+    groups, _, span = q_ref.shape
+    blocks, seq_count, span_len, _ = k_rows.shape
+    part_len = span_len // groups
+    per_tile = TQ // part_len
+    tiles, key_tiles = span_len // TQ, span_len // KT
+    per_key = KT // part_len
+    for far in range(chips):
+        for seq, near, source, lanes in pieces_of(seq_count, part_len, groups):
+            block = 2 * far + near
+            rows = slice(source * part_len, (source + 1) * part_len)
+            piece = kv_refs[far][source, :HD, lanes]
+            k_rows[block, seq, rows, :] = flipped(piece)
+            v_rows[block, seq, rows, :] = flipped(kv_refs[far][source, HD:, lanes])
+            at = source % per_key * part_len
+            k_aug[block, seq, source // per_key, :HD, at : at + part_len] = piece
+    for block in range(blocks):
+        for seq in range(seq_count):
+            for tile in range(key_tiles):
+                k_aug[block, seq, tile, HD:, :] = ones_row(KT)
+    dk_acc[...] = jnp.zeros_like(dk_acc)
+    dv_acc[...] = jnp.zeros_like(dv_acc)
+    band_ref[...] = jnp.zeros_like(band_ref)
+    sides_ref[...] = jnp.zeros_like(sides_ref)
+
+    for seq in range(seq_count):
+        for near in range(2):
+            lane_base = (near * seq_count + seq) * part_len
+
+            def query_tile(tile, _, seq=seq, near=near, lane_base=lane_base):
+                query_at = base_ref[near] + tile * TQ
+                row = (near * seq_count + seq) * tiles + tile
+                queries = lanes_of(q_ref, (), tile, per_tile, part_len, lane_base)
+                grads = lanes_of(g_ref, (), tile, per_tile, part_len, lane_base)
+                outs = lanes_of(o_ref, (), tile, per_tile, part_len, lane_base)
+                delta = jnp.sum(grads.astype(jnp.float32) * outs, axis=0, keepdims=True)
+                query_rows, grad_rows = flipped(queries), flipped(grads)
+                lse = lse_ref[near, seq, pl.ds(tile, 1), :]
+                start_row = start_ref[near, seq, pl.ds(tile, 1), :]
+                end_row = end_ref[near, seq, pl.ds(tile, 1), :]
+                dq_acc[...] = jnp.zeros_like(dq_acc)
+
+                def take(scores, shift, block, key_tile):
+                    rows = pl.ds(pl.multiple_of(key_tile * KT, KT), KT)
+                    probs = jnp.exp(scores - (lse - shift))
+                    score_grad = probs * (nn(v_rows[block, seq, rows, :], grads) - delta)
+                    score_low = score_grad.astype(jnp.bfloat16)
+                    dv_acc[block, seq, rows, :] += nn(probs.astype(jnp.bfloat16), grad_rows)
+                    dk_acc[block, seq, rows, :] += nn(score_low, query_rows)
+                    made = nn(k_aug[block, seq, key_tile], score_low)
+                    dq_acc[...] += made
+                    return score_grad, made[HD : HD + 1, :]
+
+                def key_step(step, _):
+                    block, key_tile = step // key_tiles, step % key_tiles
+                    key_at = base_ref[block] + key_tile * KT
+                    touched, plain, gap, strip = tile_class(edge_ref, row, key_at, query_at)
+
+                    def raw():
+                        keys = k_rows[block, seq, pl.ds(pl.multiple_of(key_tile * KT, KT), KT), :]
+                        return nn(keys, queries)
+
+                    @pl.when(touched & plain)
+                    def _():
+                        _, sums = take(raw(), jnp.where(gap < 0, far_ref[0], far_ref[1]), block, key_tile)
+                        side = (gap > 0).astype(jnp.int32)
+                        sides_ref[pl.ds(side, 1), :] += sums
+
+                    @pl.when(touched & jnp.logical_not(plain))
+                    def _():
+                        whole_grad, _ = take(
+                            masked(raw(), bias_ref[strip, :], key_at, start_row, end_row), 0.0, block, key_tile
+                        )
+                        band_ref[strip, :] += whole_grad
+
+                    return 0
+
+                lax.fori_loop(0, blocks * key_tiles, key_step, 0)
+                for k in range(per_tile):
+                    part = dq_acc[:HD, k * part_len : (k + 1) * part_len].astype(jnp.bfloat16)
+                    dq_ref[tile * per_tile + k, :, lane_base : lane_base + part_len] = part
+                return 0
+
+            lax.fori_loop(0, tiles, query_tile, 0)
+    for far in range(chips):
+        for seq, near, source, lanes in pieces_of(seq_count, part_len, groups):
+            block = 2 * far + near
+            rows = slice(source * part_len, (source + 1) * part_len)
+            dkv_refs[far][source, :HD, lanes] = dk_acc[block, seq, rows, :].T.astype(jnp.bfloat16)
+            dkv_refs[far][source, HD:, lanes] = dv_acc[block, seq, rows, :].T.astype(jnp.bfloat16)
+
+
+def strip_places():
+    width = TQ + 128
+    lane = np.arange(width)
+    lane = np.where(lane < TQ, lane, lane - width)
+    offset = 128 * (np.arange(TQ // 128 + 2)[:, None] - 1) - lane[None, :]
+    return np.clip(offset, -MAXREL, MAXREL) + MAXREL
+
+
+def strip_kernel(far_ref, wave_ref, strip_ref):
+    near_blocks, _, width = wave_ref.shape
+    first = KT + MARGIN - 128
+    strip_ref[:first, :] = jnp.full((first, TQ), far_ref[0], jnp.float32)
+    for k in range(near_blocks):
+        spread = jnp.broadcast_to(wave_ref[k], (128, width))
+        turned = pltpu.roll(spread, 0, 1, stride=1, stride_axis=0)
+        strip_ref[first + 128 * k : first + 128 * (k + 1), :] = turned[:, :TQ]
+    last = first + 128 * near_blocks
+    strip_ref[last:, :] = jnp.full((strip_ref.shape[0] - last, TQ), far_ref[1], jnp.float32)
+
+
+def bias_strip(far_bias, waves):
+    return pl.pallas_call(
+        strip_kernel,
+        name="bias_strip",
+        out_shape=jax.ShapeDtypeStruct((2 * KT + 2 * MARGIN + TQ, TQ), jnp.float32),
+        in_specs=[SMEM, VMEM],
+        out_specs=VMEM,
+        compiler_params=pltpu.CompilerParams(vmem_limit_bytes=32 * 2**20),
+    )(far_bias, waves)
+
+
+def band_kernel(band_ref, sides_ref, near_ref, far_ref):
+    near_blocks, _, width = near_ref.shape
+    first = KT + MARGIN - 128
+    last = first + 128 * near_blocks
+    left = jnp.sum(band_ref[:first, :], axis=0, keepdims=True) + sides_ref[0:1, :]
+    right = jnp.sum(band_ref[last:, :], axis=0, keepdims=True) + sides_ref[1:2, :]
+    far_ref[...] = jnp.concatenate([left, right, jnp.zeros((6, TQ), jnp.float32)], axis=0)
+    for k in range(near_blocks):
+        rows = band_ref[first + 128 * k : first + 128 * (k + 1), :]
+        spread = jnp.concatenate([rows, jnp.zeros((128, width - TQ), jnp.float32)], axis=1)
+        row = lax.broadcasted_iota(jnp.int32, spread.shape, 0)
+        for step in (1, 2, 4):
+            spread = jnp.where((row & step) != 0, pltpu.roll(spread, width - step, 1), spread)
+        total = spread[:8, :]
+        for at in range(8, 128, 8):
+            total = total + pltpu.roll(spread[at : at + 8, :], width - at, 1)
+        near_ref[k] = jnp.sum(total, axis=0, keepdims=True)
+
+
+def band_sums_of(band, sides):
+    return pl.pallas_call(
+        band_kernel,
+        name="band_sums",
+        out_shape=(
+            jax.ShapeDtypeStruct((TQ // 128 + 2, 1, TQ + 128), jnp.float32),
+            jax.ShapeDtypeStruct((8, TQ), jnp.float32),
+        ),
+        in_specs=[VMEM, VMEM],
+        out_specs=(VMEM, VMEM),
+        compiler_params=pltpu.CompilerParams(vmem_limit_bytes=32 * 2**20),
+    )(band, sides)
+
+
+SMEM = pl.BlockSpec(memory_space=pltpu.SMEM)
+VMEM = pl.BlockSpec(memory_space=pltpu.VMEM)
+
+
+def attend(base, edges, far_bias, q, kvs, starts, ends, bias):
+    chips = len(kvs)
+    groups, _, span = q.shape
+    _, seq_count, tiles, _ = starts.shape
+    blocks, span_len = 2 * chips, tiles * TQ
+    return pl.pallas_call(
+        functools.partial(attend_kernel, chips),
+        name="attend",
+        out_shape=(
+            jax.ShapeDtypeStruct(q.shape, jnp.float32),
+            jax.ShapeDtypeStruct(q.shape, jnp.bfloat16),
+            jax.ShapeDtypeStruct(starts.shape, jnp.float32),
+        ),
+        in_specs=[SMEM] * 3 + [VMEM] * (1 + chips + 3),
+        out_specs=(VMEM,) * 3,
+        scratch_shapes=[
+            pltpu.VMEM((blocks, seq_count, span_len, HD), jnp.bfloat16),
+            pltpu.VMEM((blocks, seq_count, span_len // KT, AUG, KT), jnp.bfloat16),
+            pltpu.VMEM((8, TQ), jnp.float32),
+            pltpu.VMEM((AUG, TQ), jnp.float32),
+        ],
+        compiler_params=pltpu.CompilerParams(vmem_limit_bytes=48 * 2**20),
+    )(base, edges, far_bias, q, *kvs, starts, ends, bias)
+
+
+def attend_back(base, edges, far_bias, q, g, o, lse, kvs, starts, ends, bias):
+    chips = len(kvs)
+    groups, _, span = q.shape
+    _, seq_count, tiles, _ = starts.shape
+    blocks, span_len = 2 * chips, tiles * TQ
+    low = jax.ShapeDtypeStruct(q.shape, jnp.bfloat16)
+    made = pl.pallas_call(
+        functools.partial(attend_back_kernel, chips),
+        name="attend_back",
+        out_shape=(low,)
+        + (jax.ShapeDtypeStruct(kvs[0].shape, jnp.bfloat16),) * chips
+        + (jax.ShapeDtypeStruct(bias.shape, jnp.float32), jax.ShapeDtypeStruct((8, TQ), jnp.float32)),
+        in_specs=[SMEM] * 3 + [VMEM] * (4 + chips + 3),
+        out_specs=(VMEM,) * (3 + chips),
+        scratch_shapes=[
+            pltpu.VMEM((blocks, seq_count, span_len, HD), jnp.bfloat16),
+            pltpu.VMEM((blocks, seq_count, span_len, HD), jnp.bfloat16),
+            pltpu.VMEM((blocks, seq_count, span_len // KT, AUG, KT), jnp.bfloat16),
+            pltpu.VMEM((blocks, seq_count, span_len, HD), jnp.float32),
+            pltpu.VMEM((blocks, seq_count, span_len, HD), jnp.float32),
+            pltpu.VMEM((AUG, TQ), jnp.float32),
+        ],
+        compiler_params=pltpu.CompilerParams(vmem_limit_bytes=56 * 2**20),
+    )(base, edges, far_bias, q, g, o, lse, *kvs, starts, ends, bias)
+    return made[0], made[1 : 1 + chips], made[-2], made[-1]
+
+
+AXES = ("head", "blk")
+
+
+def trade(block, axis, bit):
+    size = lax.axis_size(axis)
+    return lax.ppermute(block, axis, [(i, i ^ bit) for i in range(size)])
+
+
+def mate(block):
+    return trade(block, "blk", 1)
+
+
+def across_x(block):
+    return trade(block, "blk", 2)
+
+
+def across_y(block):
+    return trade(block, "head", 1)
+
+
+def across_z(block, distance):
+    return trade(block, "head", 2 * distance)
+
+
+def copy_kernel(plan, slots_ref, *arrays):
+    for source, source_rows, target, target_rows, count in plan:
+        views = []
+        for which, (slot, scale, first, columns) in ((source, source_rows), (target, target_rows)):
+            begin = first if slot is None else pl.multiple_of(slots_ref[slot] * scale, 16) + first
+            views.append(arrays[which].at[pl.ds(begin, count), pl.ds(columns[0], columns[1])])
+        views[1][...] = views[0][...]
+
+
+def moved(name, slots, sources, shapes, plan):
+    outs = tuple(jax.ShapeDtypeStruct(shape, jnp.bfloat16) for shape in shapes)
+    return pl.pallas_call(
+        functools.partial(copy_kernel, plan),
+        name=name,
+        out_shape=outs,
+        in_specs=[SMEM] + [VMEM] * len(sources),
+        out_specs=(VMEM,) * len(outs),
+        compiler_params=pltpu.CompilerParams(vmem_limit_bytes=40 * 2**20),
+    )(slots, *sources)
+
+
+DEPTH = 4
+CHIPS = 16
+
+
+def relative_slots():
+    n_blk = lax.axis_size("blk")
+    chip = lax.axis_index("head") * (n_blk // 2) + lax.axis_index("blk") // 2
+    turns = [4 * z + 2 * y + x for y, x in ((0, 0), (0, 1), (1, 0), (1, 1)) for z in range(DEPTH)]
+    return chip ^ jnp.asarray(turns, jnp.int32)
+
+
+def piece_rows(rows):
+    for k in range(CHIPS):
+        group, z = k // DEPTH, k % DEPTH
+        if group < 3:
+            yield k, group, z * rows
+        else:
+            yield k, 3 + z // 2, z % 2 * rows
+
+
+def spread_out(name, slots, payload, parts):
+    layout, shapes = parts
+    rows, width = payload.shape
+    own = jnp.concatenate([payload] + [across_z(payload, k) for k in range(1, DEPTH)], axis=0)
+    by_x, by_y = across_x(own), across_y(own)
+    half = DEPTH // 2 * rows
+    low, high = across_y(by_x[:half]), across_x(by_y[half:])
+    plan = []
+    for k, piece, at in piece_rows(rows):
+        for first, count, whole, take, put in layout:
+            plan.append(
+                (piece, (None, 0, at + first, take), 5 + whole, (k, count if put[2] is None else put[2], put[1], put[0]), count)
+            )
+    return moved(name, slots, (own, by_x, by_y, low, high), shapes, tuple(plan))
+
+
+def drawn_in(name, slots, wholes, layout, rows, width):
+    plan = []
+    for k, piece, at in piece_rows(rows):
+        for first, count, whole, take, put in layout:
+            plan.append(
+                (whole, (k, count if put[2] is None else put[2], put[1], put[0]), len(wholes) + piece, (None, 0, at + first, take), count)
+            )
+    full, half = DEPTH * rows, DEPTH // 2 * rows
+    shapes = ((full, width),) * 3 + ((half, width),) * 2
+    own, by_x, by_y, low, high = moved(name, slots, wholes, shapes, tuple(plan))
+    low, high = across_y(low), across_x(high)
+    wide = lambda block: block.astype(jnp.float32)
+    by_x = jnp.concatenate([(wide(by_x[:half]) + wide(low)).astype(jnp.bfloat16), by_x[half:]], axis=0)
+    by_y = jnp.concatenate([by_y[:half], (wide(by_y[half:]) + wide(high)).astype(jnp.bfloat16)], axis=0)
+    by_x, by_y = across_x(by_x), across_y(by_y)
+    column = wide(own) + wide(by_x) + wide(by_y)
+    total = column[:rows]
+    for k in range(1, DEPTH):
+        total = total + wide(across_z(column[k * rows : (k + 1) * rows].astype(jnp.bfloat16), k))
+    return total
+
+
+def document_bounds(segments):
+    seq_count, blocks, span_len = segments.shape
+    length = blocks * span_len
+    numbers = lax.iota(jnp.int32, length // min(512, length) + 2)
+    flat = segments.reshape(seq_count, length)
+    below = jnp.sum((flat[:, :, None] < numbers).astype(jnp.int32), axis=1)
+    here = flat[:, :, None] == numbers[:-1]
+    starts = jnp.sum(jnp.where(here, below[:, None, :-1], 0), axis=2)
+    ends = jnp.sum(jnp.where(here, below[:, None, 1:], 0), axis=2)
+    return starts.reshape(segments.shape), ends.reshape(segments.shape)
+
+
+def query_bounds(bounds, place, tile):
+    near = [lax.dynamic_index_in_dim(bounds, place ^ k, 1, keepdims=False) for k in range(2)]
+    near = jnp.stack(near, axis=0)
+    return near.reshape(near.shape[0], near.shape[1], -1, tile)
+
+
+def gelu_both(values):
+    slope = float(np.sqrt(2.0 / np.pi))
+    square = values * values
+    curve = jnp.tanh(slope * values * (1.0 + 0.044715 * square))
+    half = 0.5 * (1.0 + curve)
+    rise = half + 0.5 * values * (1.0 - curve * curve) * (slope * (1.0 + 3 * 0.044715 * square))
+    return values * half, rise
+
+
+def joined(block):
+    return jnp.concatenate([block, mate(block)], axis=0)
+
+
+def halves_added(block):
+    half = block.shape[0] // 2
+    return block[:half] + mate(block[half:])
+
+
+def norm_back(grad, rows, scale, gain):
+    weighted = grad * gain
+    inner = jnp.mean(rows * weighted, axis=-1, keepdims=True)
+    return scale * weighted - rows * (scale * scale * scale) * inner, jnp.sum(grad * rows * scale, axis=0)
+
+
+def dot_on(left, right, left_dim, right_dim):
+    return lax.dot_general(left, right, (((left_dim,), (right_dim,)), ((), ())), preferred_element_type=jnp.float32)
+
+
+def pair_body(
+    inputs,
+    segments,
+    bucket_table,
+    norm_gain,
+    w_query,
+    w_key,
+    w_value,
+    w_out,
+    rel_bias,
+    ff_gain,
+    w_in,
+    w_down,
+    cotangent,
+):
+    low = jnp.bfloat16
+    seq_count, _, part_len, width = inputs.shape
+    groups = lax.axis_size("head")
+    span_len = part_len * groups
+    blocks = lax.axis_size("blk")
+    group, place = lax.axis_index("head"), lax.axis_index("blk")
+    core, side = place % 2, place // 2
+    slots = relative_slots()
+    shard = w_query.shape[0]
+    chip_rows = 2 * shard
+    half_width = groups * HD
+    hidden = w_in.shape[1]
+    half_hidden = hidden // 2
+    down_rows = w_down.shape[0]
+
+    def by_core(first, second):
+        return jnp.where(core == 0, first, second)
+
+    def head_columns(weight, which):
+        return weight.reshape(shard, groups, 2, HD)[:, :, which]
+
+    def cut(which):
+        key_value = jnp.stack([head_columns(w_key, which), head_columns(w_value, which)], axis=2).reshape(shard, -1)
+        query = head_columns(w_query, which).reshape(shard, -1)
+        hidden_in = w_in.reshape(shard, -1, 2, down_rows)[:, :, which].reshape(shard, -1)
+        return jnp.concatenate([key_value, query, hidden_in], axis=1)
+
+    first_cut, second_cut = cut(0), cut(1)
+    gains = jnp.concatenate([norm_gain, ff_gain, rel_bias, jnp.zeros((128 - 5 * shard // 2,), low)])
+    gains = jnp.pad(gains[None, :], ((0, shard - 1), (0, 0)))
+    kept = jnp.concatenate([by_core(first_cut, second_cut), gains], axis=1)
+    given = mate(jnp.concatenate([by_core(second_cut, first_cut), gains], axis=1))
+    chip_cut = jnp.concatenate([by_core(kept, given), by_core(given, kept)], axis=0)
+    edge_kv, edge_q, edge_in = 2 * half_width, 3 * half_width, 3 * half_width + half_hidden
+    gain_rows = jnp.stack([chip_cut[0, edge_in:], chip_cut[shard, edge_in:]], axis=0)
+    gain_rows = jnp.pad(gain_rows, ((0, 14), (0, width - 128)))
+    payload_kv = jnp.concatenate([chip_cut[:, :edge_kv], gain_rows], axis=0)
+    cut_q = chip_cut[:, edge_kv:edge_q]
+    payload_q = jnp.concatenate([cut_q[:shard], cut_q[shard:]], axis=1)
+    cut_in = chip_cut[:, edge_q:edge_in]
+    swap = [(b, (b % 2) * 2 + b // 2) for b in range(blocks)]
+    payload_in = jnp.concatenate([cut_in[:, :width], cut_in[:, width:], lax.ppermute(w_out, "blk", swap)], axis=0)
+
+    every = (0, width)
+    lay_kv = ((0, chip_rows, 0, every, (every, 0, None)), (chip_rows, 16, 1, (0, 128), ((0, 128), 0, None)))
+    lay_q = (
+        (0, shard, 0, (0, half_width), ((0, half_width), 0, chip_rows)),
+        (0, shard, 0, (half_width, half_width), ((0, half_width), shard, chip_rows)),
+    )
+    lay_in = (
+        (0, chip_rows, 0, every, ((0, width), 0, None)),
+        (chip_rows, chip_rows, 0, every, ((width, width), 0, None)),
+        (2 * chip_rows, shard, 1, every, (every, 0, None)),
+    )
+    lay_down = ((0, down_rows, 0, every, (every, 0, None)),)
+    kv_w, gain_w = spread_out("whole_kv", slots, payload_kv, (lay_kv, ((width, width), (16 * CHIPS, 128))))
+    (query_w,) = spread_out("whole_q", slots, payload_q, (lay_q, ((width, half_width),)))
+    in_w, out_w = spread_out("whole_in", slots, payload_in, (lay_in, ((width, half_hidden), (half_width, width))))
+    (down_w,) = spread_out("whole_down", slots, w_down, (lay_down, ((half_hidden, width),)))
+
+    gain_w = gain_w.reshape(CHIPS, 16, 128)[:, :2].astype(jnp.float32)
+    gain_one = gain_w[:, :, :shard].reshape(-1)
+    gain_two = gain_w[:, :, shard : 2 * shard].reshape(-1)
+    rel_table = gain_w[:, :, 2 * shard : 5 * shard // 2].reshape(HEADS, BUCKETS)
+    rel_here = lax.dynamic_index_in_dim(rel_table, 2 * group + core, 0, keepdims=False)
+
+    bucket_hot = bucket_table[:, None] == lax.iota(jnp.int32, BUCKETS)[None, :]
+    by_offset = jnp.sum(jnp.where(bucket_hot, rel_here[None, :], 0.0), axis=1)
+    places = strip_places()
+    place_hot = jnp.asarray(places.reshape(-1))[:, None] == lax.iota(jnp.int32, 2 * MAXREL + 1)[None, :]
+    place_hot = place_hot.astype(jnp.float32)
+    waves = jnp.dot(place_hot, by_offset, precision=lax.Precision.HIGHEST)
+    waves = waves.reshape(places.shape[0], 1, places.shape[1])
+    far_bias = jnp.stack([by_offset[0], by_offset[-1]])
+    bias = bias_strip(far_bias, waves)
+    starts, ends = document_bounds(segments)
+    starts, ends = query_bounds(starts, place, TQ), query_bounds(ends, place, TQ)
+    edges = jnp.stack([starts[..., 0], starts[..., -1], ends[..., 0], ends[..., -1]], axis=-1).reshape(-1)
+    base = (place ^ lax.iota(jnp.int32, blocks)) * span_len
+
+    token_rows = inputs.reshape(-1, width).astype(jnp.float32)
+    scale_one = lax.rsqrt(jnp.mean(token_rows * token_rows, axis=-1, keepdims=True) + EPS)
+    first_in = joined((token_rows * scale_one * gain_one).astype(low))
+    tokens = first_in.shape[0]
+
+    def exchanged(block):
+        return lax.all_to_all(block, "head", split_axis=0, concat_axis=0, tiled=True)
+
+    key_value = exchanged(dot_on(kv_w, first_in, 0, 1).astype(low).reshape(groups, 2 * HD, tokens))
+    queries = exchanged(dot_on(query_w, first_in, 0, 1).astype(low).reshape(groups, HD, tokens))
+    kvs = [key_value, across_x(key_value)]
+    attended, attended_low, lse = attend(base, edges, far_bias, queries, kvs, starts, ends, bias)
+    attn_cols = exchanged(attended_low).reshape(half_width, tokens)
+
+    hidden_one = token_rows + halves_added(dot_on(attn_cols, out_w, 0, 0))
+    scale_two = lax.rsqrt(jnp.mean(hidden_one * hidden_one, axis=-1, keepdims=True) + EPS)
+    second_in = joined((hidden_one * scale_two * gain_two).astype(low))
+    activated, rise = gelu_both(dot_on(second_in, in_w, 1, 0))
+    activated = activated.astype(low)
+    layer_out = (hidden_one + halves_added(dot_on(activated, down_w, 1, 0))).astype(low).reshape(inputs.shape)
+
+    incoming_low = cotangent.reshape(-1, width)
+    incoming = joined(incoming_low)
+    up_grad = (dot_on(incoming, down_w, 1, 1) * rise).astype(low)
+    second_grad = halves_added(dot_on(up_grad, in_w, 1, 1))
+    hidden_part, grad_gain_two = norm_back(second_grad, hidden_one, scale_two, gain_two)
+    hidden_grad = incoming_low.astype(jnp.float32) + hidden_part
+    branch = joined(hidden_grad.astype(low))
+    grad_cols = dot_on(out_w, branch, 1, 1).astype(low).reshape(groups, HD, tokens)
+    grad_heads = exchanged(grad_cols)
+
+    whole_down = dot_on(activated, incoming, 0, 0).astype(low)
+    grad_down = drawn_in("parts_down", slots, (whole_down,), lay_down, down_rows, width)
+    whole_in = dot_on(second_in, up_grad, 0, 0).astype(low)
+    whole_out = dot_on(attn_cols, branch, 1, 0).astype(low)
+    in_sum = drawn_in("parts_in", slots, (whole_in, whole_out), lay_in, 2 * chip_rows + shard, width)
+
+    query_grad, kv_grads, band, sides = attend_back(
+        base, edges, far_bias, queries, grad_heads, attended, lse, kvs, starts, ends, bias
+    )
+    kv_grad = (kv_grads[0].astype(jnp.float32) + across_x(kv_grads[1]).astype(jnp.float32)).astype(low)
+    kv_cols = exchanged(kv_grad).reshape(2 * half_width, tokens)
+    query_cols = exchanged(query_grad).reshape(half_width, tokens)
+    first_grad = halves_added(dot_on(kv_cols, kv_w, 0, 1) + dot_on(query_cols, query_w, 0, 1))
+    input_part, grad_gain_one = norm_back(first_grad, token_rows, scale_one, gain_one)
+    input_grad = (hidden_grad + input_part).astype(low).reshape(inputs.shape)
+
+    whole_kv = dot_on(first_in, kv_cols, 0, 1).astype(low)
+    kv_sum = drawn_in("parts_kv", slots, (whole_kv,), lay_kv[:1], chip_rows, width)
+    whole_q = dot_on(first_in, query_cols, 0, 1).astype(low)
+    gain_grads = jnp.stack([grad_gain_one.reshape(CHIPS, -1), grad_gain_two.reshape(CHIPS, -1)], axis=1)
+    gain_grads = jnp.pad(gain_grads.astype(low), ((0, 0), (0, 14), (0, 128 - chip_rows))).reshape(-1, 128)
+    lay_last = lay_q + ((shard, 16, 1, (0, 128), ((0, 128), 0, None)),)
+    q_sum = drawn_in("parts_q", slots, (whole_q, gain_grads), lay_last, shard + 16, width)
+
+    def rows_of(block, which):
+        return block[which * shard : (which + 1) * shard]
+
+    q_rows = jnp.concatenate([q_sum[:shard, :half_width], q_sum[:shard, half_width:]], axis=0)
+    in_rows = jnp.concatenate([in_sum[:chip_rows], in_sum[chip_rows : 2 * chip_rows]], axis=1)
+    gain_sum = jnp.pad(q_sum[shard : shard + 2, :128], ((0, shard - 2), (0, 0)))
+
+    def traded(block):
+        mine = by_core(rows_of(block, 0), rows_of(block, 1))
+        other = mate(by_core(rows_of(block, 1), rows_of(block, 0)))
+        return by_core(mine, other), by_core(other, mine)
+
+    kv_pair = jnp.stack(traded(kv_sum), axis=0).reshape(2, shard, groups, 2, HD)
+    q_pair = jnp.stack(traded(q_rows), axis=0).reshape(2, shard, groups, HD)
+    in_pair = jnp.stack(traded(in_rows), axis=0).reshape(2, shard, -1, down_rows)
+    grad_query = q_pair.transpose(1, 2, 0, 3).reshape(shard, -1)
+    grad_key = kv_pair[:, :, :, 0].transpose(1, 2, 0, 3).reshape(shard, -1)
+    grad_value = kv_pair[:, :, :, 1].transpose(1, 2, 0, 3).reshape(shard, -1)
+    grad_in = in_pair.transpose(1, 2, 0, 3).reshape(shard, -1)
+    back_swap = [(b, (b % 2) * 2 + b // 2) for b in range(blocks)]
+    grad_out = lax.ppermute(in_sum[2 * chip_rows :], "blk", back_swap)
+    gain_sum = gain_sum + mate(gain_sum)
+    gain_mine = by_core(gain_sum[:2, :shard], gain_sum[:2, shard : 2 * shard])
+
+    near_sums, far_sums = band_sums_of(band, sides)
+    offset_sums = jnp.dot(near_sums.reshape(-1), place_hot, precision=lax.Precision.HIGHEST)
+    far_sums = jnp.sum(far_sums, axis=1)
+    end_hot = lax.iota(jnp.int32, 2 * MAXREL + 1)
+    offset_sums = offset_sums + jnp.where(end_hot == 0, far_sums[0], 0.0) + jnp.where(end_hot == 2 * MAXREL, far_sums[1], 0.0)
+    rel_grad = jnp.sum(jnp.where(bucket_hot, offset_sums[:, None], 0.0), axis=0)
+    rel_grad = jnp.pad(rel_grad[None, :], ((0, 7), (0, 128 - BUCKETS)))
+    from_mate, from_x, from_corner = mate(rel_grad), across_x(rel_grad), trade(rel_grad, "blk", 3)
+    rel_sum = jnp.where(core == side, rel_grad + from_x, from_mate + from_corner)[0]
+    rel_mine = by_core(rel_sum[: BUCKETS // 2], rel_sum[BUCKETS // 2 : BUCKETS])
+
+    return (
+        layer_out,
+        input_grad,
+        gain_mine[0],
+        grad_query,
+        grad_key,
+        grad_value,
+        grad_out,
+        rel_mine,
+        gain_mine[1],
+        grad_in,
+        grad_down,
+    )
+
+
 def solution(mesh):
     placed = (
         P(None, "blk", "head", None),
@@ -368,8 +1057,10 @@
         P(("head", "blk"), None),
         P(None, "blk", "head", None),
     )
+    n_head, n_blk = mesh.shape["head"], mesh.shape["blk"]
+    paired = HEADS == 2 * n_head and (n_head, n_blk) == (8, 4)
     return jax.shard_map(
-        body,
+        pair_body if paired else ring_body,
         mesh=mesh,
         in_specs=placed,
         out_specs=(

time: 3130 us -> 619 us (0.20)
  local copies, waits for them, and re-layouts: 1540 us -> 48.7 us
  waiting for transfers between devices: 717 us -> 247 us
  matrix products: 389 us -> 47.2 us
  other arithmetic: 277 us -> 36.1 us
  blocking collectives: 117 us -> 0 us
  Pallas kernels: 0 us -> 96.8 us
  starting transfers between devices: 39.3 us -> 132 us
    broadcast_in_dim x183 -> x2, local copies, waits for them, and re-layouts: 722 us -> 0.01 us  [the longest x1 0.01 us: pair_body(): by_offset = jnp.sum(jnp.where(bucket_hot, rel_here[None, :], 0.0), axis=1)]
    gather x1 -> x0, local copies, waits for them, and re-layouts: 713 us -> none  [band_tables(): bucket = jnp.take(bucket_table, lookup.reshape(-1), axis=0)]
    reduce_scatter x6 -> x0, waiting for transfers between devices: 645 us -> none  [the longest x1 187 us: body(): lax.psum_scatter(grad_down, ('head', 'blk'), scatter_dimension=0, tiled=T...]
    dot_general x50 -> x17, matrix products: 389 us -> 47.2 us  [the longest x15 43.8 us: dot_on(): lax.dot_general(left, right, (((left_dim,), (right_dim,)), ((), ())), pre...]
    ppermute x20 -> x76, waiting for transfers between devices: 22.5 us -> 226 us  [the longest x74 226 us: trade(): return lax.ppermute(block, axis, [(i, i ^ bit) for i in range(size)])]
    select_n x9 -> x10, other arithmetic: 183 us -> 0.88 us  [the longest x9 0.88 us: by_core(): return jnp.where(core == 0, first, second)]
    pallas_call x0 -> x12, Pallas kernels: none -> 96.8 us  [the longest x1 50.3 us: attend_back(): pl.pallas_call(functools.partial(attend_back_kernel, chips), name='attend...]
    unnamed x2 -> x0, blocking collectives: 79.9 us -> none
  transfers between devices with their start and end apart: 38 -> 82, of which waited for: 11 -> 38; matrix products, arithmetic and copies ran while one was open for 70% -> 16% of each run, Pallas kernels for 0% -> 16%
where the time goes in v1:
time: 619 us; the launch traced here: 610 us
  waiting for transfers between devices  247 us (40%)
  starting transfers between devices  132 us (21%)
  Pallas kernels  96.8 us (16%)
  local copies, waits for them, and re-layouts  48.7 us (8%)
  matrix products  47.2 us (8%)
  other arithmetic  36.1 us (6%)
    ppermute x74, waiting for transfers between devices, trade(): return lax.ppermute(block, axis, [(i, i ^ bit) for i in range(size)])  226 us
    ppermute x74, starting transfers between devices, trade(): return lax.ppermute(block, axis, [(i, i ^ bit) for i in range(size)])  83.5 us
    pallas_call x1, Pallas kernels, attend_back(): pl.pallas_call(functools.partial(attend_back_kernel, chips), name='attend...  50.3 us
    all_to_all x6, starting transfers between devices, exchanged(): lax.all_to_all(block, 'head', split_axis=0, concat_axis=0, tiled=True)  45.7 us
    dot_general x15, matrix products, dot_on(): lax.dot_general(left, right, (((left_dim,), (right_dim,)), ((), ())), pre...  43.8 us
    pallas_call x1, Pallas kernels, attend(): pl.pallas_call(functools.partial(attend_kernel, chips), name='attend', ou...  33.1 us
    all_to_all x6, waiting for transfers between devices, exchanged(): lax.all_to_all(block, 'head', split_axis=0, concat_axis=0, tiled=True)  21 us
    unnamed x136, local copies, waits for them, and re-layouts  18.1 us
  transfers between devices with their start and end apart: 82, of which 38 were waited for; matrix products, arithmetic and copies ran while one was open for 16% of the time, Pallas kernels for 16%

profile of v1, /device:TPU:0, one launch (start us, length us, event | category | flops | bytes accessed | tf_op | source)
XLA Modules:
  0.0 610.0 jit_solution(8689147472301828468)
XLA Ops:
  11.2 3.0 collective-permute-start.1
  14.2 2.6 collective-permute-start.2
  16.8 4.7 collective-permute-done.1
  21.5 7.7 %collective-permute-done.2 = bf16[80,1024]{1,0:T(8,128)(2,1)S(1)} collective-permute-done((bf16[80,1024]{1,0:T(8,128)(2,1)S(1)}, bf16[80,1024]{1,0:T(8,128)(2,1)S(1)}, u32[]{:S(2)}, u32[]{:S(2)}) %collective-permute-start.2) | collective-permute-done | bytes 163872 | tf_op jit(solution)/shard_map/ppermute | solution.py:700
  32.3 11.7 %collective-permute-done.5.arrays_2_ = bf16[320,1024]{1,0:T(8,128)(2,1)S(1)} collective-permute-done((bf16[320,1024]{1,0:T(8,128)(2,1)S(1)}, bf16[320,1024]{1,0:T(8,128)(2,1)S(1)}, u32[]{:S(2)}, u32[]{:S(2)}) %collective-permute-start.5) | collective-permute-done | bytes 655392 | tf_op jit(solution)/shard_map/ppermute | solution.py:700
  47.4 4.9 collective-permute-done.7.arrays_4_
  58.5 4.1 convolution_convert_fusion.3
  62.6 6.6 %all-to-all-start.1 = ((bf16[8,128,512]{2,1,0:T(8,128)(2,1)}), bf16[8,128,512]{2,1,0:T(8,128)(2,1)S(1)}, u32[]{:S(2)}, u32[]{:S(2)}) async-start(bf16[8,128,512]{2,1,0:T(8,128)(2,1)} %bitcast.10), calls=%async_computation.1 | async-start | bytes 2097152 | tf_op jit(solution)/shard_map/all_to_all | solution.py:945
  69.4 3.9 collective-permute-start.10
  75.4 18.1 %collective-permute-done.10 = bf16[32,1024]{1,0:T(8,128)(2,1)S(1)} collective-permute-done((bf16[32,1024]{1,0:T(8,128)(2,1)S(1)}, bf16[32,1024]{1,0:T(8,128)(2,1)S(1)}, u32[]{:S(2)}, u32[]{:S(2)}) %collective-permute-start.10) | collective-permute-done | bytes 65568 | tf_op jit(solution)/shard_map/ppermute | solution.py:700
  93.4 8.7 %collective-permute-done.9 = bf16[32,1024]{1,0:T(8,128)(2,1)S(1)} collective-permute-done((bf16[32,1024]{1,0:T(8,128)(2,1)S(1)}, bf16[32,1024]{1,0:T(8,128)(2,1)S(1)}, u32[]{:S(2)}, u32[]{:S(2)}) %collective-permute-start.9) | collective-permute-done | bytes 65568 | tf_op jit(solution)/shard_map/ppermute | solution.py:700
  106.2 4.2 collective-permute-done.12.arrays_2_
  113.0 13.8 %collective-permute-done.19 = bf16[160,1024]{1,0:T(8,128)(2,1)S(1)} collective-permute-done((bf16[160,1024]{1,0:T(8,128)(2,1)S(1)}, bf16[160,1024]{1,0:T(8,128)(2,1)S(1)}, u32[]{:S(2)}, u32[]{:S(2)}) %collective-permute-start.19) | collective-permute-done | bytes 327712 | tf_op jit(solution)/shard_map/ppermute | solution.py:700
  133.7 9.0 %all-to-all-start = ((bf16[8,64,512]{2,1,0:T(8,128)(2,1)}), bf16[8,64,512]{2,1,0:T(8,128)(2,1)S(1)}, u32[]{:S(2)}, u32[]{:S(2)}) async-start(bf16[8,64,512]{2,1,0:T(8,128)(2,1)} %bitcast.9), calls=%async_computation | async-start | bytes 1048576 | tf_op jit(solution)/shard_map/all_to_all | solution.py:945
  150.2 14.5 %all-to-all-done.q_ref = bf16[8,64,512]{2,1,0:T(8,128)(2,1)S(1)} async-done(((bf16[8,64,512]{2,1,0:T(8,128)(2,1)}), bf16[8,64,512]{2,1,0:T(8,128)(2,1)S(1)}, u32[]{:S(2)}, u32[]{:S(2)}) %all-to-all-start) | async-done | bytes 524320 | tf_op jit(solution)/shard_map/all_to_all | solution.py:945
  164.7 18.1 %collective-permute-done.16.refs_1_ = bf16[8,128,512]{2,1,0:T(8,128)(2,1)} collective-permute-done((bf16[8,128,512]{2,1,0:T(8,128)(2,1)S(1)}, bf16[8,128,512]{2,1,0:T(8,128)(2,1)}, u32[]{:S(2)}, u32[]{:S(2)}) %collective-permute-start.16) | collective-permute-done | bytes 1048608 | tf_op jit(solution)/shard_map/ppermute | solution.py:700
  182.9 33.1 %attend.1 = (f32[8,64,512]{2,1,0:T(8,128)S(1)}, bf16[8,64,512]{2,1,0:T(8,128)(2,1)}, f32[2,2,2,512]{3,2,1,0:T(2,128)S(1)}) custom-call(s32[4]{0:T(128)S(1)} %xor_multiply_fusion.base_ref, s32[32]{0:T(128)S(1)} %reshape.217.edge_ref, f32[2]{0:T(128)S(1)} %pad_maximum_fusion.29.far_ref, bf16[8,64,512]{2,1,0:T(8,128)(2,1)S(1)} %all-to-all-done.q_ref, ...), custom_call_target="tpu_custom_call" | custom-call | tf_op jit(solution)/shard_map/attend/pallas_call | solution.py:648
  217.6 9.3 %all-to-all-start.2 = ((bf16[8,64,512]{2,1,0:T(8,128)(2,1)}), bf16[8,64,512]{2,1,0:T(8,128)(2,1)}, u32[]{:S(2)}, u32[]{:S(2)}) async-start(bf16[8,64,512]{2,1,0:T(8,128)(2,1)} %get-tuple-element.47), calls=%async_computation.2 | async-start | bytes 1048576 | tf_op jit(solution)/shard_map/all_to_all | solution.py:945
  231.0 2.1 collective-permute-start.23
  234.5 2.4 collective-permute-start.28
  238.2 8.8 %collective-permute-done.27 = bf16[128,1024]{1,0:T(8,128)(2,1)S(1)} collective-permute-done((bf16[128,1024]{1,0:T(8,128)(2,1)S(1)}, bf16[128,1024]{1,0:T(8,128)(2,1)S(1)}, u32[]{:S(2)}, u32[]{:S(2)}) %collective-permute-start.27) | collective-permute-done | bytes 262176 | tf_op jit(solution)/shard_map/ppermute | solution.py:700
  247.7 11.3 %collective-permute-done.28 = bf16[128,1024]{1,0:T(8,128)(2,1)S(1)} collective-permute-done((bf16[128,1024]{1,0:T(8,128)(2,1)S(1)}, bf16[128,1024]{1,0:T(8,128)(2,1)S(1)}, u32[]{:S(2)}, u32[]{:S(2)}) %collective-permute-start.28) | collective-permute-done | bytes 262176 | tf_op jit(solution)/shard_map/ppermute | solution.py:700
  263.6 2.5 whole_in.1
  271.2 11.2 %collective-permute-done.31.arrays_2_ = bf16[512,1024]{1,0:T(8,128)(2,1)S(1)} collective-permute-done((bf16[512,1024]{1,0:T(8,128)(2,1)}, bf16[512,1024]{1,0:T(8,128)(2,1)S(1)}, u32[]{:S(2)}, u32[]{:S(2)}) %collective-permute-start.31) | collective-permute-done | bytes 1048608 | tf_op jit(solution)/shard_map/ppermute | solution.py:700
  291.0 3.9 collective-permute-done.33.arrays_4_
  296.9 2.1 whole_down.1
  299.0 2.4 fusion.18
  301.4 5.5 multiply_convert_fusion
  306.9 2.4 fusion.70
  309.3 2.9 convolution_convert_fusion.arrays_0_
  314.9 4.9 fusion.48
  327.2 8.2 %collective-permute-done.69 = bf16[256,1024]{1,0:T(8,128)(2,1)S(1)} collective-permute-done((bf16[256,1024]{1,0:T(8,128)(2,1)S(1)}, bf16[256,1024]{1,0:T(8,128)(2,1)S(1)}, u32[]{:S(2)}, u32[]{:S(2)}) %collective-permute-start.69) | collective-permute-done | bytes 524320 | tf_op jit(solution)/shard_map/ppermute | solution.py:700
  338.6 11.0 %all-to-all-start.3 = ((bf16[8,64,512]{2,1,0:T(8,128)(2,1)}), bf16[8,64,512]{2,1,0:T(8,128)(2,1)S(1)}, u32[]{:S(2)}, u32[]{:S(2)}) async-start(bf16[8,64,512]{2,1,0:T(8,128)(2,1)} %bitcast.134), calls=%async_computation.3 | async-start | bytes 1048576 | tf_op jit(solution)/shard_map/all_to_all | solution.py:945
  349.7 4.4 convolution_convert_fusion.1.arrays_0_
  362.0 3.9 fusion.49
  366.7 50.3 %attend_back.1 = (bf16[8,64,512]{2,1,0:T(8,128)(2,1)}, bf16[8,128,512]{2,1,0:T(8,128)(2,1)}, bf16[8,128,512]{2,1,0:T(8,128)(2,1)}, f32[2048,512]{1,0:T(8,128)}, f32[8,512]{1,0:T(8,128)}) custom-call(s32[4]{0:T(128)} %copy-done.17, s32[32]{0:T(128)} %copy-done.15, f32[2]{0:T(128)} %copy-done.16, bf16[8,64,512]{2,1,0:T(8,128)(2,1)} %copy-done.2, ...), custom_call_target="tpu_custom_call" | custom-call | tf_op jit(solution)/shard_map/attend_back/pallas_call | solution.py:674
  418.3 7.7 %collective-permute-start.73 = (bf16[128,1024]{1,0:T(8,128)(2,1)}, bf16[128,1024]{1,0:T(8,128)(2,1)S(1)}, u32[]{:S(2)}, u32[]{:S(2)}) collective-permute-start(bf16[128,1024]{1,0:T(8,128)(2,1)} %get-tuple-element.165), channel_id=1, source_target_pairs={{0,8},{4,12},{8,0},{12,4},{16,24},{20,28},{24,16},{28,20},{1,9},{5... | collective-permute-start | bytes 786440 | tf_op jit(solution)/shard_map/ppermute | solution.py:700
  426.0 3.2 collective-permute-start.75
  433.4 5.4 all-to-all-start.5
  438.8 2.1 collective-permute-start.57
  442.2 15.4 %collective-permute-done.74 = bf16[128,1024]{1,0:T(8,128)(2,1)} collective-permute-done((bf16[128,1024]{1,0:T(8,128)(2,1)}, bf16[128,1024]{1,0:T(8,128)(2,1)}, u32[]{:S(2)}, u32[]{:S(2)}) %collective-permute-start.74) | collective-permute-done | bytes 262176 | tf_op jit(solution)/shard_map/ppermute | solution.py:700
  464.0 2.5 add_convert_fusion
  466.5 4.4 all-to-all-start.4
  472.2 2.2 copy-done.3
  474.4 2.5 band_sums.1
  485.8 2.1 convolution_convert_fusion.5.arrays_0_
  487.9 3.1 fusion.71
  491.0 6.4 %all-to-all-done.4 = bf16[8,128,512]{2,1,0:T(8,128)(2,1)} async-done(((bf16[8,128,512]{2,1,0:T(8,128)(2,1)}), bf16[8,128,512]{2,1,0:T(8,128)(2,1)}, u32[]{:S(2)}, u32[]{:S(2)}) %all-to-all-start.4) | async-done | bytes 1048608 | tf_op jit(solution)/shard_map/all_to_all | solution.py:945
  497.5 2.8 convolution_convert_fusion.2.arrays_0_
  502.1 14.2 %collective-permute-done.58 = bf16[640,1024]{1,0:T(8,128)(2,1)S(1)} collective-permute-done((bf16[640,1024]{1,0:T(8,128)(2,1)}, bf16[640,1024]{1,0:T(8,128)(2,1)S(1)}, u32[]{:S(2)}, u32[]{:S(2)}) %collective-permute-start.58) | collective-permute-done | bytes 1310752 | tf_op jit(solution)/shard_map/ppermute | solution.py:700
  516.3 2.2 fusion.50
  520.5 2.4 collective-permute-start.63
  525.3 7.0 %collective-permute-done.49 = bf16[128,1024]{1,0:T(8,128)(2,1)S(1)} collective-permute-done((bf16[128,1024]{1,0:T(8,128)(2,1)S(1)}, bf16[128,1024]{1,0:T(8,128)(2,1)S(1)}, u32[]{:S(2)}, u32[]{:S(2)}) %collective-permute-start.49) | collective-permute-done | bytes 262176 | tf_op jit(solution)/shard_map/ppermute | solution.py:700
  532.9 5.8 collective-permute-done.63
  538.7 10.6 %collective-permute-done.62 = bf16[160,1024]{1,0:T(8,128)(2,1)S(1)} collective-permute-done((bf16[160,1024]{1,0:T(8,128)(2,1)S(1)}, bf16[160,1024]{1,0:T(8,128)(2,1)S(1)}, u32[]{:S(2)}, u32[]{:S(2)}) %collective-permute-start.62) | collective-permute-done | bytes 327712 | tf_op jit(solution)/shard_map/ppermute | solution.py:700
  552.8 2.7 collective-permute-start.55
  556.2 2.6 convolution_add_fusion
  561.3 7.0 %collective-permute-done.54 = bf16[64,1024]{1,0:T(8,128)(2,1)S(1)} collective-permute-done((bf16[64,1024]{1,0:T(8,128)(2,1)S(1)}, bf16[64,1024]{1,0:T(8,128)(2,1)S(1)}, u32[]{:S(2)}, u32[]{:S(2)}) %collective-permute-start.54) | collective-permute-done | bytes 131104 | tf_op jit(solution)/shard_map/ppermute | solution.py:700
  570.4 2.3 reshape.240
  573.8 2.2 fusion.17
  579.1 5.9 collective-permute-done.42
  587.3 7.6 %collective-permute-done.43 = bf16[192,1024]{1,0:T(8,128)(2,1)S(1)} collective-permute-done((bf16[192,1024]{1,0:T(8,128)(2,1)S(1)}, bf16[192,1024]{1,0:T(8,128)(2,1)S(1)}, u32[]{:S(2)}, u32[]{:S(2)}) %collective-permute-start.43) | collective-permute-done | bytes 393248 | tf_op jit(solution)/shard_map/ppermute | solution.py:700
  595.8 2.6 collective-permute-start.46
  602.7 3.0 collective-permute-done.45
  (431 shorter events, 151.9 us)
Async XLA Ops:
  11.2 10.3 %collective-permute-start.1 = (bf16[80,1024]{1,0:T(8,128)(2,1)S(1)}, bf16[80,1024]{1,0:T(8,128)(2,1)S(1)}, u32[]{:S(2)}, u32[]{:S(2)}) collective-permute-start(bf16[80,1024]{1,0:T(8,128)(2,1)S(1)} %pad_maximum_fusion.21), channel_id=1, source_target_pairs={{0,8},{4,12},{8,0},{12,4},{16,24},{20,28},{24,16},{28,20},{1,9},{5... | collective-permute-start | bytes 491528 | tf_op jit(solution)/shard_map/ppermute | solution.py:700
  14.2 15.0 %collective-permute-start.2 = (bf16[80,1024]{1,0:T(8,128)(2,1)S(1)}, bf16[80,1024]{1,0:T(8,128)(2,1)S(1)}, u32[]{:S(2)}, u32[]{:S(2)}) collective-permute-start(bf16[80,1024]{1,0:T(8,128)(2,1)S(1)} %pad_maximum_fusion.21), channel_id=1, source_target_pairs={{0,16},{4,20},{8,24},{12,28},{16,0},{20,4},{24,8},{28,12},{1,17},{... | collective-permute-start | bytes 491528 | tf_op jit(solution)/shard_map/ppermute | solution.py:700
  16.8 12.4 %collective-permute-start.3 = (bf16[80,1024]{1,0:T(8,128)(2,1)S(1)}, bf16[80,1024]{1,0:T(8,128)(2,1)S(1)}, u32[]{:S(2)}, u32[]{:S(2)}) collective-permute-start(bf16[80,1024]{1,0:T(8,128)(2,1)S(1)} %pad_maximum_fusion.21), channel_id=1, source_target_pairs={{0,24},{4,28},{8,16},{12,20},{16,8},{20,12},{24,0},{28,4},{1,25},{... | collective-permute-start | bytes 491528 | tf_op jit(solution)/shard_map/ppermute | solution.py:700
  29.3 14.7 %collective-permute-start.5 = (bf16[320,1024]{1,0:T(8,128)(2,1)S(1)}, bf16[320,1024]{1,0:T(8,128)(2,1)S(1)}, u32[]{:S(2)}, u32[]{:S(2)}) collective-permute-start(bf16[320,1024]{1,0:T(8,128)(2,1)S(1)} %constant_dynamic-update-slice_fusion.8.arrays_0_), channel_id=1, source_target_pairs={{0,4},{4,0},{8,12},{12,8},{16,20},{20,16},{24,28},{28,24},{1,5},{5... | collective-permute-start | bytes 1966088 | tf_op jit(solution)/shard_map/ppermute | solution.py:700
  30.8 15.8 %collective-permute-start.4 = (bf16[320,1024]{1,0:T(8,128)(2,1)S(1)}, bf16[320,1024]{1,0:T(8,128)(2,1)S(1)}, u32[]{:S(2)}, u32[]{:S(2)}) collective-permute-start(bf16[320,1024]{1,0:T(8,128)(2,1)S(1)} %constant_dynamic-update-slice_fusion.8.arrays_0_), channel_id=1, source_target_pairs={{0,2},{1,3},{2,0},{3,1},{4,6},{5,7},{6,4},{7,5},{8,10},{9,11},{10,... | collective-permute-start | bytes 1966088 | tf_op jit(solution)/shard_map/ppermute | solution.py:700
  44.0 8.2 %collective-permute-start.7 = (bf16[160,1024]{1,0:T(8,128)(2,1)S(1)}, bf16[160,1024]{1,0:T(8,128)(2,1)S(1)}, u32[]{:S(2)}, u32[]{:S(2)}) collective-permute-start(bf16[160,1024]{1,0:T(8,128)(2,1)S(1)} %slice.430), channel_id=1, source_target_pairs={{0,2},{1,3},{2,0},{3,1},{4,6},{5,7},{6,4},{7,5},{8,10},{9,11},{10,... | collective-permute-start | bytes 983048 | tf_op jit(solution)/shard_map/ppermute | solution.py:700
  56.3 17.6 %collective-permute-start.17 = (bf16[32,1024]{1,0:T(8,128)(2,1)}, bf16[32,1024]{1,0:T(8,128)(2,1)S(1)}, u32[]{:S(2)}, u32[]{:S(2)}) collective-permute-start(bf16[32,1024]{1,0:T(8,128)(2,1)} %param.22), channel_id=1, source_target_pairs={{0,0},{1,2},{2,1},{3,3},{4,4},{5,6},{6,5},{7,7},{8,8},{9,10},{10,9... | collective-permute-start | bytes 196616 | tf_op jit(solution)/shard_map/ppermute | solution.py:900
  62.6 71.1 %all-to-all-start.1 = ((bf16[8,128,512]{2,1,0:T(8,128)(2,1)}), bf16[8,128,512]{2,1,0:T(8,128)(2,1)S(1)}, u32[]{:S(2)}, u32[]{:S(2)}) async-start(bf16[8,128,512]{2,1,0:T(8,128)(2,1)} %bitcast.10), calls=%async_computation.1 | async-start | bytes 2097152 | tf_op jit(solution)/shard_map/all_to_all | solution.py:945
  69.4 24.1 %collective-permute-start.10 = (bf16[32,1024]{1,0:T(8,128)(2,1)S(1)}, bf16[32,1024]{1,0:T(8,128)(2,1)S(1)}, u32[]{:S(2)}, u32[]{:S(2)}) collective-permute-start(bf16[32,1024]{1,0:T(8,128)(2,1)S(1)} %pad_maximum_fusion.27), channel_id=1, source_target_pairs={{0,24},{4,28},{8,16},{12,20},{16,8},{20,12},{24,0},{28,4},{1,25},{... | collective-permute-start | bytes 196616 | tf_op jit(solution)/shard_map/ppermute | solution.py:700
  73.3 28.9 %collective-permute-start.9 = (bf16[32,1024]{1,0:T(8,128)(2,1)S(1)}, bf16[32,1024]{1,0:T(8,128)(2,1)S(1)}, u32[]{:S(2)}, u32[]{:S(2)}) collective-permute-start(bf16[32,1024]{1,0:T(8,128)(2,1)S(1)} %pad_maximum_fusion.27), channel_id=1, source_target_pairs={{0,16},{4,20},{8,24},{12,28},{16,0},{20,4},{24,8},{28,12},{1,17},{... | collective-permute-start | bytes 196616 | tf_op jit(solution)/shard_map/ppermute | solution.py:700
  73.3 28.9 %collective-permute-start.8 = (bf16[32,1024]{1,0:T(8,128)(2,1)S(1)}, bf16[32,1024]{1,0:T(8,128)(2,1)S(1)}, u32[]{:S(2)}, u32[]{:S(2)}) collective-permute-start(bf16[32,1024]{1,0:T(8,128)(2,1)S(1)} %pad_maximum_fusion.27), channel_id=1, source_target_pairs={{0,8},{4,12},{8,0},{12,4},{16,24},{20,28},{24,16},{28,20},{1,9},{5... | collective-permute-start | bytes 196616 | tf_op jit(solution)/shard_map/ppermute | solution.py:700
  73.9 38.3 %collective-permute-start.18 = (bf16[160,1024]{1,0:T(8,128)(2,1)S(1)}, bf16[160,1024]{1,0:T(8,128)(2,1)S(1)}, u32[]{:S(2)}, u32[]{:S(2)}) collective-permute-start(bf16[160,1024]{1,0:T(8,128)(2,1)S(1)} %pad_maximum_fusion.18), channel_id=1, source_target_pairs={{0,8},{4,12},{8,0},{12,4},{16,24},{20,28},{24,16},{28,20},{1,9},{5... | collective-permute-start | bytes 983048 | tf_op jit(solution)/shard_map/ppermute | solution.py:700
  103.4 23.4 %collective-permute-start.19 = (bf16[160,1024]{1,0:T(8,128)(2,1)S(1)}, bf16[160,1024]{1,0:T(8,128)(2,1)S(1)}, u32[]{:S(2)}, u32[]{:S(2)}) collective-permute-start(bf16[160,1024]{1,0:T(8,128)(2,1)S(1)} %pad_maximum_fusion.18), channel_id=1, source_target_pairs={{0,16},{4,20},{8,24},{12,28},{16,0},{20,4},{24,8},{28,12},{1,17},{... | collective-permute-start | bytes 983048 | tf_op jit(solution)/shard_map/ppermute | solution.py:700
  103.5 24.0 %collective-permute-start.20 = (bf16[160,1024]{1,0:T(8,128)(2,1)S(1)}, bf16[160,1024]{1,0:T(8,128)(2,1)S(1)}, u32[]{:S(2)}, u32[]{:S(2)}) collective-permute-start(bf16[160,1024]{1,0:T(8,128)(2,1)S(1)} %pad_maximum_fusion.18), channel_id=1, source_target_pairs={{0,24},{4,28},{8,16},{12,20},{16,8},{20,12},{24,0},{28,4},{1,25},{... | collective-permute-start | bytes 983048 | tf_op jit(solution)/shard_map/ppermute | solution.py:700
  110.4 21.1 %collective-permute-start.14 = (bf16[64,1024]{1,0:T(8,128)(2,1)S(1)}, bf16[64,1024]{1,0:T(8,128)(2,1)S(1)}, u32[]{:S(2)}, u32[]{:S(2)}) collective-permute-start(bf16[64,1024]{1,0:T(8,128)(2,1)S(1)} %slice.436), channel_id=1, source_target_pairs={{0,2},{1,3},{2,0},{3,1},{4,6},{5,7},{6,4},{7,5},{8,10},{9,11},{10,... | collective-permute-start | bytes 393224 | tf_op jit(solution)/shard_map/ppermute | solution.py:700
  111.3 20.1 %collective-permute-start.13 = (bf16[64,1024]{1,0:T(8,128)(2,1)S(1)}, bf16[64,1024]{1,0:T(8,128)(2,1)S(1)}, u32[]{:S(2)}, u32[]{:S(2)}) collective-permute-start(bf16[64,1024]{1,0:T(8,128)(2,1)S(1)} %slice.435), channel_id=1, source_target_pairs={{0,4},{4,0},{8,12},{12,8},{16,20},{20,16},{24,28},{28,24},{1,5},{5... | collective-permute-start | bytes 393224 | tf_op jit(solution)/shard_map/ppermute | solution.py:700
  128.3 98.6 %collective-permute-start.22 = (bf16[640,1024]{1,0:T(8,128)(2,1)}, bf16[640,1024]{1,0:T(8,128)(2,1)}, u32[]{:S(2)}, u32[]{:S(2)}) collective-permute-start(bf16[640,1024]{1,0:T(8,128)(2,1)} %constant_dynamic-update-slice_fusion.13.arrays_0_), channel_id=1, source_target_pairs={{0,4},{4,0},{8,12},{12,8},{16,20},{20,16},{24,28},{28,24},{1,5},{5... | collective-permute-start | bytes 3932168 | tf_op jit(solution)/shard_map/ppermute | solution.py:700
  129.7 100.1 %collective-permute-start.21 = (bf16[640,1024]{1,0:T(8,128)(2,1)}, bf16[640,1024]{1,0:T(8,128)(2,1)}, u32[]{:S(2)}, u32[]{:S(2)}) collective-permute-start(bf16[640,1024]{1,0:T(8,128)(2,1)} %constant_dynamic-update-slice_fusion.13.arrays_0_), channel_id=1, source_target_pairs={{0,2},{1,3},{2,0},{3,1},{4,6},{5,7},{6,4},{7,5},{8,10},{9,11},{10,... | collective-permute-start | bytes 3932168 | tf_op jit(solution)/shard_map/ppermute | solution.py:700
  133.7 31.0 %all-to-all-start = ((bf16[8,64,512]{2,1,0:T(8,128)(2,1)}), bf16[8,64,512]{2,1,0:T(8,128)(2,1)S(1)}, u32[]{:S(2)}, u32[]{:S(2)}) async-start(bf16[8,64,512]{2,1,0:T(8,128)(2,1)} %bitcast.9), calls=%async_computation | async-start | bytes 1048576 | tf_op jit(solution)/shard_map/all_to_all | solution.py:945
  142.8 40.1 %collective-permute-start.16 = (bf16[8,128,512]{2,1,0:T(8,128)(2,1)S(1)}, bf16[8,128,512]{2,1,0:T(8,128)(2,1)}, u32[]{:S(2)}, u32[]{:S(2)}) collective-permute-start(bf16[8,128,512]{2,1,0:T(8,128)(2,1)S(1)} %all-to-all-done.1.refs_0_), channel_id=1, source_target_pairs={{0,2},{1,3},{2,0},{3,1},{4,6},{5,7},{6,4},{7,5},{8,10},{9,11},{10,... | collective-permute-start | bytes 3145736 | tf_op jit(solution)/shard_map/ppermute | solution.py:700
  217.6 50.5 %all-to-all-start.2 = ((bf16[8,64,512]{2,1,0:T(8,128)(2,1)}), bf16[8,64,512]{2,1,0:T(8,128)(2,1)}, u32[]{:S(2)}, u32[]{:S(2)}) async-start(bf16[8,64,512]{2,1,0:T(8,128)(2,1)} %get-tuple-element.47), calls=%async_computation.2 | async-start | bytes 1048576 | tf_op jit(solution)/shard_map/all_to_all | solution.py:945
  228.0 35.6 %collective-permute-start.24 = (bf16[320,1024]{1,0:T(8,128)(2,1)S(1)}, bf16[320,1024]{1,0:T(8,128)(2,1)S(1)}, u32[]{:S(2)}, u32[]{:S(2)}) collective-permute-start(bf16[320,1024]{1,0:T(8,128)(2,1)S(1)} %slice.439), channel_id=1, source_target_pairs={{0,2},{1,3},{2,0},{3,1},{4,6},{5,7},{6,4},{7,5},{8,10},{9,11},{10,... | collective-permute-start | bytes 1966088 | tf_op jit(solution)/shard_map/ppermute | solution.py:700
  231.0 32.6 %collective-permute-start.23 = (bf16[320,1024]{1,0:T(8,128)(2,1)S(1)}, bf16[320,1024]{1,0:T(8,128)(2,1)S(1)}, u32[]{:S(2)}, u32[]{:S(2)}) collective-permute-start(bf16[320,1024]{1,0:T(8,128)(2,1)S(1)} %slice.438), channel_id=1, source_target_pairs={{0,4},{4,0},{8,12},{12,8},{16,20},{20,16},{24,28},{28,24},{1,5},{5... | collective-permute-start | bytes 1966088 | tf_op jit(solution)/shard_map/ppermute | solution.py:700
  233.1 13.9 %collective-permute-start.27 = (bf16[128,1024]{1,0:T(8,128)(2,1)S(1)}, bf16[128,1024]{1,0:T(8,128)(2,1)S(1)}, u32[]{:S(2)}, u32[]{:S(2)}) collective-permute-start(bf16[128,1024]{1,0:T(8,128)(2,1)S(1)} %copy-done.40), channel_id=1, source_target_pairs={{0,8},{4,12},{8,0},{12,4},{16,24},{20,28},{24,16},{28,20},{1,9},{5... | collective-permute-start | bytes 786440 | tf_op jit(solution)/shard_map/ppermute | solution.py:700
  234.5 24.5 %collective-permute-start.28 = (bf16[128,1024]{1,0:T(8,128)(2,1)S(1)}, bf16[128,1024]{1,0:T(8,128)(2,1)S(1)}, u32[]{:S(2)}, u32[]{:S(2)}) collective-permute-start(bf16[128,1024]{1,0:T(8,128)(2,1)S(1)} %copy-done.40), channel_id=1, source_target_pairs={{0,16},{4,20},{8,24},{12,28},{16,0},{20,4},{24,8},{28,12},{1,17},{... | collective-permute-start | bytes 786440 | tf_op jit(solution)/shard_map/ppermute | solution.py:700
  236.9 22.8 %collective-permute-start.29 = (bf16[128,1024]{1,0:T(8,128)(2,1)S(1)}, bf16[128,1024]{1,0:T(8,128)(2,1)S(1)}, u32[]{:S(2)}, u32[]{:S(2)}) collective-permute-start(bf16[128,1024]{1,0:T(8,128)(2,1)S(1)} %copy-done.40), channel_id=1, source_target_pairs={{0,24},{4,28},{8,16},{12,20},{16,8},{20,12},{24,0},{28,4},{1,25},{... | collective-permute-start | bytes 786440 | tf_op jit(solution)/shard_map/ppermute | solution.py:700
  260.5 21.9 %collective-permute-start.31 = (bf16[512,1024]{1,0:T(8,128)(2,1)}, bf16[512,1024]{1,0:T(8,128)(2,1)S(1)}, u32[]{:S(2)}, u32[]{:S(2)}) collective-permute-start(bf16[512,1024]{1,0:T(8,128)(2,1)} %constant_dynamic-update-slice_fusion.19.arrays_0_), channel_id=1, source_target_pairs={{0,4},{4,0},{8,12},{12,8},{16,20},{20,16},{24,28},{28,24},{1,5},{5... | collective-permute-start | bytes 3145736 | tf_op jit(solution)/shard_map/ppermute | solution.py:700
  261.9 23.6 %collective-permute-start.30 = (bf16[512,1024]{1,0:T(8,128)(2,1)}, bf16[512,1024]{1,0:T(8,128)(2,1)}, u32[]{:S(2)}, u32[]{:S(2)}) collective-permute-start(bf16[512,1024]{1,0:T(8,128)(2,1)} %constant_dynamic-update-slice_fusion.19.arrays_0_), channel_id=1, source_target_pairs={{0,2},{1,3},{2,0},{3,1},{4,6},{5,7},{6,4},{7,5},{8,10},{9,11},{10,... | collective-permute-start | bytes 3145736 | tf_op jit(solution)/shard_map/ppermute | solution.py:700
  271.2 17.1 %collective-permute-start.25 = (f32[256,1024]{1,0:T(8,128)}, f32[256,1024]{1,0:T(8,128)}, u32[]{:S(2)}, u32[]{:S(2)}) collective-permute-start(f32[256,1024]{1,0:T(8,128)} %slice.441), channel_id=1, source_target_pairs={{0,1},{1,0},{2,3},{3,2},{4,5},{5,4},{6,7},{7,6},{8,9},{9,8},{10,11... | collective-permute-start | bytes 3145736 | tf_op jit(solution)/shard_map/ppermute | solution.py:700
  283.1 11.8 %collective-permute-start.33 = (bf16[256,1024]{1,0:T(8,128)(2,1)}, bf16[256,1024]{1,0:T(8,128)(2,1)}, u32[]{:S(2)}, u32[]{:S(2)}) collective-permute-start(bf16[256,1024]{1,0:T(8,128)(2,1)} %slice.444), channel_id=1, source_target_pairs={{0,2},{1,3},{2,0},{3,1},{4,6},{5,7},{6,4},{7,5},{8,10},{9,11},{10,... | collective-permute-start | bytes 1572872 | tf_op jit(solution)/shard_map/ppermute | solution.py:700
  287.4 9.5 %collective-permute-start.32 = (bf16[256,1024]{1,0:T(8,128)(2,1)}, bf16[256,1024]{1,0:T(8,128)(2,1)}, u32[]{:S(2)}, u32[]{:S(2)}) collective-permute-start(bf16[256,1024]{1,0:T(8,128)(2,1)} %slice.443), channel_id=1, source_target_pairs={{0,4},{4,0},{8,12},{12,8},{16,20},{20,16},{24,28},{28,24},{1,5},{5... | collective-permute-start | bytes 1572872 | tf_op jit(solution)/shard_map/ppermute | solution.py:700
  290.4 8.6 %collective-permute-start.26 = (bf16[256,1024]{1,0:T(8,128)(2,1)S(1)}, bf16[256,1024]{1,0:T(8,128)(2,1)S(1)}, u32[]{:S(2)}, u32[]{:S(2)}) collective-permute-start(bf16[256,1024]{1,0:T(8,128)(2,1)S(1)} %multiply_convert_fusion.2), channel_id=1, source_target_pairs={{0,1},{1,0},{2,3},{3,2},{4,5},{5,4},{6,7},{7,6},{8,9},{9,8},{10,11... | collective-permute-start | bytes 1572872 | tf_op jit(solution)/shard_map/ppermute | solution.py:700
  290.5 10.9 %collective-permute-start.35 = (bf16[256,1024]{1,0:T(8,128)(2,1)S(1)}, bf16[256,1024]{1,0:T(8,128)(2,1)S(1)}, u32[]{:S(2)}, u32[]{:S(2)}) collective-permute-start(bf16[256,1024]{1,0:T(8,128)(2,1)S(1)} %bitcast.129), channel_id=1, source_target_pairs={{0,1},{1,0},{2,3},{3,2},{4,5},{5,4},{6,7},{7,6},{8,9},{9,8},{10,11... | collective-permute-start | bytes 1572872 | tf_op jit(solution)/shard_map/ppermute | solution.py:700
  313.1 9.2 %collective-permute-start.71 = (bf16[256,1024]{1,0:T(8,128)(2,1)S(1)}, bf16[256,1024]{1,0:T(8,128)(2,1)S(1)}, u32[]{:S(2)}, u32[]{:S(2)}) collective-permute-start(bf16[256,1024]{1,0:T(8,128)(2,1)S(1)} %get-tuple-element.78), channel_id=1, source_target_pairs={{0,2},{1,3},{2,0},{3,1},{4,6},{5,7},{6,4},{7,5},{8,10},{9,11},{10,... | collective-permute-start | bytes 1572872 | tf_op jit(solution)/shard_map/ppermute | solution.py:700
  320.6 14.9 %collective-permute-start.69 = (bf16[256,1024]{1,0:T(8,128)(2,1)S(1)}, bf16[256,1024]{1,0:T(8,128)(2,1)S(1)}, u32[]{:S(2)}, u32[]{:S(2)}) collective-permute-start(bf16[256,1024]{1,0:T(8,128)(2,1)S(1)} %get-tuple-element.76), channel_id=1, source_target_pairs={{0,4},{4,0},{8,12},{12,8},{16,20},{20,16},{24,28},{28,24},{1,5},{5... | collective-permute-start | bytes 1572872 | tf_op jit(solution)/shard_map/ppermute | solution.py:700
  325.1 12.0 %collective-permute-start.37 = (bf16[256,1024]{1,0:T(8,128)(2,1)S(1)}, bf16[256,1024]{1,0:T(8,128)(2,1)S(1)}, u32[]{:S(2)}, u32[]{:S(2)}) collective-permute-start(bf16[256,1024]{1,0:T(8,128)(2,1)S(1)} %get-tuple-element.152), channel_id=1, source_target_pairs={{0,1},{1,0},{2,3},{3,2},{4,5},{5,4},{6,7},{7,6},{8,9},{9,8},{10,11... | collective-permute-start | bytes 1572872 | tf_op jit(solution)/shard_map/ppermute | solution.py:700
  326.2 35.7 %collective-permute-start.72 = (bf16[512,1024]{1,0:T(8,128)(2,1)}, bf16[512,1024]{1,0:T(8,128)(2,1)}, u32[]{:S(2)}, u32[]{:S(2)}) collective-permute-start(bf16[512,1024]{1,0:T(8,128)(2,1)} %pad_maximum_fusion.7), channel_id=1, source_target_pairs={{0,4},{4,0},{8,12},{12,8},{16,20},{20,16},{24,28},{28,24},{1,5},{5... | collective-permute-start | bytes 3145736 | tf_op jit(solution)/shard_map/ppermute | solution.py:700
  336.7 25.3 %collective-permute-start.70 = (bf16[512,1024]{1,0:T(8,128)(2,1)}, bf16[512,1024]{1,0:T(8,128)(2,1)}, u32[]{:S(2)}, u32[]{:S(2)}) collective-permute-start(bf16[512,1024]{1,0:T(8,128)(2,1)} %pad_maximum_fusion.6), channel_id=1, source_target_pairs={{0,2},{1,3},{2,0},{3,1},{4,6},{5,7},{6,4},{7,5},{8,10},{9,11},{10,... | collective-permute-start | bytes 3145736 | tf_op jit(solution)/shard_map/ppermute | solution.py:700
  338.6 27.2 %all-to-all-start.3 = ((bf16[8,64,512]{2,1,0:T(8,128)(2,1)}), bf16[8,64,512]{2,1,0:T(8,128)(2,1)S(1)}, u32[]{:S(2)}, u32[]{:S(2)}) async-start(bf16[8,64,512]{2,1,0:T(8,128)(2,1)} %bitcast.134), calls=%async_computation.3 | async-start | bytes 1048576 | tf_op jit(solution)/shard_map/all_to_all | solution.py:945
  359.8 99.9 %collective-permute-start.59 = (bf16[320,1024]{1,0:T(8,128)(2,1)}, bf16[320,1024]{1,0:T(8,128)(2,1)}, u32[]{:S(2)}, u32[]{:S(2)}) collective-permute-start(bf16[320,1024]{1,0:T(8,128)(2,1)} %get-tuple-element.69), channel_id=1, source_target_pairs={{0,2},{1,3},{2,0},{3,1},{4,6},{5,7},{6,4},{7,5},{8,10},{9,11},{10,... | collective-permute-start | bytes 1966088 | tf_op jit(solution)/shard_map/ppermute | solution.py:700
  416.9 47.1 %collective-permute-start.38 = (bf16[8,128,512]{2,1,0:T(8,128)(2,1)}, bf16[8,128,512]{2,1,0:T(8,128)(2,1)}, u32[]{:S(2)}, u32[]{:S(2)}) collective-permute-start(bf16[8,128,512]{2,1,0:T(8,128)(2,1)} %get-tuple-element.53), channel_id=1, source_target_pairs={{0,2},{1,3},{2,0},{3,1},{4,6},{5,7},{6,4},{7,5},{8,10},{9,11},{10,... | collective-permute-start | bytes 3145736 | tf_op jit(solution)/shard_map/ppermute | solution.py:700
  418.3 20.4 %collective-permute-start.73 = (bf16[128,1024]{1,0:T(8,128)(2,1)}, bf16[128,1024]{1,0:T(8,128)(2,1)S(1)}, u32[]{:S(2)}, u32[]{:S(2)}) collective-permute-start(bf16[128,1024]{1,0:T(8,128)(2,1)} %get-tuple-element.165), channel_id=1, source_target_pairs={{0,8},{4,12},{8,0},{12,4},{16,24},{20,28},{24,16},{28,20},{1,9},{5... | collective-permute-start | bytes 786440 | tf_op jit(solution)/shard_map/ppermute | solution.py:700
  426.0 16.2 %collective-permute-start.75 = (bf16[128,1024]{1,0:T(8,128)(2,1)}, bf16[128,1024]{1,0:T(8,128)(2,1)S(1)}, u32[]{:S(2)}, u32[]{:S(2)}) collective-permute-start(bf16[128,1024]{1,0:T(8,128)(2,1)} %get-tuple-element.166), channel_id=1, source_target_pairs={{0,24},{4,28},{8,16},{12,20},{16,8},{20,12},{24,0},{28,4},{1,25},{... | collective-permute-start | bytes 786440 | tf_op jit(solution)/shard_map/ppermute | solution.py:700
  429.2 28.4 %collective-permute-start.74 = (bf16[128,1024]{1,0:T(8,128)(2,1)}, bf16[128,1024]{1,0:T(8,128)(2,1)}, u32[]{:S(2)}, u32[]{:S(2)}) collective-permute-start(bf16[128,1024]{1,0:T(8,128)(2,1)} %get-tuple-element.167), channel_id=1, source_target_pairs={{0,16},{4,20},{8,24},{12,28},{16,0},{20,4},{24,8},{28,12},{1,17},{... | collective-permute-start | bytes 786440 | tf_op jit(solution)/shard_map/ppermute | solution.py:700
  433.4 33.1 %all-to-all-start.5 = ((bf16[8,64,512]{2,1,0:T(8,128)(2,1)}), bf16[8,64,512]{2,1,0:T(8,128)(2,1)}, u32[]{:S(2)}, u32[]{:S(2)}) async-start(bf16[8,64,512]{2,1,0:T(8,128)(2,1)} %get-tuple-element.54), calls=%async_computation.5 | async-start | bytes 1048576 | tf_op jit(solution)/shard_map/all_to_all | solution.py:945
  438.8 32.1 %collective-permute-start.57 = (bf16[320,1024]{1,0:T(8,128)(2,1)S(1)}, bf16[320,1024]{1,0:T(8,128)(2,1)}, u32[]{:S(2)}, u32[]{:S(2)}) collective-permute-start(bf16[320,1024]{1,0:T(8,128)(2,1)S(1)} %get-tuple-element.67), channel_id=1, source_target_pairs={{0,4},{4,0},{8,12},{12,8},{16,20},{20,16},{24,28},{28,24},{1,5},{5... | collective-permute-start | bytes 1966088 | tf_op jit(solution)/shard_map/ppermute | solution.py:700
  462.3 39.8 %collective-permute-start.60 = (bf16[640,1024]{1,0:T(8,128)(2,1)}, bf16[640,1024]{1,0:T(8,128)(2,1)}, u32[]{:S(2)}, u32[]{:S(2)}) collective-permute-start(bf16[640,1024]{1,0:T(8,128)(2,1)} %pad_maximum_fusion.1), channel_id=1, source_target_pairs={{0,4},{4,0},{8,12},{12,8},{16,20},{20,16},{24,28},{28,24},{1,5},{5... | collective-permute-start | bytes 3932168 | tf_op jit(solution)/shard_map/ppermute | solution.py:700
  466.5 31.0 %all-to-all-start.4 = ((bf16[8,128,512]{2,1,0:T(8,128)(2,1)}), bf16[8,128,512]{2,1,0:T(8,128)(2,1)}, u32[]{:S(2)}, u32[]{:S(2)}) async-start(bf16[8,128,512]{2,1,0:T(8,128)(2,1)} %add_convert_fusion), calls=%async_computation.4 | async-start | bytes 2097152 | tf_op jit(solution)/shard_map/all_to_all | solution.py:945
  484.4 31.9 %collective-permute-start.58 = (bf16[640,1024]{1,0:T(8,128)(2,1)}, bf16[640,1024]{1,0:T(8,128)(2,1)S(1)}, u32[]{:S(2)}, u32[]{:S(2)}) collective-permute-start(bf16[640,1024]{1,0:T(8,128)(2,1)} %pad_maximum_fusion), channel_id=1, source_target_pairs={{0,2},{1,3},{2,0},{3,1},{4,6},{5,7},{6,4},{7,5},{8,10},{9,11},{10,... | collective-permute-start | bytes 3932168 | tf_op jit(solution)/shard_map/ppermute | solution.py:700
  501.0 23.5 %collective-permute-start.51 = (bf16[128,1024]{1,0:T(8,128)(2,1)S(1)}, bf16[128,1024]{1,0:T(8,128)(2,1)S(1)}, u32[]{:S(2)}, u32[]{:S(2)}) collective-permute-start(bf16[128,1024]{1,0:T(8,128)(2,1)S(1)} %get-tuple-element.64), channel_id=1, source_target_pairs={{0,2},{1,3},{2,0},{3,1},{4,6},{5,7},{6,4},{7,5},{8,10},{9,11},{10,... | collective-permute-start | bytes 786440 | tf_op jit(solution)/shard_map/ppermute | solution.py:700
  518.6 14.3 %collective-permute-start.61 = (bf16[160,1024]{1,0:T(8,128)(2,1)S(1)}, bf16[160,1024]{1,0:T(8,128)(2,1)S(1)}, u32[]{:S(2)}, u32[]{:S(2)}) collective-permute-start(bf16[160,1024]{1,0:T(8,128)(2,1)S(1)} %get-tuple-element.162), channel_id=1, source_target_pairs={{0,8},{4,12},{8,0},{12,4},{16,24},{20,28},{24,16},{28,20},{1,9},{5... | collective-permute-start | bytes 983048 | tf_op jit(solution)/shard_map/ppermute | solution.py:700
  520.5 18.1 %collective-permute-start.63 = (bf16[160,1024]{1,0:T(8,128)(2,1)S(1)}, bf16[160,1024]{1,0:T(8,128)(2,1)S(1)}, u32[]{:S(2)}, u32[]{:S(2)}) collective-permute-start(bf16[160,1024]{1,0:T(8,128)(2,1)S(1)} %get-tuple-element.163), channel_id=1, source_target_pairs={{0,24},{4,28},{8,16},{12,20},{16,8},{20,12},{24,0},{28,4},{1,25},{... | collective-permute-start | bytes 983048 | tf_op jit(solution)/shard_map/ppermute | solution.py:700
  522.9 26.4 %collective-permute-start.62 = (bf16[160,1024]{1,0:T(8,128)(2,1)S(1)}, bf16[160,1024]{1,0:T(8,128)(2,1)S(1)}, u32[]{:S(2)}, u32[]{:S(2)}) collective-permute-start(bf16[160,1024]{1,0:T(8,128)(2,1)S(1)} %get-tuple-element.164), channel_id=1, source_target_pairs={{0,16},{4,20},{8,24},{12,28},{16,0},{20,4},{24,8},{28,12},{1,17},{... | collective-permute-start | bytes 983048 | tf_op jit(solution)/shard_map/ppermute | solution.py:700
  523.0 9.3 %collective-permute-start.49 = (bf16[128,1024]{1,0:T(8,128)(2,1)S(1)}, bf16[128,1024]{1,0:T(8,128)(2,1)S(1)}, u32[]{:S(2)}, u32[]{:S(2)}) collective-permute-start(bf16[128,1024]{1,0:T(8,128)(2,1)S(1)} %get-tuple-element.62), channel_id=1, source_target_pairs={{0,4},{4,0},{8,12},{12,8},{16,20},{20,16},{24,28},{28,24},{1,5},{5... | collective-permute-start | bytes 786440 | tf_op jit(solution)/shard_map/ppermute | solution.py:700
  524.6 27.7 %collective-permute-start.52 = (bf16[256,1024]{1,0:T(8,128)(2,1)S(1)}, bf16[256,1024]{1,0:T(8,128)(2,1)S(1)}, u32[]{:S(2)}, u32[]{:S(2)}) collective-permute-start(bf16[256,1024]{1,0:T(8,128)(2,1)S(1)} %pad_maximum_fusion.15), channel_id=1, source_target_pairs={{0,4},{4,0},{8,12},{12,8},{16,20},{20,16},{24,28},{28,24},{1,5},{5... | collective-permute-start | bytes 1572872 | tf_op jit(solution)/shard_map/ppermute | solution.py:700
  532.4 20.0 %collective-permute-start.50 = (bf16[256,1024]{1,0:T(8,128)(2,1)S(1)}, bf16[256,1024]{1,0:T(8,128)(2,1)S(1)}, u32[]{:S(2)}, u32[]{:S(2)}) collective-permute-start(bf16[256,1024]{1,0:T(8,128)(2,1)S(1)} %pad_maximum_fusion.14), channel_id=1, source_target_pairs={{0,2},{1,3},{2,0},{3,1},{4,6},{5,7},{6,4},{7,5},{8,10},{9,11},{10,... | collective-permute-start | bytes 1572872 | tf_op jit(solution)/shard_map/ppermute | solution.py:700
  550.5 18.5 %collective-permute-start.68 = (f32[32,2048]{1,0:T(8,128)S(1)}, f32[32,2048]{1,0:T(8,128)S(1)}, u32[]{:S(2)}, u32[]{:S(2)}) collective-permute-start(f32[32,2048]{1,0:T(8,128)S(1)} %broadcast_select_fusion.4), channel_id=1, source_target_pairs={{0,1},{1,0},{2,3},{3,2},{4,5},{5,4},{6,7},{7,6},{8,9},{9,8},{10,11... | collective-permute-start | bytes 786440 | tf_op jit(solution)/shard_map/ppermute | solution.py:700
  552.7 8.7 %collective-permute-start.53 = (bf16[64,1024]{1,0:T(8,128)(2,1)S(1)}, bf16[64,1024]{1,0:T(8,128)(2,1)S(1)}, u32[]{:S(2)}, u32[]{:S(2)}) collective-permute-start(bf16[64,1024]{1,0:T(8,128)(2,1)S(1)} %get-tuple-element.175), channel_id=1, source_target_pairs={{0,8},{4,12},{8,0},{12,4},{16,24},{20,28},{24,16},{28,20},{1,9},{5... | collective-permute-start | bytes 393224 | tf_op jit(solution)/shard_map/ppermute | solution.py:700
  552.8 8.6 %collective-permute-start.55 = (bf16[64,1024]{1,0:T(8,128)(2,1)S(1)}, bf16[64,1024]{1,0:T(8,128)(2,1)S(1)}, u32[]{:S(2)}, u32[]{:S(2)}) collective-permute-start(bf16[64,1024]{1,0:T(8,128)(2,1)S(1)} %get-tuple-element.176), channel_id=1, source_target_pairs={{0,24},{4,28},{8,16},{12,20},{16,8},{20,12},{24,0},{28,4},{1,25},{... | collective-permute-start | bytes 393224 | tf_op jit(solution)/shard_map/ppermute | solution.py:700
  555.5 12.9 %collective-permute-start.54 = (bf16[64,1024]{1,0:T(8,128)(2,1)S(1)}, bf16[64,1024]{1,0:T(8,128)(2,1)S(1)}, u32[]{:S(2)}, u32[]{:S(2)}) collective-permute-start(bf16[64,1024]{1,0:T(8,128)(2,1)S(1)} %get-tuple-element.177), channel_id=1, source_target_pairs={{0,16},{4,20},{8,24},{12,28},{16,0},{20,4},{24,8},{28,12},{1,17},{... | collective-permute-start | bytes 393224 | tf_op jit(solution)/shard_map/ppermute | solution.py:700
  560.0 13.9 %collective-permute-start.39 = (f32[256,1024]{1,0:T(8,128)}, f32[256,1024]{1,0:T(8,128)S(1)}, u32[]{:S(2)}, u32[]{:S(2)}) collective-permute-start(f32[256,1024]{1,0:T(8,128)} %slice.450), channel_id=1, source_target_pairs={{0,1},{1,0},{2,3},{3,2},{4,5},{5,4},{6,7},{7,6},{8,9},{9,8},{10,11... | collective-permute-start | bytes 3145736 | tf_op jit(solution)/shard_map/ppermute | solution.py:700
  576.9 8.8 %collective-permute-start.40 = (bf16[96,1024]{1,0:T(8,128)(2,1)S(1)}, bf16[96,1024]{1,0:T(8,128)(2,1)S(1)}, u32[]{:S(2)}, u32[]{:S(2)}) collective-permute-start(bf16[96,1024]{1,0:T(8,128)(2,1)S(1)} %get-tuple-element.57), channel_id=1, source_target_pairs={{0,4},{4,0},{8,12},{12,8},{16,20},{20,16},{24,28},{28,24},{1,5},{5... | collective-permute-start | bytes 589832 | tf_op jit(solution)/shard_map/ppermute | solution.py:700
  585.0 9.9 %collective-permute-start.43 = (bf16[192,1024]{1,0:T(8,128)(2,1)S(1)}, bf16[192,1024]{1,0:T(8,128)(2,1)S(1)}, u32[]{:S(2)}, u32[]{:S(2)}) collective-permute-start(bf16[192,1024]{1,0:T(8,128)(2,1)S(1)} %pad_maximum_fusion.17), channel_id=1, source_target_pairs={{0,4},{4,0},{8,12},{12,8},{16,20},{20,16},{24,28},{28,24},{1,5},{5... | collective-permute-start | bytes 1179656 | tf_op jit(solution)/shard_map/ppermute | solution.py:700
  585.8 9.7 %collective-permute-start.41 = (bf16[192,1024]{1,0:T(8,128)(2,1)S(1)}, bf16[192,1024]{1,0:T(8,128)(2,1)S(1)}, u32[]{:S(2)}, u32[]{:S(2)}) collective-permute-start(bf16[192,1024]{1,0:T(8,128)(2,1)S(1)} %pad_maximum_fusion.16), channel_id=1, source_target_pairs={{0,2},{1,3},{2,0},{3,1},{4,6},{5,7},{6,4},{7,5},{8,10},{9,11},{10,... | collective-permute-start | bytes 1179656 | tf_op jit(solution)/shard_map/ppermute | solution.py:700
  (76 other events, 955.5 us)

commit v2 on v1

--- a/solution.py
+++ b/solution.py
@@ -382,8 +382,8 @@
                 yield seq, near, source, slice((near * seq_count + seq) * part_len, (near * seq_count + seq + 1) * part_len)
 
 
-def lanes_of(ref, lead, tile_at, per_tile, part_len, lane_base):
-    parts = [ref[lead + (tile_at * per_tile + k, slice(None), pl.ds(lane_base, part_len))] for k in range(per_tile)]
+def lanes_of(ref, tile_at, per_tile, part_len, lane_base):
+    parts = [ref[tile_at * per_tile + k, :HD, pl.ds(lane_base, part_len)] for k in range(per_tile)]
     return parts[0] if per_tile == 1 else jnp.concatenate(parts, axis=1)
 
 
@@ -402,8 +402,8 @@
     return jnp.where((places >= start_row) & (places < end_row), scores + bias, FLOOR)
 
 
-def attend_kernel(chips, base_ref, edge_ref, far_ref, q_ref, *refs):
-    kv_refs = refs[:chips]
+def attend_kernel(chips, base_ref, edge_ref, far_ref, *refs):
+    kv_refs, q_ref = refs[:chips], refs[0]
     start_ref, end_ref, bias_ref, o_ref, ob_ref, lse_ref, k_rows, v_aug, top_ref, acc_ref = refs[chips:]
     groups, _, span = q_ref.shape
     blocks, seq_count, span_len, _ = k_rows.shape
@@ -414,9 +414,9 @@
     for far in range(chips):
         for seq, near, source, lanes in pieces_of(seq_count, part_len, groups):
             block = 2 * far + near
-            k_rows[block, seq, source * part_len : (source + 1) * part_len, :] = flipped(kv_refs[far][source, :HD, lanes])
+            k_rows[block, seq, source * part_len : (source + 1) * part_len, :] = flipped(kv_refs[far][source, HD : 2 * HD, lanes])
             at = source % per_key * part_len
-            v_aug[block, seq, source // per_key, :HD, at : at + part_len] = kv_refs[far][source, HD:, lanes]
+            v_aug[block, seq, source // per_key, :HD, at : at + part_len] = kv_refs[far][source, 2 * HD :, lanes]
     for block in range(blocks):
         for seq in range(seq_count):
             for tile in range(key_tiles):
@@ -429,7 +429,7 @@
             def query_tile(tile, _, seq=seq, near=near, lane_base=lane_base):
                 query_at = base_ref[near] + tile * TQ
                 row = (near * seq_count + seq) * tiles + tile
-                queries = lanes_of(q_ref, (), tile, per_tile, part_len, lane_base)
+                queries = lanes_of(q_ref, tile, per_tile, part_len, lane_base)
                 top_ref[...] = jnp.full_like(top_ref, FLOOR)
                 acc_ref[...] = jnp.zeros_like(acc_ref)
                 start_row = start_ref[near, seq, pl.ds(tile, 1), :]
@@ -476,11 +476,14 @@
             lax.fori_loop(0, tiles, query_tile, 0)
 
 
-def attend_back_kernel(chips, base_ref, edge_ref, far_ref, q_ref, g_ref, o_ref, lse_ref, *refs):
-    kv_refs = refs[:chips]
-    start_ref, end_ref, bias_ref, dq_ref = refs[chips : chips + 4]
-    dkv_refs = refs[chips + 4 : 2 * chips + 4]
-    band_ref, sides_ref, k_rows, v_rows, k_aug, dk_acc, dv_acc, dq_acc = refs[2 * chips + 4 :]
+def attend_back_kernel(chips, carried, base_ref, edge_ref, far_ref, g_ref, o_ref, lse_ref, *refs):
+    kv_refs, q_ref, refs = refs[:chips], refs[0], refs[chips:]
+    start_ref, end_ref, bias_ref, *refs = refs
+    if carried:
+        old_band_ref, old_sides_ref, *refs = refs
+    made_refs, refs = refs[:chips], refs[chips:]
+    dq_ref = made_refs[0]
+    band_ref, sides_ref, k_rows, v_rows, k_aug, dk_acc, dv_acc, dq_acc = refs
     groups, _, span = q_ref.shape
     blocks, seq_count, span_len, _ = k_rows.shape
     part_len = span_len // groups
@@ -491,9 +494,9 @@
         for seq, near, source, lanes in pieces_of(seq_count, part_len, groups):
             block = 2 * far + near
             rows = slice(source * part_len, (source + 1) * part_len)
-            piece = kv_refs[far][source, :HD, lanes]
+            piece = kv_refs[far][source, HD : 2 * HD, lanes]
             k_rows[block, seq, rows, :] = flipped(piece)
-            v_rows[block, seq, rows, :] = flipped(kv_refs[far][source, HD:, lanes])
+            v_rows[block, seq, rows, :] = flipped(kv_refs[far][source, 2 * HD :, lanes])
             at = source % per_key * part_len
             k_aug[block, seq, source // per_key, :HD, at : at + part_len] = piece
     for block in range(blocks):
@@ -502,8 +505,8 @@
                 k_aug[block, seq, tile, HD:, :] = ones_row(KT)
     dk_acc[...] = jnp.zeros_like(dk_acc)
     dv_acc[...] = jnp.zeros_like(dv_acc)
-    band_ref[...] = jnp.zeros_like(band_ref)
-    sides_ref[...] = jnp.zeros_like(sides_ref)
+    band_ref[...] = old_band_ref[...] if carried else jnp.zeros_like(band_ref)
+    sides_ref[...] = old_sides_ref[...] if carried else jnp.zeros_like(sides_ref)
 
     for seq in range(seq_count):
         for near in range(2):
@@ -512,9 +515,9 @@
             def query_tile(tile, _, seq=seq, near=near, lane_base=lane_base):
                 query_at = base_ref[near] + tile * TQ
                 row = (near * seq_count + seq) * tiles + tile
-                queries = lanes_of(q_ref, (), tile, per_tile, part_len, lane_base)
-                grads = lanes_of(g_ref, (), tile, per_tile, part_len, lane_base)
-                outs = lanes_of(o_ref, (), tile, per_tile, part_len, lane_base)
+                queries = lanes_of(q_ref, tile, per_tile, part_len, lane_base)
+                grads = lanes_of(g_ref, tile, per_tile, part_len, lane_base)
+                outs = lanes_of(o_ref, tile, per_tile, part_len, lane_base)
                 delta = jnp.sum(grads.astype(jnp.float32) * outs, axis=0, keepdims=True)
                 query_rows, grad_rows = flipped(queries), flipped(grads)
                 lse = lse_ref[near, seq, pl.ds(tile, 1), :]
@@ -560,7 +563,7 @@
                 lax.fori_loop(0, blocks * key_tiles, key_step, 0)
                 for k in range(per_tile):
                     part = dq_acc[:HD, k * part_len : (k + 1) * part_len].astype(jnp.bfloat16)
-                    dq_ref[tile * per_tile + k, :, lane_base : lane_base + part_len] = part
+                    dq_ref[tile * per_tile + k, :HD, lane_base : lane_base + part_len] = part
                 return 0
 
             lax.fori_loop(0, tiles, query_tile, 0)
@@ -568,8 +571,9 @@
         for seq, near, source, lanes in pieces_of(seq_count, part_len, groups):
             block = 2 * far + near
             rows = slice(source * part_len, (source + 1) * part_len)
-            dkv_refs[far][source, :HD, lanes] = dk_acc[block, seq, rows, :].T.astype(jnp.bfloat16)
-            dkv_refs[far][source, HD:, lanes] = dv_acc[block, seq, rows, :].T.astype(jnp.bfloat16)
+            top = 0 if far else HD
+            made_refs[far][source, top : top + HD, lanes] = dk_acc[block, seq, rows, :].T.astype(jnp.bfloat16)
+            made_refs[far][source, top + HD : top + 2 * HD, lanes] = dv_acc[block, seq, rows, :].T.astype(jnp.bfloat16)
 
 
 def strip_places():
@@ -640,20 +644,21 @@
 VMEM = pl.BlockSpec(memory_space=pltpu.VMEM)
 
 
-def attend(base, edges, far_bias, q, kvs, starts, ends, bias):
+def attend(base, edges, far_bias, kvs, starts, ends, bias):
     chips = len(kvs)
-    groups, _, span = q.shape
+    groups, _, span = kvs[0].shape
+    shape = (groups, HD, span)
     _, seq_count, tiles, _ = starts.shape
     blocks, span_len = 2 * chips, tiles * TQ
     return pl.pallas_call(
         functools.partial(attend_kernel, chips),
         name="attend",
         out_shape=(
-            jax.ShapeDtypeStruct(q.shape, jnp.float32),
-            jax.ShapeDtypeStruct(q.shape, jnp.bfloat16),
+            jax.ShapeDtypeStruct(shape, jnp.float32),
+            jax.ShapeDtypeStruct(shape, jnp.bfloat16),
             jax.ShapeDtypeStruct(starts.shape, jnp.float32),
         ),
-        in_specs=[SMEM] * 3 + [VMEM] * (1 + chips + 3),
+        in_specs=[SMEM] * 3 + [VMEM] * (chips + 3),
         out_specs=(VMEM,) * 3,
         scratch_shapes=[
             pltpu.VMEM((blocks, seq_count, span_len, HD), jnp.bfloat16),
@@ -661,24 +666,24 @@
             pltpu.VMEM((8, TQ), jnp.float32),
             pltpu.VMEM((AUG, TQ), jnp.float32),
         ],
+        cost_estimate=pl.CostEstimate(flops=1, transcendentals=0, bytes_accessed=1),
         compiler_params=pltpu.CompilerParams(vmem_limit_bytes=48 * 2**20),
-    )(base, edges, far_bias, q, *kvs, starts, ends, bias)
-
-
-def attend_back(base, edges, far_bias, q, g, o, lse, kvs, starts, ends, bias):
+    )(base, edges, far_bias, *kvs, starts, ends, bias)
+
+
+def attend_back(base, edges, far_bias, g, o, lse, kvs, starts, ends, bias, sums=()):
     chips = len(kvs)
-    groups, _, span = q.shape
+    groups, _, span = g.shape
     _, seq_count, tiles, _ = starts.shape
     blocks, span_len = 2 * chips, tiles * TQ
-    low = jax.ShapeDtypeStruct(q.shape, jnp.bfloat16)
     made = pl.pallas_call(
-        functools.partial(attend_back_kernel, chips),
+        functools.partial(attend_back_kernel, chips, bool(sums)),
         name="attend_back",
-        out_shape=(low,)
-        + (jax.ShapeDtypeStruct(kvs[0].shape, jnp.bfloat16),) * chips
+        out_shape=(jax.ShapeDtypeStruct(kvs[0].shape, jnp.bfloat16),)
+        + (jax.ShapeDtypeStruct((groups, 2 * HD, span), jnp.bfloat16),) * (chips - 1)
         + (jax.ShapeDtypeStruct(bias.shape, jnp.float32), jax.ShapeDtypeStruct((8, TQ), jnp.float32)),
-        in_specs=[SMEM] * 3 + [VMEM] * (4 + chips + 3),
-        out_specs=(VMEM,) * (3 + chips),
+        in_specs=[SMEM] * 3 + [VMEM] * (3 + chips + 3 + len(sums)),
+        out_specs=(VMEM,) * (2 + chips),
         scratch_shapes=[
             pltpu.VMEM((blocks, seq_count, span_len, HD), jnp.bfloat16),
             pltpu.VMEM((blocks, seq_count, span_len, HD), jnp.bfloat16),
@@ -687,12 +692,10 @@
             pltpu.VMEM((blocks, seq_count, span_len, HD), jnp.float32),
             pltpu.VMEM((AUG, TQ), jnp.float32),
         ],
+        cost_estimate=pl.CostEstimate(flops=1, transcendentals=0, bytes_accessed=1),
         compiler_params=pltpu.CompilerParams(vmem_limit_bytes=56 * 2**20),
-    )(base, edges, far_bias, q, g, o, lse, *kvs, starts, ends, bias)
-    return made[0], made[1 : 1 + chips], made[-2], made[-1]
-
-
-AXES = ("head", "blk")
+    )(base, edges, far_bias, g, o, lse, *kvs, starts, ends, bias, *sums)
+    return made[0], made[1:chips], made[-2:]
 
 
 def trade(block, axis, bit):
@@ -720,13 +723,13 @@
     for source, source_rows, target, target_rows, count in plan:
         views = []
         for which, (slot, scale, first, columns) in ((source, source_rows), (target, target_rows)):
-            begin = first if slot is None else pl.multiple_of(slots_ref[slot] * scale, 16) + first
+            begin = first if slot is None else pl.multiple_of(slots_ref[slot] * scale, 8) + first
             views.append(arrays[which].at[pl.ds(begin, count), pl.ds(columns[0], columns[1])])
         views[1][...] = views[0][...]
 
 
 def moved(name, slots, sources, shapes, plan):
-    outs = tuple(jax.ShapeDtypeStruct(shape, jnp.bfloat16) for shape in shapes)
+    outs = tuple(jax.ShapeDtypeStruct(shape, sources[0].dtype) for shape in shapes)
     return pl.pallas_call(
         functools.partial(copy_kernel, plan),
         name=name,
@@ -741,58 +744,143 @@
 CHIPS = 16
 
 
-def relative_slots():
+def turn_of(k):
+    return k % DEPTH, k // DEPTH // 2, k // DEPTH % 2
+
+
+def slot_table():
     n_blk = lax.axis_size("blk")
-    chip = lax.axis_index("head") * (n_blk // 2) + lax.axis_index("blk") // 2
-    turns = [4 * z + 2 * y + x for y, x in ((0, 0), (0, 1), (1, 0), (1, 1)) for z in range(DEPTH)]
-    return chip ^ jnp.asarray(turns, jnp.int32)
-
-
-def piece_rows(rows):
+    group, place = lax.axis_index("head"), lax.axis_index("blk")
+    groups = group ^ jnp.asarray([2 * turn_of(k)[0] + turn_of(k)[1] for k in range(CHIPS)], jnp.int32)
+    sides = (place // 2) ^ jnp.asarray([turn_of(k)[2] for k in range(CHIPS)], jnp.int32)
+    chips = groups * (n_blk // 2) + sides
+    return jnp.concatenate([chips, groups, 2 * chips + place % 2, 2 * chips + 1 - place % 2])
+
+
+CHIP, GROUP, DEVICE, MATE = 0, CHIPS, 2 * CHIPS, 3 * CHIPS
+
+
+def after(block, *earlier):
+    return lax.optimization_barrier((block, earlier))[0]
+
+
+def beside(made, *sent):
+    return lax.optimization_barrier((made, *sent))
+
+
+def wide(block):
+    return block.astype(jnp.float32)
+
+
+def placed(name, slots, blocks, layout, shapes, order):
+    plan = []
+    for k, (which, at) in enumerate(order):
+        for first, count, whole, take, target in layout:
+            plan.append((which, (None, 0, at + first, take), len(blocks) + whole, target(k), count))
+    return moved(name, slots, blocks, shapes, tuple(plan))
+
+
+def parted(name, slots, wholes, layout, shapes, order):
+    plan = []
+    for k, (which, at) in enumerate(order):
+        for first, count, whole, take, target in layout:
+            plan.append((whole, target(k), len(wholes) + which, (None, 0, at + first, take), count))
+    return moved(name, slots, wholes, shapes, tuple(plan))
+
+
+def grouped(rows):
+    order = []
     for k in range(CHIPS):
         group, z = k // DEPTH, k % DEPTH
-        if group < 3:
-            yield k, group, z * rows
-        else:
-            yield k, 3 + z // 2, z % 2 * rows
-
-
-def spread_out(name, slots, payload, parts):
-    layout, shapes = parts
-    rows, width = payload.shape
-    own = jnp.concatenate([payload] + [across_z(payload, k) for k in range(1, DEPTH)], axis=0)
-    by_x, by_y = across_x(own), across_y(own)
-    half = DEPTH // 2 * rows
-    low, high = across_y(by_x[:half]), across_x(by_y[half:])
-    plan = []
-    for k, piece, at in piece_rows(rows):
-        for first, count, whole, take, put in layout:
-            plan.append(
-                (piece, (None, 0, at + first, take), 5 + whole, (k, count if put[2] is None else put[2], put[1], put[0]), count)
-            )
-    return moved(name, slots, (own, by_x, by_y, low, high), shapes, tuple(plan))
-
-
-def drawn_in(name, slots, wholes, layout, rows, width):
-    plan = []
-    for k, piece, at in piece_rows(rows):
-        for first, count, whole, take, put in layout:
-            plan.append(
-                (whole, (k, count if put[2] is None else put[2], put[1], put[0]), len(wholes) + piece, (None, 0, at + first, take), count)
-            )
+        order.append((group, z * rows) if group < 3 else (3 + z // 2, z % 2 * rows))
+    return order
+
+
+def gather_z(payload, *earlier):
+    payload = after(payload, *earlier) if earlier else payload
+    return [payload] + [across_z(payload, k) for k in range(1, DEPTH)]
+
+
+def gather_xy(own, *earlier):
+    own = jnp.concatenate(own, axis=0)
+    own = after(own, *earlier) if earlier else own
+    return own, across_x(own), across_y(own)
+
+
+def gather_corner(blocks, *earlier):
+    own, by_x, by_y = blocks
+    half = own.shape[0] // 2
+    low, high = by_x[:half], by_y[half:]
+    if earlier:
+        low, high = after(low, *earlier), after(high, *earlier)
+    return own, by_x, by_y, across_y(low), across_x(high)
+
+
+def sum_corner(name, slots, wholes, layout, rows, width):
     full, half = DEPTH * rows, DEPTH // 2 * rows
     shapes = ((full, width),) * 3 + ((half, width),) * 2
-    own, by_x, by_y, low, high = moved(name, slots, wholes, shapes, tuple(plan))
-    low, high = across_y(low), across_x(high)
-    wide = lambda block: block.astype(jnp.float32)
-    by_x = jnp.concatenate([(wide(by_x[:half]) + wide(low)).astype(jnp.bfloat16), by_x[half:]], axis=0)
-    by_y = jnp.concatenate([by_y[:half], (wide(by_y[half:]) + wide(high)).astype(jnp.bfloat16)], axis=0)
-    by_x, by_y = across_x(by_x), across_y(by_y)
-    column = wide(own) + wide(by_x) + wide(by_y)
+    own, by_x, by_y, low, high = parted(name, slots, wholes, layout, shapes, grouped(rows))
+    return own, by_x, by_y, across_y(low), across_x(high)
+
+
+def sum_xy(blocks, *earlier):
+    own, by_x, by_y, low, high = blocks
+    half = low.shape[0]
+    if earlier:
+        low, high = after(low, *earlier), after(high, *earlier)
+    by_x = jnp.concatenate([(wide(by_x[:half]) + wide(low)).astype(by_x.dtype), by_x[half:]], axis=0)
+    by_y = jnp.concatenate([by_y[:half], (wide(by_y[half:]) + wide(high)).astype(by_y.dtype)], axis=0)
+    return own, across_x(by_x), across_y(by_y)
+
+
+def sum_z(blocks, *earlier):
+    own, by_x, by_y = blocks
+    by_x = after(by_x, *earlier) if earlier else by_x
+    return column_sum(wide(own) + wide(by_x) + wide(by_y), own.dtype)
+
+
+def column_sum(column, kind):
+    rows = column.shape[0] // DEPTH
     total = column[:rows]
     for k in range(1, DEPTH):
-        total = total + wide(across_z(column[k * rows : (k + 1) * rows].astype(jnp.bfloat16), k))
+        total = total + wide(across_z(column[k * rows : (k + 1) * rows].astype(kind), k))
     return total
+
+
+def halves_kernel(core_ref, in_ref, out_ref, down_ref, in_w_ref, out_w_ref, down_w_ref):
+    devices, rows, width = out_ref.shape
+    for d in range(devices):
+        here = pl.ds(d * rows, rows)
+        for j in range(in_ref.shape[1] // rows):
+            in_w_ref[here, j * width : (j + 1) * width] = in_ref[d, j * rows : (j + 1) * rows, :]
+        out_w_ref[here, :] = out_ref[d]
+    chips, _, rows, _ = down_ref.shape
+    for chip in range(chips):
+        down_w_ref[pl.ds(chip * rows, rows), :] = down_ref[chip, 0]
+
+
+def own_halves(core, whole, down_rows, shard):
+    devices, rows, width = whole.shape
+    steps, chips = 4, devices // 2
+    in_rows = (rows - down_rows - shard) // 2
+    in_at, out_at = down_rows // in_rows, (rows - shard) // shard
+    shapes = ((devices * shard, in_rows // shard * width), (devices * shard, width), (chips * down_rows, width))
+    return pl.pallas_call(
+        halves_kernel,
+        name="own_halves",
+        grid_spec=pltpu.PrefetchScalarGridSpec(
+            num_scalar_prefetch=1,
+            grid=(steps,),
+            in_specs=[
+                pl.BlockSpec((devices // steps, in_rows, width), lambda i, core_ref: (i, in_at + core_ref[0], 0)),
+                pl.BlockSpec((devices // steps, shard, width), lambda i, core_ref: (i, out_at, 0)),
+                pl.BlockSpec((chips // steps, 1, down_rows, width), lambda i, core_ref: (i, core_ref[0], 0, 0)),
+            ],
+            out_specs=[pl.BlockSpec((shape[0] // steps, shape[1]), lambda i, core_ref: (i, 0)) for shape in shapes],
+        ),
+        out_shape=[jax.ShapeDtypeStruct(shape, whole.dtype) for shape in shapes],
+        compiler_params=pltpu.CompilerParams(vmem_limit_bytes=32 * 2**20),
+    )(core.reshape(1), whole, whole, whole.reshape(chips, 2, rows, width))
 
 
 def document_bounds(segments):
@@ -808,7 +896,7 @@
 
 
 def query_bounds(bounds, place, tile):
-    near = [lax.dynamic_index_in_dim(bounds, place ^ k, 1, keepdims=False) for k in range(2)]
+    near = [lax.dynamic_index_in_dim(bounds, place ^ k, 1, keepdims=False) for k in (0, 2)]
     near = jnp.stack(near, axis=0)
     return near.reshape(near.shape[0], near.shape[1], -1, tile)
 
@@ -834,7 +922,7 @@
 def norm_back(grad, rows, scale, gain):
     weighted = grad * gain
     inner = jnp.mean(rows * weighted, axis=-1, keepdims=True)
-    return scale * weighted - rows * (scale * scale * scale) * inner, jnp.sum(grad * rows * scale, axis=0)
+    return scale * weighted - rows * (scale * scale * scale) * inner
 
 
 def dot_on(left, right, left_dim, right_dim):
@@ -863,64 +951,78 @@
     blocks = lax.axis_size("blk")
     group, place = lax.axis_index("head"), lax.axis_index("blk")
     core, side = place % 2, place // 2
-    slots = relative_slots()
+    slots = slot_table()
     shard = w_query.shape[0]
     chip_rows = 2 * shard
+    head_cols = 3 * HD
+    first_cols = groups * head_cols
     half_width = groups * HD
-    hidden = w_in.shape[1]
-    half_hidden = hidden // 2
+    half_hidden = w_in.shape[1] // 2
     down_rows = w_down.shape[0]
+    half_out = half_width // 2
+    tokens = seq_count * part_len
 
     def by_core(first, second):
         return jnp.where(core == 0, first, second)
 
+    def by_side(first, second):
+        return jnp.where(side == 0, first, second)
+
+    def exchanged(block):
+        return lax.all_to_all(block, "head", split_axis=0, concat_axis=0, tiled=True)
+
+    every, first_every = (0, width), (0, first_cols)
+    gains = jnp.concatenate([norm_gain, ff_gain, rel_bias, jnp.zeros((128 - 5 * shard // 2,), low)])
+    gains_near = mate(gains[None, :])[0]
+    gains = jnp.stack([by_core(gains, gains_near), by_core(gains_near, gains)], axis=0)
+    gains = jnp.pad(gains, ((0, 14), (0, 0)))
+    lay_gain = ((0, 16, 0, (0, 128), lambda k: (CHIP + k, 16, 0, (0, 128))),)
+    gain_blocks = gather_corner(gather_xy(gather_z(gains)))
+
     def head_columns(weight, which):
         return weight.reshape(shard, groups, 2, HD)[:, :, which]
 
     def cut(which):
-        key_value = jnp.stack([head_columns(w_key, which), head_columns(w_value, which)], axis=2).reshape(shard, -1)
-        query = head_columns(w_query, which).reshape(shard, -1)
-        hidden_in = w_in.reshape(shard, -1, 2, down_rows)[:, :, which].reshape(shard, -1)
-        return jnp.concatenate([key_value, query, hidden_in], axis=1)
+        return jnp.stack([head_columns(w, which) for w in (w_query, w_key, w_value)], axis=2).reshape(shard, -1)
 
     first_cut, second_cut = cut(0), cut(1)
-    gains = jnp.concatenate([norm_gain, ff_gain, rel_bias, jnp.zeros((128 - 5 * shard // 2,), low)])
-    gains = jnp.pad(gains[None, :], ((0, shard - 1), (0, 0)))
-    kept = jnp.concatenate([by_core(first_cut, second_cut), gains], axis=1)
-    given = mate(jnp.concatenate([by_core(second_cut, first_cut), gains], axis=1))
-    chip_cut = jnp.concatenate([by_core(kept, given), by_core(given, kept)], axis=0)
-    edge_kv, edge_q, edge_in = 2 * half_width, 3 * half_width, 3 * half_width + half_hidden
-    gain_rows = jnp.stack([chip_cut[0, edge_in:], chip_cut[shard, edge_in:]], axis=0)
-    gain_rows = jnp.pad(gain_rows, ((0, 14), (0, width - 128)))
-    payload_kv = jnp.concatenate([chip_cut[:, :edge_kv], gain_rows], axis=0)
-    cut_q = chip_cut[:, edge_kv:edge_q]
-    payload_q = jnp.concatenate([cut_q[:shard], cut_q[shard:]], axis=1)
-    cut_in = chip_cut[:, edge_q:edge_in]
-    swap = [(b, (b % 2) * 2 + b // 2) for b in range(blocks)]
-    payload_in = jnp.concatenate([cut_in[:, :width], cut_in[:, width:], lax.ppermute(w_out, "blk", swap)], axis=0)
-
-    every = (0, width)
-    lay_kv = ((0, chip_rows, 0, every, (every, 0, None)), (chip_rows, 16, 1, (0, 128), ((0, 128), 0, None)))
-    lay_q = (
-        (0, shard, 0, (0, half_width), ((0, half_width), 0, chip_rows)),
-        (0, shard, 0, (half_width, half_width), ((0, half_width), shard, chip_rows)),
-    )
+    chunks = [by_side(first_cut, second_cut), across_x(by_side(second_cut, first_cut))]
+    first_blocks, pace = [], None
+    for chunk in chunks:
+        own = jnp.concatenate(gather_z(chunk), axis=0)
+        pace = own
+        both = jnp.concatenate([own, across_y(own)], axis=0)
+        first_blocks += [both, mate(both)]
+    plan = []
+    for k in range(CHIPS):
+        z, y, x = turn_of(k)
+        for far, slot in enumerate((DEVICE, MATE)):
+            source = (None, 0, (DEPTH * y + z) * shard, first_every)
+            plan.append((2 * x + far, source, 4, (slot + k, shard, 0, first_every), shard))
+    (first_w,) = moved("whole_first", slots, first_blocks, ((width, first_cols),), tuple(plan))
+
+    def hidden_columns(which):
+        return w_in.reshape(shard, -1, 2, down_rows)[:, :, which].reshape(shard, -1, width)
+
+    payload_in = jnp.stack([hidden_columns(0), hidden_columns(1)], axis=0).transpose(0, 2, 1, 3).reshape(-1, width)
+    in_rows = 2 * chip_rows + shard
+    payload = jnp.concatenate([w_down, payload_in, w_out], axis=0)
+    whole = lax.all_gather(payload, ("head", "blk"), axis=0, tiled=False)
+    in_w, out_w, down_w = own_halves(core, whole, down_rows, shard)
+
     lay_in = (
-        (0, chip_rows, 0, every, ((0, width), 0, None)),
-        (chip_rows, chip_rows, 0, every, ((width, width), 0, None)),
-        (2 * chip_rows, shard, 1, every, (every, 0, None)),
-    )
-    lay_down = ((0, down_rows, 0, every, (every, 0, None)),)
-    kv_w, gain_w = spread_out("whole_kv", slots, payload_kv, (lay_kv, ((width, width), (16 * CHIPS, 128))))
-    (query_w,) = spread_out("whole_q", slots, payload_q, (lay_q, ((width, half_width),)))
-    in_w, out_w = spread_out("whole_in", slots, payload_in, (lay_in, ((width, half_hidden), (half_width, width))))
-    (down_w,) = spread_out("whole_down", slots, w_down, (lay_down, ((half_hidden, width),)))
-
-    gain_w = gain_w.reshape(CHIPS, 16, 128)[:, :2].astype(jnp.float32)
+        (0, chip_rows, 0, every, lambda k: (CHIP + k, chip_rows, 0, (0, width))),
+        (chip_rows, chip_rows, 0, every, lambda k: (CHIP + k, chip_rows, 0, (width, width))),
+        (2 * chip_rows, shard, 1, every, lambda k: (CHIP + k, shard, 0, every)),
+    )
+    lay_down = ((0, down_rows, 0, every, lambda k: (CHIP + k, down_rows, 0, every)),)
+
+    (gain_w,) = placed("whole_gain", slots, gain_blocks, lay_gain, ((16 * CHIPS, 128),), grouped(16))
+    gain_w = wide(gain_w.reshape(CHIPS, 16, 128)[:, :2])
     gain_one = gain_w[:, :, :shard].reshape(-1)
     gain_two = gain_w[:, :, shard : 2 * shard].reshape(-1)
     rel_table = gain_w[:, :, 2 * shard : 5 * shard // 2].reshape(HEADS, BUCKETS)
-    rel_here = lax.dynamic_index_in_dim(rel_table, 2 * group + core, 0, keepdims=False)
+    rel_here = lax.dynamic_index_in_dim(rel_table, 2 * group + side, 0, keepdims=False)
 
     bucket_hot = bucket_table[:, None] == lax.iota(jnp.int32, BUCKETS)[None, :]
     by_offset = jnp.sum(jnp.where(bucket_hot, rel_here[None, :], 0.0), axis=1)
@@ -933,109 +1035,164 @@
     bias = bias_strip(far_bias, waves)
     starts, ends = document_bounds(segments)
     starts, ends = query_bounds(starts, place, TQ), query_bounds(ends, place, TQ)
-    edges = jnp.stack([starts[..., 0], starts[..., -1], ends[..., 0], ends[..., -1]], axis=-1).reshape(-1)
-    base = (place ^ lax.iota(jnp.int32, blocks)) * span_len
-
-    token_rows = inputs.reshape(-1, width).astype(jnp.float32)
-    scale_one = lax.rsqrt(jnp.mean(token_rows * token_rows, axis=-1, keepdims=True) + EPS)
-    first_in = joined((token_rows * scale_one * gain_one).astype(low))
-    tokens = first_in.shape[0]
-
-    def exchanged(block):
-        return lax.all_to_all(block, "head", split_axis=0, concat_axis=0, tiled=True)
-
-    key_value = exchanged(dot_on(kv_w, first_in, 0, 1).astype(low).reshape(groups, 2 * HD, tokens))
-    queries = exchanged(dot_on(query_w, first_in, 0, 1).astype(low).reshape(groups, HD, tokens))
-    kvs = [key_value, across_x(key_value)]
-    attended, attended_low, lse = attend(base, edges, far_bias, queries, kvs, starts, ends, bias)
-    attn_cols = exchanged(attended_low).reshape(half_width, tokens)
-
-    hidden_one = token_rows + halves_added(dot_on(attn_cols, out_w, 0, 0))
+    edges = jnp.stack([starts[..., 0], starts[..., -1], ends[..., 0], ends[..., -1]], axis=-1)
+    base = (place ^ jnp.asarray([0, 2, 1, 3], jnp.int32)) * span_len
+
+    input_rows = inputs.reshape(tokens, width)
+    both_rows = wide(jnp.concatenate([input_rows, across_x(input_rows)], axis=0))
+    both_scale = lax.rsqrt(jnp.mean(both_rows * both_rows, axis=-1, keepdims=True) + EPS)
+    token_rows, scale_one = both_rows[:tokens], both_scale[:tokens]
+    first_in = (both_rows * both_scale * gain_one).astype(low).reshape(2, seq_count, part_len, width)
+    first_in = [first_in[:, seq].reshape(2 * part_len, width) for seq in range(seq_count)]
+
+    made = [dot_on(first_w, rows, 0, 1).astype(low) for rows in first_in]
+    bounds = [(starts[:, seq : seq + 1], ends[:, seq : seq + 1], bias) for seq in range(seq_count)]
+    edges = [edges[:, seq].reshape(-1) for seq in range(seq_count)]
+    attended, heads, attn_cols = [], [], [None] * seq_count
+    sent = exchanged(made[0].reshape(groups, head_cols, 2 * part_len))
+    for seq in range(seq_count):
+        heads.append([sent, mate(sent)])
+        done = attend(base, edges[seq], far_bias, heads[seq], *bounds[seq])
+        if seq + 1 < seq_count:
+            done, sent = beside(done, exchanged(made[seq + 1].reshape(groups, head_cols, 2 * part_len)))
+        else:
+            done, attn_cols[seq - 1] = beside(done, attn_cols[seq - 1])
+        attended.append(done)
+        attn_cols[seq] = exchanged(done[1])
+    attn_cols = [block.reshape(half_width, 2 * part_len) for block in attn_cols]
+    attn_near = [block[:, :part_len] for block in attn_cols]
+    attn_far = [across_x(block[:, part_len:]) for block in attn_cols]
+    attn_near, attn_far = jnp.concatenate(attn_near, axis=1), jnp.concatenate(attn_far, axis=1)
+
+    def by_head(near, far):
+        near, far = near.reshape(groups, 1, HD, -1), far.reshape(groups, 1, HD, -1)
+        return jnp.concatenate([by_side(near, far), by_side(far, near)], axis=1).reshape(2 * half_width, -1)
+
+    attn_cols = by_head(attn_near, attn_far)
+    hidden_one = token_rows + dot_on(attn_cols, out_w, 0, 0)
     scale_two = lax.rsqrt(jnp.mean(hidden_one * hidden_one, axis=-1, keepdims=True) + EPS)
     second_in = joined((hidden_one * scale_two * gain_two).astype(low))
     activated, rise = gelu_both(dot_on(second_in, in_w, 1, 0))
     activated = activated.astype(low)
     layer_out = (hidden_one + halves_added(dot_on(activated, down_w, 1, 0))).astype(low).reshape(inputs.shape)
 
-    incoming_low = cotangent.reshape(-1, width)
+    incoming_low = cotangent.reshape(tokens, width)
     incoming = joined(incoming_low)
     up_grad = (dot_on(incoming, down_w, 1, 1) * rise).astype(low)
-    second_grad = halves_added(dot_on(up_grad, in_w, 1, 1))
-    hidden_part, grad_gain_two = norm_back(second_grad, hidden_one, scale_two, gain_two)
-    hidden_grad = incoming_low.astype(jnp.float32) + hidden_part
-    branch = joined(hidden_grad.astype(low))
-    grad_cols = dot_on(out_w, branch, 1, 1).astype(low).reshape(groups, HD, tokens)
-    grad_heads = exchanged(grad_cols)
-
     whole_down = dot_on(activated, incoming, 0, 0).astype(low)
-    grad_down = drawn_in("parts_down", slots, (whole_down,), lay_down, down_rows, width)
-    whole_in = dot_on(second_in, up_grad, 0, 0).astype(low)
-    whole_out = dot_on(attn_cols, branch, 1, 0).astype(low)
-    in_sum = drawn_in("parts_in", slots, (whole_in, whole_out), lay_in, 2 * chip_rows + shard, width)
-
-    query_grad, kv_grads, band, sides = attend_back(
-        base, edges, far_bias, queries, grad_heads, attended, lse, kvs, starts, ends, bias
-    )
-    kv_grad = (kv_grads[0].astype(jnp.float32) + across_x(kv_grads[1]).astype(jnp.float32)).astype(low)
-    kv_cols = exchanged(kv_grad).reshape(2 * half_width, tokens)
-    query_cols = exchanged(query_grad).reshape(half_width, tokens)
-    first_grad = halves_added(dot_on(kv_cols, kv_w, 0, 1) + dot_on(query_cols, query_w, 0, 1))
-    input_part, grad_gain_one = norm_back(first_grad, token_rows, scale_one, gain_one)
+    down_parts = sum_corner("parts_down", slots, (whole_down,), lay_down, down_rows, width)
+    second_grad = dot_on(up_grad, in_w, 1, 1)
+    second_grad = halves_added(second_grad)
+    hidden_part = norm_back(second_grad, hidden_one, scale_two, gain_two)
+    gain_terms = second_grad * hidden_one * scale_two
+    hidden_grad = wide(incoming_low) + hidden_part
+    branch, down_parts = beside(hidden_grad.astype(low), down_parts)
+    down_parts = sum_xy(down_parts)
+    grad_cols = dot_on(out_w, branch, 1, 1).astype(low)
+    grad_cols = grad_cols.reshape(groups, 2, HD, tokens)
+    grad_far = across_x(by_side(grad_cols[:, 1], grad_cols[:, 0]))
+    grad_near = by_side(grad_cols[:, 0], grad_cols[:, 1])
+
+    whole_in = dot_on(after(second_in, grad_cols), up_grad, 0, 0).astype(low)
+    whole_out = dot_on(attn_cols, branch, 1, 0).astype(low).reshape(-1, 2, shard, width)
+    out_mine, out_given = by_core(whole_out[:, 0], whole_out[:, 1]), by_core(whole_out[:, 1], whole_out[:, 0])
+    whole_out = (wide(out_mine) + wide(mate(out_given))).astype(low).reshape(half_width, width)
+    in_parts = sum_corner("parts_in", slots, (whole_in, whole_out), lay_in, in_rows, width)
+
+    lanes = [slice(seq * part_len, (seq + 1) * part_len) for seq in range(seq_count)]
+    grads = [block[:, :, lane] for lane in lanes for block in (grad_near, grad_far)]
+    grads = exchanged(jnp.concatenate(grads, axis=2))
+    grads = [grads[:, :, 2 * part_len * seq : 2 * part_len * (seq + 1)] for seq in range(seq_count)]
+    grads[0], down_parts = beside(grads[0], down_parts)
+    sums, made, sent = (), [], None
+    for seq in range(seq_count):
+        outs, _, lse = attended[seq]
+        done = attend_back(base, edges[seq], far_bias, grads[seq], outs, lse, heads[seq], *bounds[seq], sums)
+        if seq == 0:
+            done, in_parts, grad_down = beside(done, in_parts, sum_z(down_parts))
+        else:
+            done, in_parts, made[0] = beside(done, in_parts, made[0])
+        near_grad, (far_grad,), sums = done
+        far_grad = wide(mate(far_grad))
+        near_grad = jnp.concatenate([near_grad[:, :HD], (wide(near_grad[:, HD:]) + far_grad).astype(low)], axis=1)
+        if seq == 0:
+            grads[1], near_grad = beside(grads[1], near_grad)
+            in_parts = sum_xy(in_parts)
+        else:
+            in_sum = sum_z(in_parts, near_grad)
+        made.append(exchanged(near_grad))
+    made = [block.reshape(first_cols, 2 * part_len) for block in made]
+    whole_first = sum(dot_on(first_in[seq], made[seq], 0, 1) for seq in range(seq_count))
+    first_grads = [dot_on(block, first_w, 0, 1) for block in made]
+    band, sides = sums
+
+    ones = lax.broadcasted_iota(jnp.int32, (2 * tokens, 128), 1)
+    terms = jnp.stack([grad.reshape(2, part_len, width) for grad in first_grads], axis=1).reshape(2 * tokens, width)
+    terms = (terms * both_rows * both_scale).astype(low)
+    gain_cols = dot_on(terms, (ones == 0).astype(low), 0, 0)
+    gain_cols = gain_cols + dot_on(gain_terms.astype(low), (ones[:tokens] == 1).astype(low), 0, 0)
+    whole_first = jnp.concatenate([whole_first.astype(low), gain_cols.astype(low)], axis=1)
+    plan, all_cols = [], (0, first_cols + 128)
+    for k in range(CHIPS):
+        z, y, x = turn_of(k)
+        at = (None, 0, (DEPTH * y + z) * shard, all_cols)
+        plan.append((0, (MATE + k, shard, 0, all_cols), 1 + 3 * x, at, shard))
+        at = (None, 0, z * shard, all_cols)
+        plan.append((0, (DEVICE + k, shard, 0, all_cols), 2 + 3 * x + y, at, shard))
+    column = DEPTH * shard
+    shapes = ((2 * column, all_cols[1]), (column, all_cols[1]), (column, all_cols[1])) * 2
+    parts = moved("parts_first", slots, (whole_first,), shapes, tuple(plan))
+    first_sums, pace = [None, None], None
+    for x in (1, 0):
+        given, near, by_y = parts[3 * x : 3 * x + 3]
+        got = mate(given)
+        by_y = across_y((wide(by_y) + wide(got[column:])).astype(low))
+        total = column_sum(wide(near) + wide(got[:column]) + wide(by_y), low)
+        first_sums[x] = across_x(total) if x else total
+        pace = got if pace is None else pace
+
+    near_part = jnp.concatenate([grad[:part_len] for grad in first_grads], axis=0)
+    far_part = jnp.concatenate([grad[part_len:] for grad in first_grads], axis=0).astype(low)
+    first_grad = near_part + wide(across_x(after(far_part, pace)))
+    input_part = norm_back(first_grad, token_rows, scale_one, gain_one)
     input_grad = (hidden_grad + input_part).astype(low).reshape(inputs.shape)
 
-    whole_kv = dot_on(first_in, kv_cols, 0, 1).astype(low)
-    kv_sum = drawn_in("parts_kv", slots, (whole_kv,), lay_kv[:1], chip_rows, width)
-    whole_q = dot_on(first_in, query_cols, 0, 1).astype(low)
-    gain_grads = jnp.stack([grad_gain_one.reshape(CHIPS, -1), grad_gain_two.reshape(CHIPS, -1)], axis=1)
-    gain_grads = jnp.pad(gain_grads.astype(low), ((0, 0), (0, 14), (0, 128 - chip_rows))).reshape(-1, 128)
-    lay_last = lay_q + ((shard, 16, 1, (0, 128), ((0, 128), 0, None)),)
-    q_sum = drawn_in("parts_q", slots, (whole_q, gain_grads), lay_last, shard + 16, width)
-
-    def rows_of(block, which):
-        return block[which * shard : (which + 1) * shard]
-
-    q_rows = jnp.concatenate([q_sum[:shard, :half_width], q_sum[:shard, half_width:]], axis=0)
-    in_rows = jnp.concatenate([in_sum[:chip_rows], in_sum[chip_rows : 2 * chip_rows]], axis=1)
-    gain_sum = jnp.pad(q_sum[shard : shard + 2, :128], ((0, shard - 2), (0, 0)))
-
-    def traded(block):
-        mine = by_core(rows_of(block, 0), rows_of(block, 1))
-        other = mate(by_core(rows_of(block, 1), rows_of(block, 0)))
-        return by_core(mine, other), by_core(other, mine)
-
-    kv_pair = jnp.stack(traded(kv_sum), axis=0).reshape(2, shard, groups, 2, HD)
-    q_pair = jnp.stack(traded(q_rows), axis=0).reshape(2, shard, groups, HD)
-    in_pair = jnp.stack(traded(in_rows), axis=0).reshape(2, shard, -1, down_rows)
-    grad_query = q_pair.transpose(1, 2, 0, 3).reshape(shard, -1)
-    grad_key = kv_pair[:, :, :, 0].transpose(1, 2, 0, 3).reshape(shard, -1)
-    grad_value = kv_pair[:, :, :, 1].transpose(1, 2, 0, 3).reshape(shard, -1)
-    grad_in = in_pair.transpose(1, 2, 0, 3).reshape(shard, -1)
-    back_swap = [(b, (b % 2) * 2 + b // 2) for b in range(blocks)]
-    grad_out = lax.ppermute(in_sum[2 * chip_rows :], "blk", back_swap)
-    gain_sum = gain_sum + mate(gain_sum)
-    gain_mine = by_core(gain_sum[:2, :shard], gain_sum[:2, shard : 2 * shard])
-
-    near_sums, far_sums = band_sums_of(band, sides)
+    gain_mine = first_sums[0][:, first_cols : first_cols + 2] + first_sums[1][:, first_cols : first_cols + 2]
+    first_sums = [block[:, :first_cols] for block in first_sums]
+    first_pair = [by_side(*first_sums), by_side(*first_sums[::-1])]
+    first_pair = [block.reshape(shard, groups, 3, HD) for block in first_pair]
+    grad_query, grad_key, grad_value = (
+        jnp.stack([block[:, :, which] for block in first_pair], axis=2).reshape(shard, -1) for which in range(3)
+    )
+
+    hidden_rows = jnp.concatenate([in_sum[:chip_rows], in_sum[chip_rows : 2 * chip_rows]], axis=1)
+    mine = by_core(hidden_rows[:shard], hidden_rows[shard:])
+    other = mate(by_core(hidden_rows[shard:], hidden_rows[:shard]))
+    in_pair = [block.reshape(shard, -1, down_rows) for block in (by_core(mine, other), by_core(other, mine))]
+    grad_in = jnp.stack(in_pair, axis=2).reshape(shard, -1)
+    grad_out = in_sum[2 * chip_rows :]
+
+    near_sums, far_sums = band_sums_of(after(band, pace), sides)
     offset_sums = jnp.dot(near_sums.reshape(-1), place_hot, precision=lax.Precision.HIGHEST)
     far_sums = jnp.sum(far_sums, axis=1)
     end_hot = lax.iota(jnp.int32, 2 * MAXREL + 1)
-    offset_sums = offset_sums + jnp.where(end_hot == 0, far_sums[0], 0.0) + jnp.where(end_hot == 2 * MAXREL, far_sums[1], 0.0)
+    offset_sums = offset_sums + jnp.where(end_hot == 0, far_sums[0], 0.0)
+    offset_sums = offset_sums + jnp.where(end_hot == 2 * MAXREL, far_sums[1], 0.0)
     rel_grad = jnp.sum(jnp.where(bucket_hot, offset_sums[:, None], 0.0), axis=0)
     rel_grad = jnp.pad(rel_grad[None, :], ((0, 7), (0, 128 - BUCKETS)))
-    from_mate, from_x, from_corner = mate(rel_grad), across_x(rel_grad), trade(rel_grad, "blk", 3)
-    rel_sum = jnp.where(core == side, rel_grad + from_x, from_mate + from_corner)[0]
+    rel_sum = (rel_grad + mate(rel_grad))[0]
     rel_mine = by_core(rel_sum[: BUCKETS // 2], rel_sum[BUCKETS // 2 : BUCKETS])
 
     return (
         layer_out,
         input_grad,
-        gain_mine[0],
+        gain_mine[:, 0],
         grad_query,
         grad_key,
         grad_value,
         grad_out,
         rel_mine,
-        gain_mine[1],
+        gain_mine[:, 1],
         grad_in,
         grad_down,
     )

time: 619 us -> 512 us (0.83)
  waiting for transfers between devices: 247 us -> 165 us
  starting transfers between devices: 132 us -> 98.3 us
  local copies, waits for them, and re-layouts: 48.7 us -> 33.5 us
  between operations: 2.72 us -> 16.4 us
  Pallas kernels: 96.8 us -> 107 us
    ppermute x74 -> x60, waiting for transfers between devices: 226 us -> 107 us  [trade(): return lax.ppermute(block, axis, [(i, i ^ bit) for i in range(size)])]
    all_to_all x6 -> x7, waiting for transfers between devices: 21 us -> 57.7 us  [exchanged(): lax.all_to_all(block, 'head', split_axis=0, concat_axis=0, tiled=True)]
    ppermute x74 -> x60, starting transfers between devices: 83.5 us -> 64.6 us  [trade(): return lax.ppermute(block, axis, [(i, i ^ bit) for i in range(size)])]
    all_to_all x6 -> x7, starting transfers between devices: 45.7 us -> 33.6 us  [exchanged(): lax.all_to_all(block, 'head', split_axis=0, concat_axis=0, tiled=True)]
    pallas_call x1 -> x3, Pallas kernels: 50.3 us -> 61.4 us  [the longest x2 56.4 us: attend_back(): pl.pallas_call(functools.partial(attend_back_kernel, chips, bool(sums)),...]
    unnamed x136 -> x164, local copies, waits for them, and re-layouts: 18.1 us -> 11.5 us
    dot_general x15 -> x17, matrix products: 43.8 us -> 39.9 us  [dot_on(): lax.dot_general(left, right, (((left_dim,), (right_dim,)), ((), ())), pre...]
    pallas_call x1 -> x2, Pallas kernels: 33.1 us -> 36 us  [attend(): pl.pallas_call(functools.partial(attend_kernel, chips), name='attend', ou...]
  transfers between devices with their start and end apart: 82 -> 68, of which waited for: 38 -> 31; matrix products, arithmetic and copies ran while one was open for 16% -> 15% of each run, Pallas kernels for 16% -> 20%
where the time goes in v2:
time: 512 us; the launch traced here: 502 us
  waiting for transfers between devices  165 us (32%)
  Pallas kernels  107 us (21%)
  starting transfers between devices  98.3 us (19%)
  matrix products  43.5 us (8%)
  other arithmetic  39.3 us (8%)
  local copies, waits for them, and re-layouts  33.5 us (7%)
  between operations  16.4 us (3%)
    ppermute x60, waiting for transfers between devices, trade(): return lax.ppermute(block, axis, [(i, i ^ bit) for i in range(size)])  107 us
    ppermute x60, starting transfers between devices, trade(): return lax.ppermute(block, axis, [(i, i ^ bit) for i in range(size)])  64.6 us
    all_to_all x7, waiting for transfers between devices, exchanged(): lax.all_to_all(block, 'head', split_axis=0, concat_axis=0, tiled=True)  57.7 us
    pallas_call x2, Pallas kernels, attend_back(): pl.pallas_call(functools.partial(attend_back_kernel, chips, bool(sums)),...  56.4 us
    dot_general x17, matrix products, dot_on(): lax.dot_general(left, right, (((left_dim,), (right_dim,)), ((), ())), pre...  39.9 us
    pallas_call x2, Pallas kernels, attend(): pl.pallas_call(functools.partial(attend_kernel, chips), name='attend', ou...  36 us
    all_to_all x7, starting transfers between devices, exchanged(): lax.all_to_all(block, 'head', split_axis=0, concat_axis=0, tiled=True)  33.6 us
    unnamed x164, local copies, waits for them, and re-layouts  11.5 us
  transfers between devices with their start and end apart: 68, of which 31 were waited for; matrix products, arithmetic and copies ran while one was open for 15% of the time, Pallas kernels for 20%

profile of v2, /device:TPU:0, one launch (start us, length us, event | category | flops | bytes accessed | tf_op | source)
XLA Modules:
  0.0 502.5 jit_solution(15752588307415353536)
XLA Ops:
  13.8 5.1 %collective-permute-start.11 = (bf16[32,1536]{1,0:T(8,128)(2,1)S(1)}, bf16[32,1536]{1,0:T(8,128)(2,1)S(1)}, u32[]{:S(2)}, u32[]{:S(2)}) collective-permute-start(bf16[32,1536]{1,0:T(8,128)(2,1)S(1)} %select_n.208), channel_id=1, source_target_pairs={{0,24},{4,28},{8,16},{12,20},{16,8},{20,12},{24,0},{28,4},{1,25},{... | collective-permute-start | bytes 294920 | tf_op jit(solution)/shard_map/ppermute | solution.py:703
  20.2 2.0 collective-permute-start.4
  25.8 7.1 %collective-permute-start.9 = (bf16[32,1536]{1,0:T(8,128)(2,1)S(1)}, bf16[32,1536]{1,0:T(8,128)(2,1)S(1)}, u32[]{:S(2)}, u32[]{:S(2)}) collective-permute-start(bf16[32,1536]{1,0:T(8,128)(2,1)S(1)} %select_n.208), channel_id=1, source_target_pairs={{0,8},{4,12},{8,0},{12,4},{16,24},{20,28},{24,16},{28,20},{1,9},{5... | collective-permute-start | bytes 294920 | tf_op jit(solution)/shard_map/ppermute | solution.py:703
  45.2 3.7 collective-permute-start.17
  49.6 3.5 collective-permute-done.17
  53.1 5.1 %collective-permute-done.16 = bf16[32,1536]{1,0:T(8,128)(2,1)S(1)} collective-permute-done((bf16[32,1536]{1,0:T(8,128)(2,1)S(1)}, bf16[32,1536]{1,0:T(8,128)(2,1)S(1)}, u32[]{:S(2)}, u32[]{:S(2)}) %collective-permute-start.16) | collective-permute-done | bytes 98336 | tf_op jit(solution)/shard_map/ppermute | solution.py:703
  61.6 7.1 %collective-permute-done.18 = bf16[128,1536]{1,0:T(8,128)(2,1)S(1)} collective-permute-done((bf16[128,1536]{1,0:T(8,128)(2,1)S(1)}, bf16[128,1536]{1,0:T(8,128)(2,1)S(1)}, u32[]{:S(2)}, u32[]{:S(2)}) %collective-permute-start.18) | collective-permute-done | bytes 393248 | tf_op jit(solution)/shard_map/ppermute | solution.py:703
  69.2 1.9 collective-permute-done.19.arrays_3_
  71.9 1.9 convolution_convert_fusion.3
  73.8 5.2 %all-to-all-start = ((bf16[8,192,256]{2,1,0:T(8,128)(2,1)}), bf16[8,192,256]{2,1,0:T(8,128)(2,1)S(1)}, u32[]{:S(2)}, u32[]{:S(2)}) async-start(bf16[8,192,256]{2,1,0:T(8,128)(2,1)} %bitcast.14), calls=%async_computation | async-start | bytes 1572864 | tf_op jit(solution)/shard_map/all_to_all | solution.py:972
  79.4 3.8 convolution_convert_fusion.2
  83.2 32.5 %all-to-all-done.refs_0_ = bf16[8,192,256]{2,1,0:T(8,128)(2,1)S(1)} async-done(((bf16[8,192,256]{2,1,0:T(8,128)(2,1)}), bf16[8,192,256]{2,1,0:T(8,128)(2,1)S(1)}, u32[]{:S(2)}, u32[]{:S(2)}) %all-to-all-start) | async-done | bytes 786464 | tf_op jit(solution)/shard_map/all_to_all | solution.py:972
  115.7 7.5 %all-to-all-start.1 = ((bf16[8,192,256]{2,1,0:T(8,128)(2,1)}), bf16[8,192,256]{2,1,0:T(8,128)(2,1)S(1)}, u32[]{:S(2)}, u32[]{:S(2)}) async-start(bf16[8,192,256]{2,1,0:T(8,128)(2,1)} %bitcast.17), calls=%async_computation.1 | async-start | bytes 1572864 | tf_op jit(solution)/shard_map/all_to_all | solution.py:972
  128.4 2.0 copy-done
  130.4 24.1 %attend.2 = (f32[8,64,256]{2,1,0:T(8,128)S(1)}, bf16[8,64,256]{2,1,0:T(8,128)(2,1)}, f32[2,1,2,512]{3,2,1,0:T(2,128)S(1)}) custom-call(s32[4]{0:T(128)S(1)} %xor_multiply_fusion.base_ref, s32[16]{0:T(128)S(1)} %reshape_squeeze.13.edge_ref, f32[2]{0:T(128)S(1)} %pad_maximum_fusion.28.far_ref, bf16[8,192,256]{2,1,0:T(8,128)(2,1)S(1)} %all-to-all-done.refs_0_, ...), custom_call_target="tpu_custom_call" | custom-call | flops 1 | bytes 1 | tf_op jit(solution)/shard_map/attend/pallas_call | solution.py:653
  155.9 5.9 %all-to-all-done.1.refs_0_ = bf16[8,192,256]{2,1,0:T(8,128)(2,1)S(1)} async-done(((bf16[8,192,256]{2,1,0:T(8,128)(2,1)}), bf16[8,192,256]{2,1,0:T(8,128)(2,1)S(1)}, u32[]{:S(2)}, u32[]{:S(2)}) %all-to-all-start.1) | async-done | bytes 786464 | tf_op jit(solution)/shard_map/all_to_all | solution.py:972
  161.9 3.4 all-to-all-start.2
  165.4 11.9 %attend.3 = (f32[8,64,256]{2,1,0:T(8,128)S(1)}, bf16[8,64,256]{2,1,0:T(8,128)(2,1)}, f32[2,1,2,512]{3,2,1,0:T(2,128)S(1)}) custom-call(s32[4]{0:T(128)S(1)} %xor_multiply_fusion.base_ref, s32[16]{0:T(128)S(1)} %reshape_squeeze.12.edge_ref, f32[2]{0:T(128)S(1)} %pad_maximum_fusion.28.far_ref, bf16[8,192,256]{2,1,0:T(8,128)(2,1)S(1)} %all-to-all-done.1.refs_0_, ...), custom_call_target="tpu_custom_call" | custom-call | flops 1 | bytes 1 | tf_op jit(solution)/shard_map/attend/pallas_call | solution.py:653
  178.1 5.8 %all-to-all-start.3 = ((bf16[8,64,256]{2,1,0:T(8,128)(2,1)}), bf16[8,64,256]{2,1,0:T(8,128)(2,1)S(1)}, u32[]{:S(2)}, u32[]{:S(2)}) async-start(bf16[8,64,256]{2,1,0:T(8,128)(2,1)} %get-tuple-element.97), calls=%async_computation.3 | async-start | bytes 524288 | tf_op jit(solution)/shard_map/all_to_all | solution.py:972
  185.5 7.7 %all-to-all-done.3 = bf16[8,64,256]{2,1,0:T(8,128)(2,1)S(1)} async-done(((bf16[8,64,256]{2,1,0:T(8,128)(2,1)}), bf16[8,64,256]{2,1,0:T(8,128)(2,1)S(1)}, u32[]{:S(2)}, u32[]{:S(2)}) %all-to-all-start.3) | async-done | bytes 262176 | tf_op jit(solution)/shard_map/all_to_all | solution.py:972
  194.8 3.4 collective-permute-done.23
  198.5 5.0 own_halves.1
  206.5 2.4 fusion.39
  208.9 5.5 %multiply_convert_fusion = bf16[512,2048]{1,0:T(8,128)(2,1)S(1)} fusion(f32[512,2048]{1,0:T(8,128)S(1)} %fusion.39, bf16[2048,1024]{1,0:T(8,128)(2,1)S(1)} %get-tuple-element.100, bf16[256,1024]{1,0:T(8,128)(2,1)S(1)} %collective-permute-done.26, bf16[256,1024]{1,0:T(8,128)(2,1)S(1)} %bitcast.185), kind=kOutput, calls=%fused_computation.1 | convolution fusion | flops 2168455168 | bytes 11534336 | tf_op jit(solution)/shard_map/dot_general | solution.py:929
  214.4 2.4 fusion.72
  217.2 2.7 fusion.40
  220.4 5.1 %convolution_convert_fusion.1.arrays_0_ = bf16[2048,1024]{1,0:T(8,128)(2,1)S(1)} fusion(bf16[256,1024]{1,0:T(8,128)(2,1)S(1)} %collective-permute-done.26, bf16[256,1024]{1,0:T(8,128)(2,1)S(1)} %bitcast.186, f32[512,2048]{1,0:T(8,128)} %copy-done.74), kind=kOutput, calls=%fused_computation.10 | convolution fusion | flops 2161115136 | bytes 9437184 | tf_op jit(solution)/shard_map/dot_general | solution.py:929
  231.2 9.2 %collective-permute-done.28 = bf16[256,1024]{1,0:T(8,128)(2,1)S(1)} collective-permute-done((bf16[256,1024]{1,0:T(8,128)(2,1)S(1)}, bf16[256,1024]{1,0:T(8,128)(2,1)S(1)}, u32[]{:S(2)}, u32[]{:S(2)}) %collective-permute-start.28) | collective-permute-done | bytes 524320 | tf_op jit(solution)/shard_map/ppermute | solution.py:703
  251.8 3.7 all-to-all-start.4
  257.2 2.4 convolution_convert_fusion.arrays_0_
  259.6 1.9 fusion.2
  261.5 2.0 parts_in.1
  264.5 2.0 collective-permute-start.34
  267.8 10.1 %all-to-all-done.4 = bf16[8,64,512]{2,1,0:T(8,128)(2,1)S(1)} async-done(((bf16[8,64,512]{2,1,0:T(8,128)(2,1)}), bf16[8,64,512]{2,1,0:T(8,128)(2,1)S(1)}, u32[]{:S(2)}, u32[]{:S(2)}) %all-to-all-start.4) | async-done | bytes 524320 | tf_op jit(solution)/shard_map/all_to_all | solution.py:972
  278.8 2.5 fusion.44
  283.0 1.9 collective-permute-start.37
  285.0 35.5 %attend_back.2 = (bf16[8,192,256]{2,1,0:T(8,128)(2,1)}, bf16[8,128,256]{2,1,0:T(8,128)(2,1)}, f32[2048,512]{1,0:T(8,128)}, f32[8,512]{1,0:T(8,128)}) custom-call(s32[4]{0:T(128)} %copy-done.20, s32[16]{0:T(128)} %copy-done.22, f32[2]{0:T(128)} %copy-done.17, bf16[8,64,256]{2,1,0:T(8,128)(2,1)} %get-tuple-element.112.g_ref, f32[8,64,256]{2,1,0:T(8,128)} %copy-done.11, ...), custom_call_target="tpu_custom_call" | custom-call | flops 1 | bytes 1 | tf_op jit(solution)/shard_map/attend_back/pallas_call | solution.py:679
  327.3 3.6 all-to-all-start.5
  331.6 20.9 %attend_back.3 = (bf16[8,192,256]{2,1,0:T(8,128)(2,1)}, bf16[8,128,256]{2,1,0:T(8,128)(2,1)}, f32[2048,512]{1,0:T(8,128)}, f32[8,512]{1,0:T(8,128)}) custom-call(s32[4]{0:T(128)} %copy-done.20, s32[16]{0:T(128)} %copy-done.21, f32[2]{0:T(128)} %copy-done.17, bf16[8,64,256]{2,1,0:T(8,128)(2,1)} %get-tuple-element.130.g_ref, f32[8,64,256]{2,1,0:T(8,128)} %copy-done.10, ...), custom_call_target="tpu_custom_call" | custom-call | flops 1 | bytes 1 | tf_op jit(solution)/shard_map/attend_back/pallas_call | solution.py:679
  352.6 9.9 %collective-permute-done.41 = bf16[640,1024]{1,0:T(8,128)(2,1)} collective-permute-done((bf16[640,1024]{1,0:T(8,128)(2,1)}, bf16[640,1024]{1,0:T(8,128)(2,1)}, u32[]{:S(2)}, u32[]{:S(2)}) %collective-permute-start.41) | collective-permute-done | bytes 1310752 | tf_op jit(solution)/shard_map/ppermute | solution.py:703
  364.0 3.0 fusion.13
  368.2 4.4 all-to-all-start.6
  372.6 3.2 fusion.41
  375.9 1.9 collective-permute-start.55
  377.8 2.4 collective-permute-start.57
  380.2 2.0 fusion.73
  382.2 12.7 %collective-permute-done.55 = bf16[160,1024]{1,0:T(8,128)(2,1)S(1)} collective-permute-done((bf16[160,1024]{1,0:T(8,128)(2,1)S(1)}, bf16[160,1024]{1,0:T(8,128)(2,1)S(1)}, u32[]{:S(2)}, u32[]{:S(2)}) %collective-permute-start.55) | collective-permute-done | bytes 327712 | tf_op jit(solution)/shard_map/ppermute | solution.py:703
  395.0 9.8 %collective-permute-done.57 = bf16[160,1024]{1,0:T(8,128)(2,1)S(1)} collective-permute-done((bf16[160,1024]{1,0:T(8,128)(2,1)S(1)}, bf16[160,1024]{1,0:T(8,128)(2,1)S(1)}, u32[]{:S(2)}, u32[]{:S(2)}) %collective-permute-start.57) | collective-permute-done | bytes 327712 | tf_op jit(solution)/shard_map/ppermute | solution.py:703
  404.7 16.5 %collective-permute-done.56 = bf16[160,1024]{1,0:T(8,128)(2,1)S(1)} collective-permute-done((bf16[160,1024]{1,0:T(8,128)(2,1)S(1)}, bf16[160,1024]{1,0:T(8,128)(2,1)S(1)}, u32[]{:S(2)}, u32[]{:S(2)}) %collective-permute-start.56) | collective-permute-done | bytes 327712 | tf_op jit(solution)/shard_map/ppermute | solution.py:703
  423.0 2.2 fusion.74
  425.3 2.6 fusion.75
  438.2 2.3 reshape.336
  441.5 1.9 slice.517
  444.3 2.2 copy-done.3
  446.5 2.4 band_sums.1
  448.9 2.2 fusion.7
  459.5 8.2 %collective-permute-done.50 = bf16[128,1664]{1,0:T(8,128)(2,1)S(1)} collective-permute-done((bf16[128,1664]{1,0:T(8,128)(2,1)S(1)}, bf16[128,1664]{1,0:T(8,128)(2,1)S(1)}, u32[]{:S(2)}, u32[]{:S(2)}) %collective-permute-start.50) | collective-permute-done | bytes 426016 | tf_op jit(solution)/shard_map/ppermute | solution.py:703
  469.1 1.8 collective-permute-start.53
  470.8 1.7 collective-permute-start.52
  472.5 3.4 collective-permute-done.46
  477.3 1.8 collective-permute-start.49
  480.5 1.7 collective-permute-start.48
  482.9 1.7 collective-permute-done.47
  484.7 4.8 collective-permute-done.48
  (430 shorter events, 110.1 us)
Async XLA Ops:
  7.2 191.3 %all-gather.3.cloned.1.call-start = ((), (), s32[]{:S(2)}) async-start(), calls=%async_computation.7 | async-start | bytes 19464192 | tf_op jit(solution)/shard_map/all_gather | solution.py:1010
  13.8 30.2 %collective-permute-start.11 = (bf16[32,1536]{1,0:T(8,128)(2,1)S(1)}, bf16[32,1536]{1,0:T(8,128)(2,1)S(1)}, u32[]{:S(2)}, u32[]{:S(2)}) collective-permute-start(bf16[32,1536]{1,0:T(8,128)(2,1)S(1)} %select_n.208), channel_id=1, source_target_pairs={{0,24},{4,28},{8,16},{12,20},{16,8},{20,12},{24,0},{28,4},{1,25},{... | collective-permute-start | bytes 294920 | tf_op jit(solution)/shard_map/ppermute | solution.py:703
  18.9 25.1 %collective-permute-start.10 = (bf16[32,1536]{1,0:T(8,128)(2,1)S(1)}, bf16[32,1536]{1,0:T(8,128)(2,1)S(1)}, u32[]{:S(2)}, u32[]{:S(2)}) collective-permute-start(bf16[32,1536]{1,0:T(8,128)(2,1)S(1)} %select_n.208), channel_id=1, source_target_pairs={{0,16},{4,20},{8,24},{12,28},{16,0},{20,4},{24,8},{28,12},{1,17},{... | collective-permute-start | bytes 294920 | tf_op jit(solution)/shard_map/ppermute | solution.py:703
  20.2 5.6 %collective-permute-start.4 = (bf16[16,128]{1,0:T(8,128)(2,1)S(1)}, bf16[16,128]{1,0:T(8,128)(2,1)S(1)}, u32[]{:S(2)}, u32[]{:S(2)}) collective-permute-start(bf16[16,128]{1,0:T(8,128)(2,1)S(1)} %fusion.32), channel_id=1, source_target_pairs={{0,24},{4,28},{8,16},{12,20},{16,8},{20,12},{24,0},{28,4},{1,25},{... | collective-permute-start | bytes 12296 | tf_op jit(solution)/shard_map/ppermute | solution.py:703
  22.2 10.7 %collective-permute-start.3 = (bf16[16,128]{1,0:T(8,128)(2,1)S(1)}, bf16[16,128]{1,0:T(8,128)(2,1)S(1)}, u32[]{:S(2)}, u32[]{:S(2)}) collective-permute-start(bf16[16,128]{1,0:T(8,128)(2,1)S(1)} %fusion.32), channel_id=1, source_target_pairs={{0,16},{4,20},{8,24},{12,28},{16,0},{20,4},{24,8},{28,12},{1,17},{... | collective-permute-start | bytes 12296 | tf_op jit(solution)/shard_map/ppermute | solution.py:703
  23.3 9.6 %collective-permute-start.2 = (bf16[16,128]{1,0:T(8,128)(2,1)S(1)}, bf16[16,128]{1,0:T(8,128)(2,1)S(1)}, u32[]{:S(2)}, u32[]{:S(2)}) collective-permute-start(bf16[16,128]{1,0:T(8,128)(2,1)S(1)} %fusion.32), channel_id=1, source_target_pairs={{0,8},{4,12},{8,0},{12,4},{16,24},{20,28},{24,16},{28,20},{1,9},{5... | collective-permute-start | bytes 12296 | tf_op jit(solution)/shard_map/ppermute | solution.py:703
  25.8 18.2 %collective-permute-start.9 = (bf16[32,1536]{1,0:T(8,128)(2,1)S(1)}, bf16[32,1536]{1,0:T(8,128)(2,1)S(1)}, u32[]{:S(2)}, u32[]{:S(2)}) collective-permute-start(bf16[32,1536]{1,0:T(8,128)(2,1)S(1)} %select_n.208), channel_id=1, source_target_pairs={{0,8},{4,12},{8,0},{12,4},{16,24},{20,28},{24,16},{28,20},{1,9},{5... | collective-permute-start | bytes 294920 | tf_op jit(solution)/shard_map/ppermute | solution.py:703
  32.9 3.8 collective-permute-start.6
  34.1 3.9 collective-permute-start.5
  36.7 3.8 collective-permute-start.8
  38.0 3.8 collective-permute-start.7
  40.5 4.6 collective-permute-start.14
  41.8 19.0 %collective-permute-start = (bf16[256,1024]{1,0:T(8,128)(2,1)S(1)}, bf16[256,1024]{1,0:T(8,128)(2,1)S(1)}, u32[]{:S(2)}, u32[]{:S(2)}) collective-permute-start(bf16[256,1024]{1,0:T(8,128)(2,1)S(1)} %bitcast.165), channel_id=1, source_target_pairs={{0,2},{1,3},{2,0},{3,1},{4,6},{5,7},{6,4},{7,5},{8,10},{9,11},{10,... | collective-permute-start | bytes 1572872 | tf_op jit(solution)/shard_map/ppermute | solution.py:703
  44.0 16.7 %collective-permute-start.12 = (bf16[128,1536]{1,0:T(8,128)(2,1)S(1)}, bf16[128,1536]{1,0:T(8,128)(2,1)S(1)}, u32[]{:S(2)}, u32[]{:S(2)}) collective-permute-start(bf16[128,1536]{1,0:T(8,128)(2,1)S(1)} %pad_maximum_fusion.17), channel_id=1, source_target_pairs={{0,4},{4,0},{8,12},{12,8},{16,20},{20,16},{24,28},{28,24},{1,5},{5... | collective-permute-start | bytes 1179656 | tf_op jit(solution)/shard_map/ppermute | solution.py:703
  45.2 7.9 %collective-permute-start.17 = (bf16[32,1536]{1,0:T(8,128)(2,1)S(1)}, bf16[32,1536]{1,0:T(8,128)(2,1)S(1)}, u32[]{:S(2)}, u32[]{:S(2)}) collective-permute-start(bf16[32,1536]{1,0:T(8,128)(2,1)S(1)} %collective-permute-done.14), channel_id=1, source_target_pairs={{0,24},{4,28},{8,16},{12,20},{16,8},{20,12},{24,0},{28,4},{1,25},{... | collective-permute-start | bytes 294920 | tf_op jit(solution)/shard_map/ppermute | solution.py:703
  48.9 9.3 %collective-permute-start.16 = (bf16[32,1536]{1,0:T(8,128)(2,1)S(1)}, bf16[32,1536]{1,0:T(8,128)(2,1)S(1)}, u32[]{:S(2)}, u32[]{:S(2)}) collective-permute-start(bf16[32,1536]{1,0:T(8,128)(2,1)S(1)} %collective-permute-done.14), channel_id=1, source_target_pairs={{0,16},{4,20},{8,24},{12,28},{16,0},{20,4},{24,8},{28,12},{1,17},{... | collective-permute-start | bytes 294920 | tf_op jit(solution)/shard_map/ppermute | solution.py:703
  48.9 10.5 %collective-permute-start.15 = (bf16[32,1536]{1,0:T(8,128)(2,1)S(1)}, bf16[32,1536]{1,0:T(8,128)(2,1)S(1)}, u32[]{:S(2)}, u32[]{:S(2)}) collective-permute-start(bf16[32,1536]{1,0:T(8,128)(2,1)S(1)} %collective-permute-done.14), channel_id=1, source_target_pairs={{0,8},{4,12},{8,0},{12,4},{16,24},{20,28},{24,16},{28,20},{1,9},{5... | collective-permute-start | bytes 294920 | tf_op jit(solution)/shard_map/ppermute | solution.py:703
  59.4 9.3 %collective-permute-start.18 = (bf16[128,1536]{1,0:T(8,128)(2,1)S(1)}, bf16[128,1536]{1,0:T(8,128)(2,1)S(1)}, u32[]{:S(2)}, u32[]{:S(2)}) collective-permute-start(bf16[128,1536]{1,0:T(8,128)(2,1)S(1)} %pad_maximum_fusion.18), channel_id=1, source_target_pairs={{0,4},{4,0},{8,12},{12,8},{16,20},{20,16},{24,28},{28,24},{1,5},{5... | collective-permute-start | bytes 1179656 | tf_op jit(solution)/shard_map/ppermute | solution.py:703
  60.7 8.5 %collective-permute-start.13 = (bf16[256,1536]{1,0:T(8,128)(2,1)S(1)}, bf16[256,1536]{1,0:T(8,128)(2,1)S(1)}, u32[]{:S(2)}, u32[]{:S(2)}) collective-permute-start(bf16[256,1536]{1,0:T(8,128)(2,1)S(1)} %constant_dynamic-update-slice_fusion.4.arrays_0_), channel_id=1, source_target_pairs={{0,1},{1,0},{2,3},{3,2},{4,5},{5,4},{6,7},{7,6},{8,9},{9,8},{10,11... | collective-permute-start | bytes 2359304 | tf_op jit(solution)/shard_map/ppermute | solution.py:703
  73.8 41.9 %all-to-all-start = ((bf16[8,192,256]{2,1,0:T(8,128)(2,1)}), bf16[8,192,256]{2,1,0:T(8,128)(2,1)S(1)}, u32[]{:S(2)}, u32[]{:S(2)}) async-start(bf16[8,192,256]{2,1,0:T(8,128)(2,1)} %bitcast.14), calls=%async_computation | async-start | bytes 1572864 | tf_op jit(solution)/shard_map/all_to_all | solution.py:972
  115.7 46.1 %all-to-all-start.1 = ((bf16[8,192,256]{2,1,0:T(8,128)(2,1)}), bf16[8,192,256]{2,1,0:T(8,128)(2,1)S(1)}, u32[]{:S(2)}, u32[]{:S(2)}) async-start(bf16[8,192,256]{2,1,0:T(8,128)(2,1)} %bitcast.17), calls=%async_computation.1 | async-start | bytes 1572864 | tf_op jit(solution)/shard_map/all_to_all | solution.py:972
  123.3 7.1 %collective-permute-start.20 = (bf16[8,192,256]{2,1,0:T(8,128)(2,1)S(1)}, bf16[8,192,256]{2,1,0:T(8,128)(2,1)S(1)}, u32[]{:S(2)}, u32[]{:S(2)}) collective-permute-start(bf16[8,192,256]{2,1,0:T(8,128)(2,1)S(1)} %all-to-all-done.refs_0_), channel_id=1, source_target_pairs={{0,1},{1,0},{2,3},{3,2},{4,5},{5,4},{6,7},{7,6},{8,9},{9,8},{10,11... | collective-permute-start | bytes 2359304 | tf_op jit(solution)/shard_map/ppermute | solution.py:703
  161.8 3.6 collective-permute-start.21
  161.9 16.3 %all-to-all-start.2 = ((bf16[8,64,256]{2,1,0:T(8,128)(2,1)}), bf16[8,64,256]{2,1,0:T(8,128)(2,1)S(1)}, u32[]{:S(2)}, u32[]{:S(2)}) async-start(bf16[8,64,256]{2,1,0:T(8,128)(2,1)} %get-tuple-element.95), calls=%async_computation.2 | async-start | bytes 524288 | tf_op jit(solution)/shard_map/all_to_all | solution.py:972
  178.1 15.1 %all-to-all-start.3 = ((bf16[8,64,256]{2,1,0:T(8,128)(2,1)}), bf16[8,64,256]{2,1,0:T(8,128)(2,1)S(1)}, u32[]{:S(2)}, u32[]{:S(2)}) async-start(bf16[8,64,256]{2,1,0:T(8,128)(2,1)} %get-tuple-element.97), calls=%async_computation.3 | async-start | bytes 524288 | tf_op jit(solution)/shard_map/all_to_all | solution.py:972
  184.0 10.8 %collective-permute-start.22 = (bf16[512,128]{1,0:T(8,128)(2,1)S(1)}, bf16[512,128]{1,0:T(8,128)(2,1)S(1)}, u32[]{:S(2)}, u32[]{:S(2)}) collective-permute-start(bf16[512,128]{1,0:T(8,128)(2,1)S(1)} %get-tuple-element.291), channel_id=1, source_target_pairs={{0,2},{1,3},{2,0},{3,1},{4,6},{5,7},{6,4},{7,5},{8,10},{9,11},{10,... | collective-permute-start | bytes 393224 | tf_op jit(solution)/shard_map/ppermute | solution.py:703
  193.2 5.0 %collective-permute-start.23 = (bf16[512,128]{1,0:T(8,128)(2,1)S(1)}, bf16[512,128]{1,0:T(8,128)(2,1)S(1)}, u32[]{:S(2)}, u32[]{:S(2)}) collective-permute-start(bf16[512,128]{1,0:T(8,128)(2,1)S(1)} %get-tuple-element.293), channel_id=1, source_target_pairs={{0,2},{1,3},{2,0},{3,1},{4,6},{5,7},{6,4},{7,5},{8,10},{9,11},{10,... | collective-permute-start | bytes 393224 | tf_op jit(solution)/shard_map/ppermute | solution.py:703
  204.6 4.3 collective-permute-start.26
  217.0 12.3 %collective-permute-start.27 = (f32[256,1024]{1,0:T(8,128)S(1)}, f32[256,1024]{1,0:T(8,128)S(1)}, u32[]{:S(2)}, u32[]{:S(2)}) collective-permute-start(f32[256,1024]{1,0:T(8,128)S(1)} %slice.501), channel_id=1, source_target_pairs={{0,1},{1,0},{2,3},{3,2},{4,5},{5,4},{6,7},{7,6},{8,9},{9,8},{10,11... | collective-permute-start | bytes 3145736 | tf_op jit(solution)/shard_map/ppermute | solution.py:703
  219.9 9.6 %collective-permute-start.25 = (f32[256,1024]{1,0:T(8,128)S(1)}, f32[256,1024]{1,0:T(8,128)S(1)}, u32[]{:S(2)}, u32[]{:S(2)}) collective-permute-start(f32[256,1024]{1,0:T(8,128)S(1)} %slice.499), channel_id=1, source_target_pairs={{0,1},{1,0},{2,3},{3,2},{4,5},{5,4},{6,7},{7,6},{8,9},{9,8},{10,11... | collective-permute-start | bytes 3145736 | tf_op jit(solution)/shard_map/ppermute | solution.py:703
  226.3 14.0 %collective-permute-start.28 = (bf16[256,1024]{1,0:T(8,128)(2,1)S(1)}, bf16[256,1024]{1,0:T(8,128)(2,1)S(1)}, u32[]{:S(2)}, u32[]{:S(2)}) collective-permute-start(bf16[256,1024]{1,0:T(8,128)(2,1)S(1)} %get-tuple-element.104), channel_id=1, source_target_pairs={{0,4},{4,0},{8,12},{12,8},{16,20},{20,16},{24,28},{28,24},{1,5},{5... | collective-permute-start | bytes 1572872 | tf_op jit(solution)/shard_map/ppermute | solution.py:703
  227.8 13.7 %collective-permute-start.29 = (bf16[256,1024]{1,0:T(8,128)(2,1)S(1)}, bf16[256,1024]{1,0:T(8,128)(2,1)S(1)}, u32[]{:S(2)}, u32[]{:S(2)}) collective-permute-start(bf16[256,1024]{1,0:T(8,128)(2,1)S(1)} %get-tuple-element.105), channel_id=1, source_target_pairs={{0,2},{1,3},{2,0},{3,1},{4,6},{5,7},{6,4},{7,5},{8,10},{9,11},{10,... | collective-permute-start | bytes 1572872 | tf_op jit(solution)/shard_map/ppermute | solution.py:703
  243.5 7.3 %collective-permute-start.30 = (bf16[8,64,256]{2,1,0:T(8,128)(2,1)S(1)}, bf16[8,64,256]{2,1,0:T(8,128)(2,1)S(1)}, u32[]{:S(2)}, u32[]{:S(2)}) collective-permute-start(bf16[8,64,256]{2,1,0:T(8,128)(2,1)S(1)} %get-tuple-element.275), channel_id=1, source_target_pairs={{0,2},{1,3},{2,0},{3,1},{4,6},{5,7},{6,4},{7,5},{8,10},{9,11},{10,... | collective-permute-start | bytes 786440 | tf_op jit(solution)/shard_map/ppermute | solution.py:703
  246.0 32.8 %collective-permute-start.32 = (bf16[512,1024]{1,0:T(8,128)(2,1)}, bf16[512,1024]{1,0:T(8,128)(2,1)}, u32[]{:S(2)}, u32[]{:S(2)}) collective-permute-start(bf16[512,1024]{1,0:T(8,128)(2,1)} %pad_maximum_fusion.7), channel_id=1, source_target_pairs={{0,4},{4,0},{8,12},{12,8},{16,20},{20,16},{24,28},{28,24},{1,5},{5... | collective-permute-start | bytes 3145736 | tf_op jit(solution)/shard_map/ppermute | solution.py:703
  247.8 11.8 %collective-permute-start.33 = (bf16[16,32,1024]{2,1,0:T(8,128)(2,1)}, bf16[16,32,1024]{2,1,0:T(8,128)(2,1)}, u32[]{:S(2)}, u32[]{:S(2)}) collective-permute-start(bf16[16,32,1024]{2,1,0:T(8,128)(2,1)} %select_bitcast_fusion), channel_id=1, source_target_pairs={{0,1},{1,0},{2,3},{3,2},{4,5},{5,4},{6,7},{7,6},{8,9},{9,8},{10,11... | collective-permute-start | bytes 3145736 | tf_op jit(solution)/shard_map/ppermute | solution.py:703
  248.9 29.9 %collective-permute-start.31 = (bf16[512,1024]{1,0:T(8,128)(2,1)}, bf16[512,1024]{1,0:T(8,128)(2,1)}, u32[]{:S(2)}, u32[]{:S(2)}) collective-permute-start(bf16[512,1024]{1,0:T(8,128)(2,1)} %pad_maximum_fusion.6), channel_id=1, source_target_pairs={{0,2},{1,3},{2,0},{3,1},{4,6},{5,7},{6,4},{7,5},{8,10},{9,11},{10,... | collective-permute-start | bytes 3145736 | tf_op jit(solution)/shard_map/ppermute | solution.py:703
  251.8 26.2 %all-to-all-start.4 = ((bf16[8,64,512]{2,1,0:T(8,128)(2,1)}), bf16[8,64,512]{2,1,0:T(8,128)(2,1)S(1)}, u32[]{:S(2)}, u32[]{:S(2)}) async-start(bf16[8,64,512]{2,1,0:T(8,128)(2,1)} %pad_maximum_fusion.14), calls=%async_computation.4 | async-start | bytes 1048576 | tf_op jit(solution)/shard_map/all_to_all | solution.py:972
  264.5 56.9 %collective-permute-start.34 = (bf16[320,1024]{1,0:T(8,128)(2,1)}, bf16[320,1024]{1,0:T(8,128)(2,1)}, u32[]{:S(2)}, u32[]{:S(2)}) collective-permute-start(bf16[320,1024]{1,0:T(8,128)(2,1)} %get-tuple-element.123), channel_id=1, source_target_pairs={{0,4},{4,0},{8,12},{12,8},{16,20},{20,16},{24,28},{28,24},{1,5},{5... | collective-permute-start | bytes 1966088 | tf_op jit(solution)/shard_map/ppermute | solution.py:703
  266.5 55.0 %collective-permute-start.35 = (bf16[320,1024]{1,0:T(8,128)(2,1)}, bf16[320,1024]{1,0:T(8,128)(2,1)}, u32[]{:S(2)}, u32[]{:S(2)}) collective-permute-start(bf16[320,1024]{1,0:T(8,128)(2,1)} %get-tuple-element.124), channel_id=1, source_target_pairs={{0,2},{1,3},{2,0},{3,1},{4,6},{5,7},{6,4},{7,5},{8,10},{9,11},{10,... | collective-permute-start | bytes 1966088 | tf_op jit(solution)/shard_map/ppermute | solution.py:703
  281.4 39.1 %collective-permute-start.36 = (bf16[128,1024]{1,0:T(8,128)(2,1)S(1)}, bf16[128,1024]{1,0:T(8,128)(2,1)S(1)}, u32[]{:S(2)}, u32[]{:S(2)}) collective-permute-start(bf16[128,1024]{1,0:T(8,128)(2,1)S(1)} %get-tuple-element.254), channel_id=1, source_target_pairs={{0,8},{4,12},{8,0},{12,4},{16,24},{20,28},{24,16},{28,20},{1,9},{5... | collective-permute-start | bytes 786440 | tf_op jit(solution)/shard_map/ppermute | solution.py:703
  281.6 38.9 %collective-permute-start.38 = (bf16[128,1024]{1,0:T(8,128)(2,1)S(1)}, bf16[128,1024]{1,0:T(8,128)(2,1)S(1)}, u32[]{:S(2)}, u32[]{:S(2)}) collective-permute-start(bf16[128,1024]{1,0:T(8,128)(2,1)S(1)} %get-tuple-element.255), channel_id=1, source_target_pairs={{0,24},{4,28},{8,16},{12,20},{16,8},{20,12},{24,0},{28,4},{1,25},{... | collective-permute-start | bytes 786440 | tf_op jit(solution)/shard_map/ppermute | solution.py:703
  283.0 37.4 %collective-permute-start.37 = (bf16[128,1024]{1,0:T(8,128)(2,1)S(1)}, bf16[128,1024]{1,0:T(8,128)(2,1)S(1)}, u32[]{:S(2)}, u32[]{:S(2)}) collective-permute-start(bf16[128,1024]{1,0:T(8,128)(2,1)S(1)} %get-tuple-element.256), channel_id=1, source_target_pairs={{0,16},{4,20},{8,24},{12,28},{16,0},{20,4},{24,8},{28,12},{1,17},{... | collective-permute-start | bytes 786440 | tf_op jit(solution)/shard_map/ppermute | solution.py:703
  321.4 4.8 collective-permute-start.39
  324.2 38.2 %collective-permute-start.41 = (bf16[640,1024]{1,0:T(8,128)(2,1)}, bf16[640,1024]{1,0:T(8,128)(2,1)}, u32[]{:S(2)}, u32[]{:S(2)}) collective-permute-start(bf16[640,1024]{1,0:T(8,128)(2,1)} %pad_maximum_fusion.3), channel_id=1, source_target_pairs={{0,4},{4,0},{8,12},{12,8},{16,20},{20,16},{24,28},{28,24},{1,5},{5... | collective-permute-start | bytes 3932168 | tf_op jit(solution)/shard_map/ppermute | solution.py:703
  327.3 36.7 %all-to-all-start.5 = ((bf16[8,192,256]{2,1,0:T(8,128)(2,1)}), bf16[8,192,256]{2,1,0:T(8,128)(2,1)S(1)}, u32[]{:S(2)}, u32[]{:S(2)}) async-start(bf16[8,192,256]{2,1,0:T(8,128)(2,1)} %pad_maximum_fusion.8), calls=%async_computation.5 | async-start | bytes 1572864 | tf_op jit(solution)/shard_map/all_to_all | solution.py:972
  331.0 31.4 %collective-permute-start.40 = (bf16[640,1024]{1,0:T(8,128)(2,1)S(1)}, bf16[640,1024]{1,0:T(8,128)(2,1)}, u32[]{:S(2)}, u32[]{:S(2)}) collective-permute-start(bf16[640,1024]{1,0:T(8,128)(2,1)S(1)} %pad_maximum_fusion.2), channel_id=1, source_target_pairs={{0,2},{1,3},{2,0},{3,1},{4,6},{5,7},{6,4},{7,5},{8,10},{9,11},{10,... | collective-permute-start | bytes 3932168 | tf_op jit(solution)/shard_map/ppermute | solution.py:703
  364.0 3.1 collective-permute-start.42
  368.2 54.8 %all-to-all-start.6 = ((bf16[8,192,256]{2,1,0:T(8,128)(2,1)}), bf16[8,192,256]{2,1,0:T(8,128)(2,1)}, u32[]{:S(2)}, u32[]{:S(2)}) async-start(bf16[8,192,256]{2,1,0:T(8,128)(2,1)} %pad_maximum_fusion.9), calls=%async_computation.6 | async-start | bytes 1572864 | tf_op jit(solution)/shard_map/all_to_all | solution.py:972
  375.9 19.1 %collective-permute-start.55 = (bf16[160,1024]{1,0:T(8,128)(2,1)S(1)}, bf16[160,1024]{1,0:T(8,128)(2,1)S(1)}, u32[]{:S(2)}, u32[]{:S(2)}) collective-permute-start(bf16[160,1024]{1,0:T(8,128)(2,1)S(1)} %get-tuple-element.251), channel_id=1, source_target_pairs={{0,8},{4,12},{8,0},{12,4},{16,24},{20,28},{24,16},{28,20},{1,9},{5... | collective-permute-start | bytes 983048 | tf_op jit(solution)/shard_map/ppermute | solution.py:703
  377.8 26.9 %collective-permute-start.57 = (bf16[160,1024]{1,0:T(8,128)(2,1)S(1)}, bf16[160,1024]{1,0:T(8,128)(2,1)S(1)}, u32[]{:S(2)}, u32[]{:S(2)}) collective-permute-start(bf16[160,1024]{1,0:T(8,128)(2,1)S(1)} %get-tuple-element.252), channel_id=1, source_target_pairs={{0,24},{4,28},{8,16},{12,20},{16,8},{20,12},{24,0},{28,4},{1,25},{... | collective-permute-start | bytes 983048 | tf_op jit(solution)/shard_map/ppermute | solution.py:703
  380.2 41.0 %collective-permute-start.56 = (bf16[160,1024]{1,0:T(8,128)(2,1)S(1)}, bf16[160,1024]{1,0:T(8,128)(2,1)S(1)}, u32[]{:S(2)}, u32[]{:S(2)}) collective-permute-start(bf16[160,1024]{1,0:T(8,128)(2,1)S(1)} %get-tuple-element.253), channel_id=1, source_target_pairs={{0,16},{4,20},{8,24},{12,28},{16,0},{20,4},{24,8},{28,12},{1,17},{... | collective-permute-start | bytes 983048 | tf_op jit(solution)/shard_map/ppermute | solution.py:703
  433.8 10.5 %collective-permute-start.43 = (bf16[256,1664]{1,0:T(8,128)(2,1)}, bf16[256,1664]{1,0:T(8,128)(2,1)}, u32[]{:S(2)}, u32[]{:S(2)}) collective-permute-start(bf16[256,1664]{1,0:T(8,128)(2,1)} %get-tuple-element.148), channel_id=1, source_target_pairs={{0,1},{1,0},{2,3},{3,2},{4,5},{5,4},{6,7},{7,6},{8,9},{9,8},{10,11... | collective-permute-start | bytes 2555912 | tf_op jit(solution)/shard_map/ppermute | solution.py:703
  443.4 13.6 %collective-permute-start.45 = (bf16[256,1664]{1,0:T(8,128)(2,1)S(1)}, bf16[256,1664]{1,0:T(8,128)(2,1)}, u32[]{:S(2)}, u32[]{:S(2)}) collective-permute-start(bf16[256,1664]{1,0:T(8,128)(2,1)S(1)} %get-tuple-element.151), channel_id=1, source_target_pairs={{0,1},{1,0},{2,3},{3,2},{4,5},{5,4},{6,7},{7,6},{8,9},{9,8},{10,11... | collective-permute-start | bytes 2555912 | tf_op jit(solution)/shard_map/ppermute | solution.py:703
  453.3 5.6 %collective-permute-start.58 = (f32[8,128]{1,0:T(8,128)S(1)}, f32[8,128]{1,0:T(8,128)S(1)}, u32[]{:S(2)}, u32[]{:S(2)}) collective-permute-start(f32[8,128]{1,0:T(8,128)S(1)} %pad.9), channel_id=1, source_target_pairs={{0,1},{1,0},{2,3},{3,2},{4,5},{5,4},{6,7},{7,6},{8,9},{9,8},{10,11... | collective-permute-start | bytes 12296 | tf_op jit(solution)/shard_map/ppermute | solution.py:703
  455.0 12.7 %collective-permute-start.50 = (bf16[128,1664]{1,0:T(8,128)(2,1)S(1)}, bf16[128,1664]{1,0:T(8,128)(2,1)S(1)}, u32[]{:S(2)}, u32[]{:S(2)}) collective-permute-start(bf16[128,1664]{1,0:T(8,128)(2,1)S(1)} %add_convert_fusion.8), channel_id=1, source_target_pairs={{0,4},{4,0},{8,12},{12,8},{16,20},{20,16},{24,28},{28,24},{1,5},{5... | collective-permute-start | bytes 1277960 | tf_op jit(solution)/shard_map/ppermute | solution.py:703
  456.4 20.8 %collective-permute-start.44 = (bf16[256,1024]{1,0:T(8,128)(2,1)}, bf16[256,1024]{1,0:T(8,128)(2,1)S(1)}, u32[]{:S(2)}, u32[]{:S(2)}) collective-permute-start(bf16[256,1024]{1,0:T(8,128)(2,1)} %pad_maximum_fusion.15), channel_id=1, source_target_pairs={{0,2},{1,3},{2,0},{3,1},{4,6},{5,7},{6,4},{7,5},{8,10},{9,11},{10,... | collective-permute-start | bytes 1572872 | tf_op jit(solution)/shard_map/ppermute | solution.py:703
  458.2 17.7 %collective-permute-start.46 = (bf16[128,1664]{1,0:T(8,128)(2,1)S(1)}, bf16[128,1664]{1,0:T(8,128)(2,1)S(1)}, u32[]{:S(2)}, u32[]{:S(2)}) collective-permute-start(bf16[128,1664]{1,0:T(8,128)(2,1)S(1)} %add_convert_fusion.9), channel_id=1, source_target_pairs={{0,4},{4,0},{8,12},{12,8},{16,20},{20,16},{24,28},{28,24},{1,5},{5... | collective-permute-start | bytes 1277960 | tf_op jit(solution)/shard_map/ppermute | solution.py:703
  469.0 11.5 %collective-permute-start.51 = (bf16[32,1664]{1,0:T(8,128)(2,1)S(1)}, bf16[32,1664]{1,0:T(8,128)(2,1)S(1)}, u32[]{:S(2)}, u32[]{:S(2)}) collective-permute-start(bf16[32,1664]{1,0:T(8,128)(2,1)S(1)} %get-tuple-element.283), channel_id=1, source_target_pairs={{0,8},{4,12},{8,0},{12,4},{16,24},{20,28},{24,16},{28,20},{1,9},{5... | collective-permute-start | bytes 319496 | tf_op jit(solution)/shard_map/ppermute | solution.py:703
  469.1 13.1 %collective-permute-start.53 = (bf16[32,1664]{1,0:T(8,128)(2,1)S(1)}, bf16[32,1664]{1,0:T(8,128)(2,1)S(1)}, u32[]{:S(2)}, u32[]{:S(2)}) collective-permute-start(bf16[32,1664]{1,0:T(8,128)(2,1)S(1)} %get-tuple-element.284), channel_id=1, source_target_pairs={{0,24},{4,28},{8,16},{12,20},{16,8},{20,12},{24,0},{28,4},{1,25},{... | collective-permute-start | bytes 319496 | tf_op jit(solution)/shard_map/ppermute | solution.py:703
  470.8 11.4 %collective-permute-start.52 = (bf16[32,1664]{1,0:T(8,128)(2,1)S(1)}, bf16[32,1664]{1,0:T(8,128)(2,1)S(1)}, u32[]{:S(2)}, u32[]{:S(2)}) collective-permute-start(bf16[32,1664]{1,0:T(8,128)(2,1)S(1)} %get-tuple-element.285), channel_id=1, source_target_pairs={{0,16},{4,20},{8,24},{12,28},{16,0},{20,4},{24,8},{28,12},{1,17},{... | collective-permute-start | bytes 319496 | tf_op jit(solution)/shard_map/ppermute | solution.py:703
  477.2 7.5 %collective-permute-start.47 = (bf16[32,1664]{1,0:T(8,128)(2,1)S(1)}, bf16[32,1664]{1,0:T(8,128)(2,1)S(1)}, u32[]{:S(2)}, u32[]{:S(2)}) collective-permute-start(bf16[32,1664]{1,0:T(8,128)(2,1)S(1)} %get-tuple-element.280), channel_id=1, source_target_pairs={{0,8},{4,12},{8,0},{12,4},{16,24},{20,28},{24,16},{28,20},{1,9},{5... | collective-permute-start | bytes 319496 | tf_op jit(solution)/shard_map/ppermute | solution.py:703
  477.3 7.5 %collective-permute-start.49 = (bf16[32,1664]{1,0:T(8,128)(2,1)S(1)}, bf16[32,1664]{1,0:T(8,128)(2,1)S(1)}, u32[]{:S(2)}, u32[]{:S(2)}) collective-permute-start(bf16[32,1664]{1,0:T(8,128)(2,1)S(1)} %get-tuple-element.281), channel_id=1, source_target_pairs={{0,24},{4,28},{8,16},{12,20},{16,8},{20,12},{24,0},{28,4},{1,25},{... | collective-permute-start | bytes 319496 | tf_op jit(solution)/shard_map/ppermute | solution.py:703
  480.5 9.0 %collective-permute-start.48 = (bf16[32,1664]{1,0:T(8,128)(2,1)S(1)}, bf16[32,1664]{1,0:T(8,128)(2,1)S(1)}, u32[]{:S(2)}, u32[]{:S(2)}) collective-permute-start(bf16[32,1664]{1,0:T(8,128)(2,1)S(1)} %get-tuple-element.282), channel_id=1, source_target_pairs={{0,16},{4,20},{8,24},{12,28},{16,0},{20,4},{24,8},{28,12},{1,17},{... | collective-permute-start | bytes 319496 | tf_op jit(solution)/shard_map/ppermute | solution.py:703
  482.3 7.3 %collective-permute-start.54 = (f32[32,1664]{1,0:T(8,128)S(1)}, f32[32,1664]{1,0:T(8,128)S(1)}, u32[]{:S(2)}, u32[]{:S(2)}) collective-permute-start(f32[32,1664]{1,0:T(8,128)S(1)} %fusion.22), channel_id=1, source_target_pairs={{0,2},{1,3},{2,0},{3,1},{4,6},{5,7},{6,4},{7,5},{8,10},{9,11},{10,... | collective-permute-start | bytes 638984 | tf_op jit(solution)/shard_map/ppermute | solution.py:703
  (79 other events, 777.5 us)
Sparse Core Ops, SparseCore 0:
  11.4 158.3 all-gather.2
